TPU v7x, 128 devices: a whole 4x4x4 slice. The times are simulated.
128 devices in a mesh: dp: 64 (over z, y, x), narrow: 2 (over core).
Axes of the slice: x: 4, y: 4, z: 4, core: 2. Of those that a mesh axis runs over, the one named last changes fastest.
Arguments:
- inputs: bfloat16 [2, 128, 128, 896], P(None, ('dp', 'narrow')), may hold values from -6 to 6
- cotangent: bfloat16 [2, 128, 128, 896], P(None, ('dp', 'narrow')), may hold values from -6 to 6
- lengths: int32 [2, 128], replicated, may hold values from 32 to 128, as said below
- query_weight: float32 [896, 896], P(('dp', 'narrow')), may hold values from -0.1875 to 0.1875
- key_weight: float32 [896, 128], P(('dp', 'narrow')), may hold values from -0.1875 to 0.1875
- value_weight: float32 [896, 128], P(('dp', 'narrow')), may hold values from -0.1875 to 0.1875
- out_weight: float32 [896, 896], P(('dp', 'narrow')), may hold values from -0.5 to 0.5
- gate_weight: float32 [896, 4864], P(None, ('dp', 'narrow')), may hold values from -0.1875 to 0.1875
- up_weight: float32 [896, 4864], P(None, ('dp', 'narrow')), may hold values from -0.1875 to 0.1875
- down_weight: float32 [4864, 896], P(('dp', 'narrow')), may hold values from -0.15625 to 0.15625
- vectors: float32 [2944], P(('dp', 'narrow')), may hold values from -1.2 to 3.15
- query_prior: float32 [896, 896], P(('dp', 'narrow')), may hold values from -378.585832 to 378.585832
- key_prior: float32 [896, 128], P(('dp', 'narrow')), may hold values from -378.585832 to 378.585832
- value_prior: float32 [896, 128], P(('dp', 'narrow')), may hold values from -2523.9055 to 2523.9055
- out_prior: float32 [896, 896], P(('dp', 'narrow')), may hold values from -441.68347 to 441.68347
- gate_prior: float32 [896, 4864], P(None, ('dp', 'narrow')), may hold values from -883.36694 to 883.36694
- up_prior: float32 [896, 4864], P(None, ('dp', 'narrow')), may hold values from -1009.5622 to 1009.5622
- down_prior: float32 [4864, 896], P(('dp', 'narrow')), may hold values from -1009.5622 to 1009.5622
- first_prior: float32 [2944], P(('dp', 'narrow')), may hold values from -123.39094 to 123.39094
- second_prior: float32 [2944], P(('dp', 'narrow')), may hold values from 0.786432 to 314.5728
Outputs:
- block_output: bfloat16 [2, 128, 128, 896], P(None, ('dp', 'narrow'))
- input_grad: bfloat16 [2, 128, 128, 896], P(None, ('dp', 'narrow'))
- query_momentum: float32 [896, 896], P(('dp', 'narrow'))
- key_momentum: float32 [896, 128], P(('dp', 'narrow'))
- value_momentum: float32 [896, 128], P(('dp', 'narrow'))
- out_momentum: float32 [896, 896], P(('dp', 'narrow'))
- gate_momentum: float32 [896, 4864], P(None, ('dp', 'narrow'))
- up_momentum: float32 [896, 4864], P(None, ('dp', 'narrow'))
- down_momentum: float32 [4864, 896], P(('dp', 'narrow'))
- query_new: float32 [896, 896], P(('dp', 'narrow'))
- key_new: float32 [896, 128], P(('dp', 'narrow'))
- value_new: float32 [896, 128], P(('dp', 'narrow'))
- out_new: float32 [896, 896], P(('dp', 'narrow'))
- gate_new: float32 [896, 4864], P(None, ('dp', 'narrow'))
- up_new: float32 [896, 4864], P(None, ('dp', 'narrow'))
- down_new: float32 [4864, 896], P(('dp', 'narrow'))
- vector_first: float32 [2944], P(('dp', 'narrow'))
- vector_second: float32 [2944], P(('dp', 'narrow'))
- vector_new: float32 [2944], P(('dp', 'narrow'))
Inputs may be any that keep to these rules, and one draw needn't show every extreme that they name: `lengths`: in every micro-batch one sequence has 128 live tokens and another 128 // 4.
All inputs are finite; a program needn't handle non-finite values.
Results may differ from a plain program's by a relative error of at most 0.024.
Values may be sent and summed in bfloat16 or wider, within the bound.
A program may use at most 320 MiB of HBM per device.

v0:
```python
import math

import jax
import jax.numpy as jnp
from jax import lax
from jax.sharding import PartitionSpec as P

D = 896
FF = 4864
HEADS = 14
KV_HEADS = 2
HEAD = 64
NS_STEPS = 2
STEP = 10


NORM_EPSILON = 1e-06
ROPE_BASE = 1000000.0
MOMENTUM = 0.95
NEWTON_A = 3.4445
NEWTON_B = -4.775
NEWTON_C = 2.0315
MUON_RATE = 0.4
MUON_DECAY = 0.1
ADAM_RATE = 0.5
ADAM_DECAY = 0.01
BETA_FIRST = 0.9
BETA_SECOND = 0.999
ADAM_EPSILON = 1e-08
MASKED = -1e30


def from_partner(x, axis, distance):
    return lax.ppermute(x, axis, [(i, i ^ 1 << distance) for i in range(lax.axis_size(axis))])


def product(left, right):
    return jnp.dot(left, right, preferred_element_type=jnp.float32)


def inner_rows(left, right):
    return lax.dot_general(
        left, right, (((0,), (0,)), ((), ())), preferred_element_type=jnp.float32
    )


def outer_cols(left, right):
    return lax.dot_general(
        left, right, (((1,), (1,)), ((), ())), preferred_element_type=jnp.float32
    )


def rotate_half(values):
    half = values.shape[-1] // 2
    return jnp.concatenate([-values[..., half:], values[..., :half]], axis=-1)


def rotate_back(values):
    half = values.shape[-1] // 2
    return jnp.concatenate([values[..., half:], -values[..., :half]], axis=-1)


def rotary_tables(length):
    half = HEAD // 2
    freqs = ROPE_BASE ** (-jnp.arange(half, dtype=jnp.float32) * 2.0 / HEAD)
    angles = jnp.arange(length, dtype=jnp.float32)[:, None] * freqs[None, :]
    angles = jnp.concatenate([angles, angles], axis=-1)
    return (jnp.cos(angles), jnp.sin(angles))


def rotary(values, cosine, sine):
    return values * cosine[:, None, :] + rotate_half(values) * sine[:, None, :]


def rotary_grad(grads, cosine, sine):
    return grads * cosine[:, None, :] + rotate_back(grads * sine[:, None, :])


def norm_back(grad, normed, scale):
    return scale * (grad - normed * jnp.mean(grad * normed, axis=-1, keepdims=True))


def masked_scores(query_heads, key_heads, allowed):
    scores = jnp.einsum(
        "igrd,jgd->grij", query_heads, key_heads, preferred_element_type=jnp.float32
    )
    return jnp.where(allowed, scores * HEAD ** (-0.5), MASKED)


def slot_pass(full, tokens, cotangent, length):
    (
        query_weight,
        key_weight,
        value_weight,
        out_weight,
        gate_weight,
        up_weight,
        down_weight,
        vectors,
    ) = full
    rows = tokens.shape[0]
    kv_width = key_weight.shape[1]
    group = HEADS // KV_HEADS
    gains = vectors.astype(jnp.float32)
    first_gain = gains[:D]
    second_gain = gains[D : 2 * D]
    query_bias = gains[2 * D : 3 * D]
    key_bias = gains[3 * D : 3 * D + kv_width]
    value_bias = gains[3 * D + kv_width :]
    positions = jnp.arange(rows, dtype=jnp.int32)
    live = (positions < length).astype(jnp.float32)[:, None]
    allowed = (positions[None, :] <= positions[:, None]) & (positions[None, :] < length)
    cosine, sine = rotary_tables(rows)
    inputs = tokens.astype(jnp.float32)
    first_scale = lax.rsqrt(jnp.mean(inputs * inputs, axis=-1, keepdims=True) + NORM_EPSILON)
    first_normed = inputs * first_scale
    normed = (first_normed * first_gain).astype(jnp.bfloat16)
    queries = product(normed, query_weight) + query_bias
    keys = product(normed, key_weight) + key_bias
    values = (product(normed, value_weight) + value_bias).astype(jnp.bfloat16)
    query_heads = rotary(queries.reshape(rows, HEADS, HEAD), cosine, sine).astype(jnp.bfloat16)
    query_heads = query_heads.reshape(rows, KV_HEADS, group, HEAD)
    key_heads = rotary(keys.reshape(rows, KV_HEADS, HEAD), cosine, sine).astype(jnp.bfloat16)
    value_heads = values.reshape(rows, KV_HEADS, HEAD)
    scores = masked_scores(query_heads, key_heads, allowed)
    peak = jnp.max(scores, axis=-1, keepdims=True)
    shifted = jnp.exp(scores - peak)
    total = jnp.sum(shifted, axis=-1, keepdims=True)
    log_total = peak + jnp.log(total)
    weights = (shifted / total).astype(jnp.bfloat16)
    mixed = jnp.einsum("grij,jgd->igrd", weights, value_heads, preferred_element_type=jnp.float32)
    mixed = mixed.reshape(rows, D).astype(jnp.bfloat16)
    middle = inputs + product(mixed, out_weight)
    second_scale = lax.rsqrt(jnp.mean(middle * middle, axis=-1, keepdims=True) + NORM_EPSILON)
    second_normed = middle * second_scale
    normed_two = (second_normed * second_gain).astype(jnp.bfloat16)
    gate = product(normed_two, gate_weight)
    up = product(normed_two, up_weight)
    sigma = jax.nn.sigmoid(gate)
    hidden = (gate * sigma * up).astype(jnp.bfloat16)
    result = ((middle + product(hidden, down_weight)) * live).astype(jnp.bfloat16)
    back = cotangent.astype(jnp.float32) * live
    back_half = back.astype(jnp.bfloat16)
    grad_down_w = inner_rows(hidden, back_half)
    grad_hidden = outer_cols(back_half, down_weight)
    grad_gate = (grad_hidden * up * sigma * (1.0 + gate * (1.0 - sigma))).astype(jnp.bfloat16)
    grad_up = (grad_hidden * gate * sigma).astype(jnp.bfloat16)
    grad_gate_w = inner_rows(normed_two, grad_gate)
    grad_up_w = inner_rows(normed_two, grad_up)
    grad_normed_two = outer_cols(grad_gate, gate_weight) + outer_cols(grad_up, up_weight)
    second_gain_grad = jnp.sum(grad_normed_two * second_normed, axis=0)
    grad_middle = back + norm_back(grad_normed_two * second_gain, second_normed, second_scale)
    branch_grad = grad_middle.astype(jnp.bfloat16)
    grad_out_w = inner_rows(mixed, branch_grad)
    grad_mixed = outer_cols(branch_grad, out_weight).astype(jnp.bfloat16)
    grad_mixed = grad_mixed.reshape(rows, KV_HEADS, group, HEAD)
    probs = jnp.exp(masked_scores(query_heads, key_heads, allowed) - log_total)
    grad_probs = jnp.einsum(
        "igrd,jgd->grij", grad_mixed, value_heads, preferred_element_type=jnp.float32
    )
    grad_scores = probs * (grad_probs - jnp.sum(probs * grad_probs, axis=-1, keepdims=True))
    grad_scores = grad_scores.astype(jnp.bfloat16)
    grad_query = jnp.einsum(
        "grij,jgd->igrd", grad_scores, key_heads, preferred_element_type=jnp.float32
    ) * HEAD ** (-0.5)
    grad_key = jnp.einsum(
        "grij,igrd->jgd", grad_scores, query_heads, preferred_element_type=jnp.float32
    ) * HEAD ** (-0.5)
    grad_value = jnp.einsum(
        "grij,igrd->jgd", weights, grad_mixed, preferred_element_type=jnp.float32
    )
    grad_value = grad_value.astype(jnp.bfloat16).reshape(rows, kv_width)
    grad_query = (
        rotary_grad(grad_query.reshape(rows, HEADS, HEAD), cosine, sine)
        .astype(jnp.bfloat16)
        .reshape(rows, D)
    )
    grad_key = rotary_grad(grad_key, cosine, sine).astype(jnp.bfloat16).reshape(rows, kv_width)
    query_bias_grad = jnp.sum(grad_query.astype(jnp.float32), axis=0)
    key_bias_grad = jnp.sum(grad_key.astype(jnp.float32), axis=0)
    value_bias_grad = jnp.sum(grad_value.astype(jnp.float32), axis=0)
    grad_query_w = inner_rows(normed, grad_query)
    grad_key_w = inner_rows(normed, grad_key)
    grad_value_w = inner_rows(normed, grad_value)
    grad_normed = (
        outer_cols(grad_query, query_weight)
        + outer_cols(grad_key, key_weight)
        + outer_cols(grad_value, value_weight)
    )
    first_gain_grad = jnp.sum(grad_normed * first_normed, axis=0)
    grad_inputs = (
        grad_middle + norm_back(grad_normed * first_gain, first_normed, first_scale)
    ).astype(jnp.bfloat16)
    vector_grad = jnp.concatenate(
        [first_gain_grad, second_gain_grad, query_bias_grad, key_bias_grad, value_bias_grad]
    )
    grads = (
        grad_query_w,
        grad_key_w,
        grad_value_w,
        grad_out_w,
        grad_gate_w,
        grad_up_w,
        grad_down_w,
        vector_grad,
    )
    return (result, grad_inputs, grads)


def gram_part(current, left):
    if left:
        return outer_cols(current, current)
    return inner_rows(current, current)


def newton_step(current, gram, left):
    gram_half = gram.astype(jnp.bfloat16)
    mixer = (NEWTON_B * gram + NEWTON_C * product(gram_half, gram_half)).astype(jnp.bfloat16)
    moved = product(mixer, current) if left else product(current, mixer)
    return (NEWTON_A * current.astype(jnp.float32) + moved).astype(jnp.bfloat16)


def body(
    inputs,
    cotangent,
    lengths,
    query_weight,
    key_weight,
    value_weight,
    out_weight,
    gate_weight,
    up_weight,
    down_weight,
    vectors,
    query_prior,
    key_prior,
    value_prior,
    out_prior,
    gate_prior,
    up_prior,
    down_prior,
    first_prior,
    second_prior,
):
    copy_query = query_weight.astype(jnp.bfloat16)
    copy_key = key_weight.astype(jnp.bfloat16)
    copy_value = value_weight.astype(jnp.bfloat16)
    copy_out = out_weight.astype(jnp.bfloat16)
    copy_gate = gate_weight.astype(jnp.bfloat16)
    copy_up = up_weight.astype(jnp.bfloat16)
    copy_down = down_weight.astype(jnp.bfloat16)
    copy_vectors = vectors.astype(jnp.bfloat16)
    data_index = lax.axis_index("dp")
    narrow_index = lax.axis_index("narrow")
    narrow_count = lax.axis_size("narrow")
    data_count = lax.axis_size("dp")
    bits = data_count.bit_length() - 1
    kv_width = key_weight.shape[1]
    vec_width = 3 * D + 2 * kv_width
    masters = (
        query_weight,
        key_weight,
        value_weight,
        out_weight,
        gate_weight,
        up_weight,
        down_weight,
    )
    shapes = ((D, D), (D, kv_width), (D, kv_width), (D, D), (D, FF), (D, FF), (FF, D))
    start = tuple((jnp.zeros(shape, jnp.float32) for shape in shapes)) + (
        jnp.zeros((vec_width,), jnp.float32),
    )

    def one_batch(carry, pieces):
        tokens, back, batch_lengths = pieces
        key_bits = 1 + jnp.sum(batch_lengths) % (data_count - 1)
        full = (
            lax.all_gather(copy_query, ("dp", "narrow"), axis=0, tiled=True),
            lax.all_gather(copy_key, ("dp", "narrow"), axis=0, tiled=True),
            lax.all_gather(copy_value, ("dp", "narrow"), axis=0, tiled=True),
            lax.all_gather(copy_out, ("dp", "narrow"), axis=0, tiled=True),
            lax.all_gather(copy_gate, ("dp", "narrow"), axis=1, tiled=True),
            lax.all_gather(copy_up, ("dp", "narrow"), axis=1, tiled=True),
            lax.all_gather(copy_down, ("dp", "narrow"), axis=0, tiled=True),
            lax.all_gather(copy_vectors, ("dp", "narrow"), axis=0, tiled=True),
        )
        for bit in range(bits):
            moved = from_partner((tokens, back), "dp", bit)
            take = jnp.right_shift(key_bits, bit) % 2 == 1
            tokens = jnp.where(take, moved[0], tokens)
            back = jnp.where(take, moved[1], back)
        source = jnp.bitwise_xor(data_index, key_bits) * narrow_count + narrow_index
        length = batch_lengths[source]
        result, grad_inputs, grads = slot_pass(full, tokens, back, length)
        for bit in range(bits):
            moved = from_partner((result, grad_inputs), "dp", bit)
            take = jnp.right_shift(key_bits, bit) % 2 == 1
            result = jnp.where(take, moved[0], result)
            grad_inputs = jnp.where(take, moved[1], grad_inputs)
        carry = tuple((first + second for first, second in zip(carry, grads)))
        return (carry, (result, grad_inputs))

    totals, (outputs, input_grads) = lax.scan(
        one_batch, start, (inputs[:, 0], cotangent[:, 0], lengths)
    )
    owned = (
        lax.psum_scatter(totals[0], ("dp", "narrow"), scatter_dimension=0, tiled=True),
        lax.psum_scatter(totals[1], ("dp", "narrow"), scatter_dimension=0, tiled=True),
        lax.psum_scatter(totals[2], ("dp", "narrow"), scatter_dimension=0, tiled=True),
        lax.psum_scatter(totals[3], ("dp", "narrow"), scatter_dimension=0, tiled=True),
        lax.psum_scatter(totals[4], ("dp", "narrow"), scatter_dimension=1, tiled=True),
        lax.psum_scatter(totals[5], ("dp", "narrow"), scatter_dimension=1, tiled=True),
        lax.psum_scatter(totals[6], ("dp", "narrow"), scatter_dimension=0, tiled=True),
        lax.psum_scatter(totals[7], ("dp", "narrow"), scatter_dimension=0, tiled=True),
    )
    block_output = outputs[:, None]
    input_grad = input_grads[:, None]
    priors = (query_prior, key_prior, value_prior, out_prior, gate_prior, up_prior, down_prior)
    lefts = (False, False, False, False, True, True, False)
    momenta = tuple((MOMENTUM * priors[index] + owned[index] for index in range(7)))
    local_squares = tuple((jnp.sum(moment * moment) for moment in momenta))
    squares = lax.psum(
        (
            local_squares[0],
            local_squares[1],
            local_squares[2],
            local_squares[3],
            local_squares[4],
            local_squares[5],
            local_squares[6],
        ),
        ("dp", "narrow"),
    )
    current = tuple(
        (
            (momenta[index] / (jnp.sqrt(squares[index]) + 1e-07)).astype(jnp.bfloat16)
            for index in range(7)
        )
    )
    for step in range(NS_STEPS):
        partial_grams = tuple((gram_part(current[index], lefts[index]) for index in range(7)))
        grams = lax.psum(
            (
                partial_grams[0],
                partial_grams[1],
                partial_grams[2],
                partial_grams[3],
                partial_grams[4],
                partial_grams[5],
                partial_grams[6],
            ),
            ("dp", "narrow"),
        )
        current = tuple(
            (newton_step(current[index], grams[index], lefts[index]) for index in range(7))
        )
    updated = []
    for index in range(7):
        factor = MUON_RATE * 0.2 * math.sqrt(max(shapes[index][0], shapes[index][1]))
        updated.append(
            masters[index] * (1.0 - MUON_RATE * MUON_DECAY)
            - factor * current[index].astype(jnp.float32)
        )
    grad_vector = owned[7]
    vector_first = BETA_FIRST * first_prior + (1.0 - BETA_FIRST) * grad_vector
    vector_second = BETA_SECOND * second_prior + (1.0 - BETA_SECOND) * grad_vector * grad_vector
    first_hat = vector_first / (1.0 - BETA_FIRST**STEP)
    second_hat = vector_second / (1.0 - BETA_SECOND**STEP)
    vector_new = vectors * (1.0 - ADAM_RATE * ADAM_DECAY) - ADAM_RATE * first_hat / (
        jnp.sqrt(second_hat) + ADAM_EPSILON
    )
    return (
        block_output,
        input_grad,
        momenta[0],
        momenta[1],
        momenta[2],
        momenta[3],
        momenta[4],
        momenta[5],
        momenta[6],
        updated[0],
        updated[1],
        updated[2],
        updated[3],
        updated[4],
        updated[5],
        updated[6],
        vector_first,
        vector_second,
        vector_new,
    )


def solution(mesh):
    placed = (
        P(None, ("dp", "narrow"), None, None),
        P(None, ("dp", "narrow"), None, None),
        P(),
        P(("dp", "narrow"), None),
        P(("dp", "narrow"), None),
        P(("dp", "narrow"), None),
        P(("dp", "narrow"), None),
        P(None, ("dp", "narrow")),
        P(None, ("dp", "narrow")),
        P(("dp", "narrow"), None),
        P(("dp", "narrow")),
        P(("dp", "narrow"), None),
        P(("dp", "narrow"), None),
        P(("dp", "narrow"), None),
        P(("dp", "narrow"), None),
        P(None, ("dp", "narrow")),
        P(None, ("dp", "narrow")),
        P(("dp", "narrow"), None),
        P(("dp", "narrow")),
        P(("dp", "narrow")),
    )
    return jax.shard_map(
        body,
        mesh=mesh,
        in_specs=placed,
        out_specs=(
            P(None, ("dp", "narrow"), None, None),
            P(None, ("dp", "narrow"), None, None),
            P(("dp", "narrow"), None),
            P(("dp", "narrow"), None),
            P(("dp", "narrow"), None),
            P(("dp", "narrow"), None),
            P(None, ("dp", "narrow")),
            P(None, ("dp", "narrow")),
            P(("dp", "narrow"), None),
            P(("dp", "narrow"), None),
            P(("dp", "narrow"), None),
            P(("dp", "narrow"), None),
            P(("dp", "narrow"), None),
            P(None, ("dp", "narrow")),
            P(None, ("dp", "narrow")),
            P(("dp", "narrow"), None),
            P(("dp", "narrow")),
            P(("dp", "narrow")),
            P(("dp", "narrow")),
        ),
        check_vma=False,
    )
```

profile of v0, /device:TPU:1, one launch (start us, length us, event | category | flops | bytes accessed | tf_op | source)
XLA Modules:
  0.0 3019.7 jit_solution(2310116437090488761)
XLA Ops:
  18.0 1070.8 %while.32 = (s32[]{:T(128)}, f32[896,896]{1,0:T(8,128)}, f32[896,128]{1,0:T(8,128)}, f32[896,128]{1,0:T(8,128)}, f32[896,896]{1,0:T(8,128)}, /*index=5*/f32[896,...) while((s32[]{:T(128)}, f32[896,896]{1,0:T(8,128)}, ...), condition=%wide.region_14.15_spmd.clone, body=%wide.region_0.14_spmd.clone.sunk | while | flops 11684199424 | bytes 734010240 | solution.py:303
  30.0 68.6 %all-reduce.19 = bf16[2944]{0:T(1024)(128)(2,1)S(1)} all-reduce(bf16[2944]{0:T(1024)(128)(2,1)S(1)} %dynamic-update-slice.23), channel_id=1, replica_groups=mesh['dp'=64,'narrow'=2] {'dp','narrow'}, use_global_device_ids=true, to_apply=%add | all-reduce | flops 2944 | bytes 11776 | tf_op jit(solution)/shard_map/while
  99.3 33.8 %all-gather.21 = bf16[128,7,128]{2,1,0:T(8,128)(2,1)S(1)} all-gather(bf16[1,7,128]{2,1,0:T(8,128)(2,1)S(1)} %bitcast.326), channel_id=1, replica_groups=mesh['dp'=64,'narrow'=2] {'dp','narrow'}, dimensions={0}, use_global_device_ids=true | all-gather | bytes 231168 | tf_op jit(solution)/shard_map/while/body/eval_jaxpr/all_gather | solution.py:279
  133.1 33.2 %all-gather.23 = bf16[128,7,128]{2,1,0:T(8,128)(2,1)S(1)} all-gather(bf16[1,7,128]{2,1,0:T(8,128)(2,1)S(1)} %bitcast.327), channel_id=1, replica_groups=mesh['dp'=64,'narrow'=2] {'dp','narrow'}, dimensions={0}, use_global_device_ids=true | all-gather | bytes 231168 | tf_op jit(solution)/shard_map/while/body/eval_jaxpr/all_gather | solution.py:280
  196.6 9.0 collective-permute-start.4
  206.2 8.4 collective-permute-start.10
  214.7 9.0 collective-permute-start.5
  227.0 9.7 collective-permute-start.11
  255.6 13.1 reshape.316
  268.7 46.6 %all-gather.40.cloned.1.call-done = bf16[128,38,896]{2,1,0:T(8,128)(2,1)} async-done(((bf16[1,38,896]{2,1,0:T(8,128)(2,1)}), bf16[128,38,896]{2,1,0:T(8,128)(2,1)}) %all-gather.40.cloned.1.call-update) | async-done | bytes 8716304 | tf_op jit(solution)/shard_map/while/body/eval_jaxpr/all_gather | solution.py:282
  315.3 13.0 reshape.317
  339.7 47.5 %all-gather.42.cloned.1.call-done = bf16[128,38,896]{2,1,0:T(8,128)(2,1)} async-done(((bf16[1,38,896]{2,1,0:T(8,128)(2,1)}), bf16[128,38,896]{2,1,0:T(8,128)(2,1)}) %all-gather.42.cloned.1.call-update) | async-done | bytes 8716304 | tf_op jit(solution)/shard_map/while/body/eval_jaxpr/all_gather | solution.py:284
  387.2 13.0 reshape.318
  400.2 10.4 multiply_convert_fusion.9
  435.6 10.0 select_add_fusion.15
  445.6 9.9 select_add_fusion.14
  482.4 9.4 collective-permute-start.21
  500.4 7.9 collective-permute-start.22
  508.3 9.0 collective-permute-start.16
  517.3 9.0 collective-permute-start.23
  526.3 9.0 collective-permute-start.17
  535.4 8.9 collective-permute-done.17
  556.5 65.8 %all-reduce.19 = bf16[2944]{0:T(1024)(128)(2,1)S(1)} all-reduce(bf16[2944]{0:T(1024)(128)(2,1)S(1)} %dynamic-update-slice.23), channel_id=1, replica_groups=mesh['dp'=64,'narrow'=2] {'dp','narrow'}, use_global_device_ids=true, to_apply=%add | all-reduce | flops 2944 | bytes 11776 | tf_op jit(solution)/shard_map/while
  622.9 33.8 %all-gather.21 = bf16[128,7,128]{2,1,0:T(8,128)(2,1)S(1)} all-gather(bf16[1,7,128]{2,1,0:T(8,128)(2,1)S(1)} %bitcast.326), channel_id=1, replica_groups=mesh['dp'=64,'narrow'=2] {'dp','narrow'}, dimensions={0}, use_global_device_ids=true | all-gather | bytes 231168 | tf_op jit(solution)/shard_map/while/body/eval_jaxpr/all_gather | solution.py:279
  656.7 33.2 %all-gather.23 = bf16[128,7,128]{2,1,0:T(8,128)(2,1)S(1)} all-gather(bf16[1,7,128]{2,1,0:T(8,128)(2,1)S(1)} %bitcast.327), channel_id=1, replica_groups=mesh['dp'=64,'narrow'=2] {'dp','narrow'}, dimensions={0}, use_global_device_ids=true | all-gather | bytes 231168 | tf_op jit(solution)/shard_map/while/body/eval_jaxpr/all_gather | solution.py:280
  712.4 7.9 collective-permute-start.9
  720.5 8.7 collective-permute-start.4
  730.2 8.1 collective-permute-start.10
  738.3 9.0 collective-permute-start.5
  750.6 9.8 collective-permute-start.11
  779.4 13.1 reshape.316
  792.4 46.8 %all-gather.40.cloned.1.call-done = bf16[128,38,896]{2,1,0:T(8,128)(2,1)} async-done(((bf16[1,38,896]{2,1,0:T(8,128)(2,1)}), bf16[128,38,896]{2,1,0:T(8,128)(2,1)}) %all-gather.40.cloned.1.call-update) | async-done | bytes 8716304 | tf_op jit(solution)/shard_map/while/body/eval_jaxpr/all_gather | solution.py:282
  839.2 13.0 reshape.317
  863.6 47.5 %all-gather.42.cloned.1.call-done = bf16[128,38,896]{2,1,0:T(8,128)(2,1)} async-done(((bf16[1,38,896]{2,1,0:T(8,128)(2,1)}), bf16[128,38,896]{2,1,0:T(8,128)(2,1)}) %all-gather.42.cloned.1.call-update) | async-done | bytes 8716304 | tf_op jit(solution)/shard_map/while/body/eval_jaxpr/all_gather | solution.py:284
  911.1 13.0 reshape.318
  924.1 10.0 multiply_convert_fusion.9
  959.2 15.0 select_add_fusion.15
  974.2 15.0 select_add_fusion.14
  994.0 7.9 select_add_fusion.13
  1019.4 9.4 collective-permute-start.21
  1037.4 7.9 collective-permute-start.22
  1045.3 9.0 collective-permute-start.16
  1054.3 9.0 collective-permute-start.23
  1063.4 9.0 collective-permute-start.17
  1072.4 8.9 collective-permute-done.17
  1088.8 377.4 %fusion.2 = f32[48,896]{1,0:T(8,128)S(1)} fusion(f32[4864,896]{1,0:T(8,128)} %get-tuple-element.398), kind=kCustom, calls=%all-reduce-scatter.2 | all-reduce-scatter fusion | flops 5505025 | bytes 17604608
  1471.5 18.7 copy.68
  1490.2 19.1 copy.69
  1509.3 424.2 %fusion.274 = (f32[896,48]{0,1:T(8,128)S(1)}, f32[896,48]{0,1:T(8,128)S(1)}) fusion(f32[896,4864]{0,1:T(8,128)} %copy.68, f32[896,4864]{0,1:T(8,128)} %copy.69), kind=kCustom, calls=%all-reduce-scatter.3 | all-reduce-scatter fusion | flops 11010049 | bytes 35209216
  2024.4 8.1 collective-permute-start.96
  2037.1 9.4 collective-permute-start.51
  2073.5 8.1 collective-permute-start.59
  2094.0 7.9 collective-permute-start.64
  2101.9 11.4 collective-permute-start.65
  2117.2 10.3 collective-permute-start.68
  2148.9 9.7 collective-permute-start.74
  2216.6 10.3 collective-permute-start.39
  2239.5 9.7 collective-permute-start.44
  2268.1 43.5 %concatenate.84 = f32[1318,896]{1,0:T(8,128)} concatenate(f32[22,896]{1,0:T(8,128)} %copy-done.102, f32[48,896]{1,0:T(8,128)S(1)} %collective-permute-done.103, f32[48,896]{1,0:T(8,128)S(1)} %collective-permute-done.102, f32[48,896]{1,0:T(8,128)S(1)} %collective-permute-done.101, f32[48,896]{1,0:T(8,128)S(1)} %collective-permute-done.100, f32[48,896]{1,0:T(8,128)} %copy-done.57, ...), dimensions={0} | concatenate | bytes 9447424
  2311.6 46.0 %concatenate.83 = f32[896,1318]{0,1:T(8,128)} concatenate(f32[896,22]{0,1:T(8,128)} %copy-done.103, f32[896,48]{0,1:T(8,128)} %copy-done.87, f32[896,48]{0,1:T(8,128)} %copy-done.84, f32[896,48]{0,1:T(8,128)} %copy-done.81, f32[896,48]{0,1:T(8,128)} %copy-done.80, f32[896,48]{0,1:T(8,128)} %copy-done.79, f32[896,48]{0,1:T(8,128)} %copy-done.78, f32[896,48]{0,1:T(8,128)} %copy-done.77, ...), dimensions={1} | concatenate | bytes 9447424
  2357.7 44.4 %concatenate.82 = f32[896,1318]{0,1:T(8,128)} concatenate(f32[896,22]{0,1:T(8,128)S(1)} %collective-permute-done.50, f32[896,48]{0,1:T(8,128)} %collective-permute-done.49, f32[896,48]{0,1:T(8,128)} %collective-permute-done.48, f32[896,48]{0,1:T(8,128)} %collective-permute-done.47, f32[896,48]{0,1:T(8,128)} %collective-permute-done.46, f32[896,48]{0,1:T(8,128)} %collective-permute-done.45, ...), dimensions={1} | concatenate | bytes 9447424
  2409.9 63.6 %all-reduce.13 = (f32[]{:T(128)}, f32[]{:T(128)}, f32[]{:T(128)}, f32[]{:T(128)}, f32[]{:T(128)}, /*index=5*/f32[]{:T(128)}, f32[]{:T(128)}, f32[2944]{0:T(1024)S(1)}) all-reduce(f32[]{:T(128)} %get-tuple-element.612, f32[]{:T(128)} %get-tuple-element.614, ...), channel_id=1, replica_groups=mesh['dp'=64,'narrow'=2] {'dp','narrow'}, use_global_device_ids=true, to_apply=%region_23.24 | all-reduce | flops 2951 | bytes 23608 | tf_op jit(solution)/shard_map/psum | solution.py:322
  2492.0 218.0 %all-reduce.26.cloned.1.call-done = (f32[896,896]{1,0:T(8,128)}, f32[128,128]{1,0:T(8,128)}, f32[128,128]{1,0:T(8,128)}, f32[896,896]{1,0:T(8,128)}, f32[896,896...) async-done(((f32[896,896]{1,0:T(8,128)}, f32[128,128]{1,0:T(8,128)}, f32[128,128]{1,0:T(8,128)}, f32[896,896]{1,0:T(8,128)}, f32[896,896]{1,0:T(8,128)}, ...) | async-done | bytes 16187408 | tf_op jit(solution)/shard_map/psum | solution.py:342
  2757.0 217.8 %all-reduce.24.cloned.1.call-done = (f32[896,896]{1,0:T(8,128)}, f32[128,128]{1,0:T(8,128)}, f32[128,128]{1,0:T(8,128)}, f32[896,896]{1,0:T(8,128)}, f32[896,896...) async-done(((f32[896,896]{1,0:T(8,128)}, f32[128,128]{1,0:T(8,128)}, f32[128,128]{1,0:T(8,128)}, f32[896,896]{1,0:T(8,128)}, f32[896,896]{1,0:T(8,128)}, ...) | async-done | bytes 16187408 | tf_op jit(solution)/shard_map/psum | solution.py:342
  (941 shorter events, 629.9 us)
Async XLA Ops:
  18.3 228.0 %all-gather.34.cloned.1.call-start = ((), (), s32[]{:S(2)}) async-start(), calls=%async_computation.3 | async-start | bytes 1849344 | tf_op jit(solution)/shard_map/while/body/eval_jaxpr/all_gather | solution.py:278
  19.1 230.6 %all-gather.36.cloned.1.call-start = ((), (), s32[]{:S(2)}) async-start(), calls=%async_computation.4 | async-start | bytes 1849344 | tf_op jit(solution)/shard_map/while/body/eval_jaxpr/all_gather | solution.py:281
  19.8 235.8 %all-gather.38.cloned.1.call-start = ((), (), s32[]{:S(2)}) async-start(), calls=%async_computation.5 | async-start | bytes 9246720 | tf_op jit(solution)/shard_map/while/body/eval_jaxpr/all_gather | solution.py:283
  20.6 294.7 %all-gather.40.cloned.1.call-start = ((), (), s32[]{:S(2)}) async-start(), calls=%async_computation.6 | async-start | bytes 9246720 | tf_op jit(solution)/shard_map/while/body/eval_jaxpr/all_gather | solution.py:282
  21.1 366.0 %all-gather.42.cloned.1.call-start = ((), (), s32[]{:S(2)}) async-start(), calls=%async_computation.7 | async-start | bytes 9246720 | tf_op jit(solution)/shard_map/while/body/eval_jaxpr/all_gather | solution.py:284
  22.7 145.5 %collective-permute-start = (bf16[128,896]{1,0:T(8,128)(2,1)S(1)}, bf16[128,896]{1,0:T(8,128)(2,1)S(1)}, u32[]{:S(2)}, u32[]{:S(2)}) collective-permute-start(bf16[128,896]{1,0:T(8,128)(2,1)S(1)} %dynamic-slice_bitcast_fusion.4), channel_id=1, source_target_pairs={{0,2},{2,0},{4,6},{6,4},{8,10},{10,8},{12,14},{14,12},{16,18},{18,... | collective-permute-start | bytes 688136 | tf_op jit(solution)/shard_map/while/body/eval_jaxpr/ppermute | solution.py:34
  25.8 144.1 %collective-permute-start.6 = (bf16[128,896]{1,0:T(8,128)(2,1)S(1)}, bf16[128,896]{1,0:T(8,128)(2,1)S(1)}, u32[]{:S(2)}, u32[]{:S(2)}) collective-permute-start(bf16[128,896]{1,0:T(8,128)(2,1)S(1)} %dynamic-slice_bitcast_fusion.5), channel_id=1, source_target_pairs={{0,2},{2,0},{4,6},{6,4},{8,10},{10,8},{12,14},{14,12},{16,18},{18,... | collective-permute-start | bytes 688136 | tf_op jit(solution)/shard_map/while/body/eval_jaxpr/ppermute | solution.py:34
  214.7 23.9 collective-permute-start.5
  429.7 38.2 %collective-permute-start.18 = (bf16[128,896]{1,0:T(8,128)(2,1)}, bf16[128,896]{1,0:T(8,128)(2,1)}, u32[]{:S(2)}, u32[]{:S(2)}) collective-permute-start(bf16[128,896]{1,0:T(8,128)(2,1)} %fusion.505), channel_id=1, source_target_pairs={{0,2},{2,0},{4,6},{6,4},{8,10},{10,8},{12,14},{14,12},{16,18},{18,... | collective-permute-start | bytes 688136 | tf_op jit(solution)/shard_map/while/body/eval_jaxpr/ppermute | solution.py:34
  432.2 38.5 %collective-permute-start.12 = (bf16[128,896]{1,0:T(8,128)(2,1)}, bf16[128,896]{1,0:T(8,128)(2,1)}, u32[]{:S(2)}, u32[]{:S(2)}) collective-permute-start(bf16[128,896]{1,0:T(8,128)(2,1)} %fusion.504), channel_id=1, source_target_pairs={{0,2},{2,0},{4,6},{6,4},{8,10},{10,8},{12,14},{14,12},{16,18},{18,... | collective-permute-start | bytes 688136 | tf_op jit(solution)/shard_map/while/body/eval_jaxpr/ppermute | solution.py:34
  545.4 224.7 %all-gather.34.cloned.1.call-start = ((), (), s32[]{:S(2)}) async-start(), calls=%async_computation.3 | async-start | bytes 1849344 | tf_op jit(solution)/shard_map/while/body/eval_jaxpr/all_gather | solution.py:278
  546.0 227.5 %all-gather.36.cloned.1.call-start = ((), (), s32[]{:S(2)}) async-start(), calls=%async_computation.4 | async-start | bytes 1849344 | tf_op jit(solution)/shard_map/while/body/eval_jaxpr/all_gather | solution.py:281
  546.7 232.7 %all-gather.38.cloned.1.call-start = ((), (), s32[]{:S(2)}) async-start(), calls=%async_computation.5 | async-start | bytes 9246720 | tf_op jit(solution)/shard_map/while/body/eval_jaxpr/all_gather | solution.py:283
  547.5 291.8 %all-gather.40.cloned.1.call-start = ((), (), s32[]{:S(2)}) async-start(), calls=%async_computation.6 | async-start | bytes 9246720 | tf_op jit(solution)/shard_map/while/body/eval_jaxpr/all_gather | solution.py:282
  548.2 362.9 %all-gather.42.cloned.1.call-start = ((), (), s32[]{:S(2)}) async-start(), calls=%async_computation.7 | async-start | bytes 9246720 | tf_op jit(solution)/shard_map/while/body/eval_jaxpr/all_gather | solution.py:284
  549.7 142.1 %collective-permute-start = (bf16[128,896]{1,0:T(8,128)(2,1)S(1)}, bf16[128,896]{1,0:T(8,128)(2,1)S(1)}, u32[]{:S(2)}, u32[]{:S(2)}) collective-permute-start(bf16[128,896]{1,0:T(8,128)(2,1)S(1)} %dynamic-slice_bitcast_fusion.4), channel_id=1, source_target_pairs={{0,2},{2,0},{4,6},{6,4},{8,10},{10,8},{12,14},{14,12},{16,18},{18,... | collective-permute-start | bytes 688136 | tf_op jit(solution)/shard_map/while/body/eval_jaxpr/ppermute | solution.py:34
  552.0 141.8 %collective-permute-start.6 = (bf16[128,896]{1,0:T(8,128)(2,1)S(1)}, bf16[128,896]{1,0:T(8,128)(2,1)S(1)}, u32[]{:S(2)}, u32[]{:S(2)}) collective-permute-start(bf16[128,896]{1,0:T(8,128)(2,1)S(1)} %dynamic-slice_bitcast_fusion.5), channel_id=1, source_target_pairs={{0,2},{2,0},{4,6},{6,4},{8,10},{10,8},{12,14},{14,12},{16,18},{18,... | collective-permute-start | bytes 688136 | tf_op jit(solution)/shard_map/while/body/eval_jaxpr/ppermute | solution.py:34
  738.3 23.8 collective-permute-start.5
  953.3 51.7 %collective-permute-start.18 = (bf16[128,896]{1,0:T(8,128)(2,1)}, bf16[128,896]{1,0:T(8,128)(2,1)}, u32[]{:S(2)}, u32[]{:S(2)}) collective-permute-start(bf16[128,896]{1,0:T(8,128)(2,1)} %fusion.505), channel_id=1, source_target_pairs={{0,2},{2,0},{4,6},{6,4},{8,10},{10,8},{12,14},{14,12},{16,18},{18,... | collective-permute-start | bytes 688136 | tf_op jit(solution)/shard_map/while/body/eval_jaxpr/ppermute | solution.py:34
  955.7 52.0 %collective-permute-start.12 = (bf16[128,896]{1,0:T(8,128)(2,1)}, bf16[128,896]{1,0:T(8,128)(2,1)}, u32[]{:S(2)}, u32[]{:S(2)}) collective-permute-start(bf16[128,896]{1,0:T(8,128)(2,1)} %fusion.504), channel_id=1, source_target_pairs={{0,2},{2,0},{4,6},{6,4},{8,10},{10,8},{12,14},{14,12},{16,18},{18,... | collective-permute-start | bytes 688136 | tf_op jit(solution)/shard_map/while/body/eval_jaxpr/ppermute | solution.py:34
  1088.8 1318.2 %all-reduce.28.cloned.1.call-start = ((), (), s32[]{:S(2)}) async-start(), calls=%async_computation.2 | async-start | bytes 14680064
  1466.2 488.0 %collective-permute-start.100 = (f32[48,896]{1,0:T(8,128)S(1)}, f32[48,896]{1,0:T(8,128)S(1)}, u32[]{:S(2)}, u32[]{:S(2)}) collective-permute-start(f32[48,896]{1,0:T(8,128)S(1)} %fusion.2), channel_id=1, source_target_pairs={{0,23},{1,24},{2,25},{3,26},{4,27},{5,28},{6,29},{7,30},{8,31},{9,... | collective-permute-start | bytes 516104
  1467.5 488.8 %collective-permute-start.101 = (f32[48,896]{1,0:T(8,128)S(1)}, f32[48,896]{1,0:T(8,128)S(1)}, u32[]{:S(2)}, u32[]{:S(2)}) collective-permute-start(f32[48,896]{1,0:T(8,128)S(1)} %fusion.2), channel_id=1, source_target_pairs={{0,24},{1,25},{2,26},{3,27},{4,28},{5,29},{6,30},{7,31},{8,32},{9,... | collective-permute-start | bytes 516104
  1468.8 492.6 %collective-permute-start.102 = (f32[48,896]{1,0:T(8,128)S(1)}, f32[48,896]{1,0:T(8,128)S(1)}, u32[]{:S(2)}, u32[]{:S(2)}) collective-permute-start(f32[48,896]{1,0:T(8,128)S(1)} %fusion.2), channel_id=1, source_target_pairs={{0,25},{1,26},{2,27},{3,28},{4,29},{5,30},{6,31},{7,32},{8,33},{9,... | collective-permute-start | bytes 516104
  1470.1 470.4 %collective-permute-start.104 = (f32[22,896]{1,0:T(8,128)S(1)}, f32[22,896]{1,0:T(8,128)S(1)}, u32[]{:S(2)}, u32[]{:S(2)}) collective-permute-start(f32[22,896]{1,0:T(8,128)S(1)} %slice.119), channel_id=1, source_target_pairs={{0,27},{1,28},{2,29},{3,30},{4,31},{5,32},{6,33},{7,34},{8,35},{9,... | collective-permute-start | bytes 236552
  1471.5 1238.5 %all-reduce.26.cloned.1.call-start = ((), (), s32[]{:S(2)}) async-start(), calls=%async_computation.1 | async-start | bytes 32374784 | tf_op jit(solution)/shard_map/psum | solution.py:342
  1982.2 22.7 collective-permute-start.87
  1985.9 26.5 collective-permute-start.88
  1989.3 27.4 collective-permute-start.89
  1994.8 24.5 collective-permute-start.90
  2000.9 23.6 collective-permute-start.91
  2004.9 27.6 collective-permute-start.92
  2024.4 22.0 collective-permute-start.96
  2035.2 22.0 collective-permute-start.99
  2037.1 25.6 collective-permute-start.51
  2057.3 24.3 collective-permute-start.55
  2064.4 23.4 collective-permute-start.57
  2083.6 29.7 collective-permute-start.61
  2087.8 27.5 collective-permute-start.62
  2091.5 25.7 collective-permute-start.63
  2094.0 33.5 %collective-permute-start.64 = (f32[896,48]{0,1:T(8,128)S(1)}, f32[896,48]{0,1:T(8,128)S(1)}, u32[]{:S(2)}, u32[]{:S(2)}) collective-permute-start(f32[896,48]{0,1:T(8,128)S(1)} %get-tuple-element.556), channel_id=1, source_target_pairs={{0,14},{1,15},{2,16},{3,17},{4,18},{5,19},{6,20},{7,21},{8,22},{9,... | collective-permute-start | bytes 516104
  2101.9 29.6 collective-permute-start.65
  2117.2 23.9 collective-permute-start.68
  2131.5 27.1 collective-permute-start.70
  2133.8 26.2 collective-permute-start.71
  2136.6 24.7 collective-permute-start.72
  2141.1 22.2 collective-permute-start.73
  2164.9 23.9 collective-permute-start.26
  2172.7 23.5 collective-permute-start.28
  2200.9 26.0 collective-permute-start.35
  2208.1 24.1 collective-permute-start.36
  2211.2 23.5 collective-permute-start.37
  2214.6 22.9 collective-permute-start.38
  2216.6 23.0 collective-permute-start.39
  2226.9 22.4 collective-permute-start.40
  2234.7 25.8 collective-permute-start.42
  2237.6 26.3 collective-permute-start.43
  2239.5 26.3 collective-permute-start.44
  2249.3 108.4 %collective-permute-start.45 = (f32[896,48]{0,1:T(8,128)S(1)}, f32[896,48]{0,1:T(8,128)}, u32[]{:S(2)}, u32[]{:S(2)}) collective-permute-start(f32[896,48]{0,1:T(8,128)S(1)} %get-tuple-element.555), channel_id=1, source_target_pairs={{0,22},{1,23},{2,24},{3,25},{4,26},{5,27},{6,28},{7,29},{8,30},{9,... | collective-permute-start | bytes 516104
  2253.3 104.3 %collective-permute-start.46 = (f32[896,48]{0,1:T(8,128)S(1)}, f32[896,48]{0,1:T(8,128)}, u32[]{:S(2)}, u32[]{:S(2)}) collective-permute-start(f32[896,48]{0,1:T(8,128)S(1)} %get-tuple-element.555), channel_id=1, source_target_pairs={{0,23},{1,24},{2,25},{3,26},{4,27},{5,28},{6,29},{7,30},{8,31},{9,... | collective-permute-start | bytes 516104
  2260.5 97.2 %collective-permute-start.47 = (f32[896,48]{0,1:T(8,128)S(1)}, f32[896,48]{0,1:T(8,128)}, u32[]{:S(2)}, u32[]{:S(2)}) collective-permute-start(f32[896,48]{0,1:T(8,128)S(1)} %get-tuple-element.555), channel_id=1, source_target_pairs={{0,24},{1,25},{2,26},{3,27},{4,28},{5,29},{6,30},{7,31},{8,32},{9,... | collective-permute-start | bytes 516104
  2263.9 93.8 %collective-permute-start.48 = (f32[896,48]{0,1:T(8,128)S(1)}, f32[896,48]{0,1:T(8,128)}, u32[]{:S(2)}, u32[]{:S(2)}) collective-permute-start(f32[896,48]{0,1:T(8,128)S(1)} %get-tuple-element.555), channel_id=1, source_target_pairs={{0,25},{1,26},{2,27},{3,28},{4,29},{5,30},{6,31},{7,32},{8,33},{9,... | collective-permute-start | bytes 516104
  2265.8 91.9 %collective-permute-start.49 = (f32[896,48]{0,1:T(8,128)S(1)}, f32[896,48]{0,1:T(8,128)}, u32[]{:S(2)}, u32[]{:S(2)}) collective-permute-start(f32[896,48]{0,1:T(8,128)S(1)} %get-tuple-element.555), channel_id=1, source_target_pairs={{0,26},{1,27},{2,28},{3,29},{4,30},{5,31},{6,32},{7,33},{8,34},{9,... | collective-permute-start | bytes 516104
  2491.5 483.2 %all-reduce.24.cloned.1.call-start = ((), (), s32[]{:S(2)}) async-start(), calls=%async_computation | async-start | bytes 32374784 | tf_op jit(solution)/shard_map/psum | solution.py:342
  (288 other events, 14896.5 us)
Sparse Core Ops, SparseCore 0:
  22.6 68.5 all-gather.33
  94.7 62.3 all-gather.35
  160.8 79.2 all-gather.37
  243.7 71.5 all-gather.39
  318.8 68.3 all-gather.41
  549.3 64.7 all-gather.33
  617.6 62.3 all-gather.35
  683.6 80.2 all-gather.37
  767.6 71.5 all-gather.39
  842.8 68.3 all-gather.41
Sparse Core Ops, SparseCore 1:
  1471.6 173.1 all-reduce.27
  2491.6 218.3 all-reduce.25
  2755.8 218.9 all-reduce.23
where the time goes:
time: 3030 us; the launch traced here: 3020 us
  blocking collectives  1130 us (37%)
  waiting for transfers between devices  729 us (24%)
  starting transfers between devices  547 us (18%)
  local copies, waits for them, and re-layouts  287 us (9%)
  matrix products  252 us (8%)
  other arithmetic  37.5 us (1%)
    unnamed x2, blocking collectives  802 us
    psum x2, waiting for transfers between devices, body(): lax.psum((partial_grams[0], partial_grams[1], partial_grams[2], partial_g...  436 us
    unnamed x82, starting transfers between devices  338 us
    ppermute x48, starting transfers between devices, from_partner(): lax.ppermute(x, axis, [(i, i ^ 1 << distance) for i in range(lax.axis_siz...  208 us
    unnamed x154, local copies, waits for them, and re-layouts  135 us
    while x2, blocking collectives  134 us
    while x298, local copies, waits for them, and re-layouts  100 us
    dot_general x28, matrix products, product(): return jnp.dot(left, right, preferred_element_type=jnp.float32)  100 us
  transfers between devices with their start and end apart: 142, of which 32 were waited for; matrix products, arithmetic and copies ran while one was open for 27% of the time, Pallas kernels for 0%

commit v1 on v0

v1 whole, which is shorter than its diff:
```python
import math

import jax
import jax.numpy as jnp
from jax import lax
from jax.sharding import PartitionSpec as P

D = 896
FF = 4864
HEADS = 14
KV_HEADS = 2
HEAD = 64
STEP = 10


NORM_EPSILON = 1e-06
ROPE_BASE = 1000000.0
MOMENTUM = 0.95
NEWTON_A = 3.4445
NEWTON_B = -4.775
NEWTON_C = 2.0315
MUON_RATE = 0.4
MUON_DECAY = 0.1
ADAM_RATE = 0.5
ADAM_DECAY = 0.01
BETA_FIRST = 0.9
BETA_SECOND = 0.999
ADAM_EPSILON = 1e-08
MASKED = -1e30


def product(left, right):
    return jnp.dot(left, right, preferred_element_type=jnp.float32)


def inner_rows(left, right):
    return lax.dot_general(
        left, right, (((0,), (0,)), ((), ())), preferred_element_type=jnp.float32
    )


def outer_cols(left, right):
    return lax.dot_general(
        left, right, (((1,), (1,)), ((), ())), preferred_element_type=jnp.float32
    )


def rotate_half(values):
    half = values.shape[-1] // 2
    return jnp.concatenate([-values[..., half:], values[..., :half]], axis=-1)


def rotate_back(values):
    half = values.shape[-1] // 2
    return jnp.concatenate([values[..., half:], -values[..., :half]], axis=-1)


def rotary_tables(length):
    half = HEAD // 2
    freqs = ROPE_BASE ** (-jnp.arange(half, dtype=jnp.float32) * 2.0 / HEAD)
    angles = jnp.arange(length, dtype=jnp.float32)[:, None] * freqs[None, :]
    angles = jnp.concatenate([angles, angles], axis=-1)
    return (jnp.cos(angles), jnp.sin(angles))


def rotary(values, cosine, sine):
    return values * cosine[None, :, None, :] + rotate_half(values) * sine[None, :, None, :]


def rotary_grad(grads, cosine, sine):
    return grads * cosine[None, :, None, :] + rotate_back(grads * sine[None, :, None, :])


def norm_back(grad, normed, scale):
    return scale * (grad - normed * jnp.mean(grad * normed, axis=-1, keepdims=True))


def slot_pass(full, tokens, cotangent, lengths):
    (
        query_weight,
        key_weight,
        value_weight,
        out_weight,
        gate_rows,
        up_rows,
        down_weight,
        vectors,
    ) = full
    batch, rows = tokens.shape[0], tokens.shape[1]
    count = batch * rows
    kv_width = key_weight.shape[1]
    group = HEADS // KV_HEADS
    gains = vectors.astype(jnp.float32)
    first_gain = gains[:D]
    second_gain = gains[D : 2 * D]
    query_bias = gains[2 * D : 3 * D]
    key_bias = gains[3 * D : 3 * D + kv_width]
    value_bias = gains[3 * D + kv_width :]
    positions = jnp.arange(rows, dtype=jnp.int32)
    live = (positions[None, :] < lengths[:, None]).astype(jnp.float32).reshape(count, 1)
    allowed = (positions[None, None, :] <= positions[None, :, None]) & (
        positions[None, None, :] < lengths[:, None, None]
    )
    allowed = allowed[:, None, None]
    cosine, sine = rotary_tables(rows)
    inputs = tokens.astype(jnp.float32).reshape(count, D)
    first_scale = lax.rsqrt(jnp.mean(inputs * inputs, axis=-1, keepdims=True) + NORM_EPSILON)
    first_normed = inputs * first_scale
    normed = (first_normed * first_gain).astype(jnp.bfloat16)
    queries = product(normed, query_weight) + query_bias
    keys = product(normed, key_weight) + key_bias
    values = (product(normed, value_weight) + value_bias).astype(jnp.bfloat16)
    query_heads = rotary(queries.reshape(batch, rows, HEADS, HEAD), cosine, sine).astype(jnp.bfloat16)
    query_heads = query_heads.reshape(batch, rows, KV_HEADS, group, HEAD)
    key_heads = rotary(keys.reshape(batch, rows, KV_HEADS, HEAD), cosine, sine).astype(jnp.bfloat16)
    value_heads = values.reshape(batch, rows, KV_HEADS, HEAD)
    scores = jnp.einsum(
        "bigrd,bjgd->bgrij", query_heads, key_heads, preferred_element_type=jnp.float32
    )
    scores = jnp.where(allowed, scores * HEAD ** (-0.5), MASKED)
    peak = jnp.max(scores, axis=-1, keepdims=True)
    shifted = jnp.exp(scores - peak)
    total = jnp.sum(shifted, axis=-1, keepdims=True)
    probs = shifted / total
    weights = probs.astype(jnp.bfloat16)
    mixed = jnp.einsum("bgrij,bjgd->bigrd", weights, value_heads, preferred_element_type=jnp.float32)
    mixed = mixed.reshape(count, D).astype(jnp.bfloat16)
    middle = inputs + product(mixed, out_weight)
    second_scale = lax.rsqrt(jnp.mean(middle * middle, axis=-1, keepdims=True) + NORM_EPSILON)
    second_normed = middle * second_scale
    normed_two = (second_normed * second_gain).astype(jnp.bfloat16)
    gate = outer_cols(normed_two, gate_rows)
    up = outer_cols(normed_two, up_rows)
    sigma = jax.nn.sigmoid(gate)
    hidden = (gate * sigma * up).astype(jnp.bfloat16)
    result = ((middle + product(hidden, down_weight)) * live).astype(jnp.bfloat16)
    back = cotangent.astype(jnp.float32).reshape(count, D) * live
    back_half = back.astype(jnp.bfloat16)
    grad_down_w = inner_rows(hidden, back_half)
    grad_hidden = outer_cols(back_half, down_weight)
    grad_gate = (grad_hidden * up * sigma * (1.0 + gate * (1.0 - sigma))).astype(jnp.bfloat16)
    grad_up = (grad_hidden * gate * sigma).astype(jnp.bfloat16)
    grad_gate_w = inner_rows(grad_gate, normed_two)
    grad_up_w = inner_rows(grad_up, normed_two)
    grad_normed_two = product(grad_gate, gate_rows) + product(grad_up, up_rows)
    second_gain_grad = jnp.sum(grad_normed_two * second_normed, axis=0)
    grad_middle = back + norm_back(grad_normed_two * second_gain, second_normed, second_scale)
    branch_grad = grad_middle.astype(jnp.bfloat16)
    grad_out_w = inner_rows(mixed, branch_grad)
    grad_mixed = outer_cols(branch_grad, out_weight).astype(jnp.bfloat16)
    grad_mixed = grad_mixed.reshape(batch, rows, KV_HEADS, group, HEAD)
    grad_probs = jnp.einsum(
        "bigrd,bjgd->bgrij", grad_mixed, value_heads, preferred_element_type=jnp.float32
    )
    grad_scores = probs * (grad_probs - jnp.sum(probs * grad_probs, axis=-1, keepdims=True))
    grad_scores = grad_scores.astype(jnp.bfloat16)
    grad_query = jnp.einsum(
        "bgrij,bjgd->bigrd", grad_scores, key_heads, preferred_element_type=jnp.float32
    ) * HEAD ** (-0.5)
    grad_key = jnp.einsum(
        "bgrij,bigrd->bjgd", grad_scores, query_heads, preferred_element_type=jnp.float32
    ) * HEAD ** (-0.5)
    grad_value = jnp.einsum(
        "bgrij,bigrd->bjgd", weights, grad_mixed, preferred_element_type=jnp.float32
    )
    grad_value = grad_value.astype(jnp.bfloat16).reshape(count, kv_width)
    grad_query = (
        rotary_grad(grad_query.reshape(batch, rows, HEADS, HEAD), cosine, sine)
        .astype(jnp.bfloat16)
        .reshape(count, D)
    )
    grad_key = rotary_grad(grad_key, cosine, sine).astype(jnp.bfloat16).reshape(count, kv_width)
    query_bias_grad = jnp.sum(grad_query.astype(jnp.float32), axis=0)
    key_bias_grad = jnp.sum(grad_key.astype(jnp.float32), axis=0)
    value_bias_grad = jnp.sum(grad_value.astype(jnp.float32), axis=0)
    grad_query_w = inner_rows(normed, grad_query)
    grad_key_w = inner_rows(normed, grad_key)
    grad_value_w = inner_rows(normed, grad_value)
    grad_normed = (
        outer_cols(grad_query, query_weight)
        + outer_cols(grad_key, key_weight)
        + outer_cols(grad_value, value_weight)
    )
    first_gain_grad = jnp.sum(grad_normed * first_normed, axis=0)
    grad_inputs = (
        grad_middle + norm_back(grad_normed * first_gain, first_normed, first_scale)
    ).astype(jnp.bfloat16)
    vector_grad = jnp.concatenate(
        [first_gain_grad, second_gain_grad, query_bias_grad, key_bias_grad, value_bias_grad]
    )
    grads = (
        grad_query_w,
        grad_key_w,
        grad_value_w,
        grad_out_w,
        grad_gate_w,
        grad_up_w,
        grad_down_w,
        vector_grad,
    )
    return (
        result.reshape(batch, 1, rows, D),
        grad_inputs.reshape(batch, 1, rows, D),
        grads,
    )


def half(value):
    return value.astype(jnp.bfloat16)


def mixing(gram):
    gram_half = half(gram)
    first = half(NEWTON_B * gram + NEWTON_C * product(gram_half, gram_half))
    cross = product(gram_half, first)
    after = (
        NEWTON_A * NEWTON_A * gram + 2.0 * NEWTON_A * cross + product(half(cross), first)
    )
    after_half = half(after)
    second = NEWTON_B * after + NEWTON_C * product(after_half, after_half)
    return half(
        NEWTON_A * (first.astype(jnp.float32) + second) + product(first, half(second))
    )


def body(
    inputs,
    cotangent,
    lengths,
    query_weight,
    key_weight,
    value_weight,
    out_weight,
    gate_weight,
    up_weight,
    down_weight,
    vectors,
    query_prior,
    key_prior,
    value_prior,
    out_prior,
    gate_prior,
    up_prior,
    down_prior,
    first_prior,
    second_prior,
):
    axes = ("dp", "narrow")
    count = lax.axis_size("dp") * lax.axis_size("narrow")
    index = lax.axis_index("dp") * lax.axis_size("narrow") + lax.axis_index("narrow")
    rows = query_weight.shape[0]
    units = down_weight.shape[0]
    kv_width = key_weight.shape[1]
    packed = half(
        jnp.concatenate([query_weight, out_weight, gate_weight.T, up_weight.T, down_weight])
    )
    narrow = half(jnp.concatenate([key_weight, value_weight], axis=1))
    gathered = lax.all_gather(packed, axes, axis=0)
    gathered_narrow = lax.all_gather(narrow, axes, axis=0)
    gathered_vectors = lax.all_gather(half(vectors), axes, axis=0)
    cuts = (0, rows, 2 * rows, 2 * rows + units, 2 * rows + 2 * units, 2 * rows + 3 * units)
    pieces = [
        gathered[:, cuts[k] : cuts[k + 1]].reshape(count * (cuts[k + 1] - cuts[k]), D)
        for k in range(5)
    ]
    full = (
        pieces[0],
        gathered_narrow[:, :, :kv_width].reshape(D, kv_width),
        gathered_narrow[:, :, kv_width:].reshape(D, kv_width),
        pieces[1],
        pieces[2],
        pieces[3],
        pieces[4],
        gathered_vectors.reshape(-1),
    )
    own_lengths = lax.dynamic_slice_in_dim(lengths, index, 1, axis=1)[:, 0]
    block_output, input_grad, grads = slot_pass(full, inputs[:, 0], cotangent[:, 0], own_lengths)
    wide = jnp.concatenate(
        [
            half(grads[k]).reshape(count, -1, D)
            for k in (0, 3, 4, 5, 6)
        ],
        axis=1,
    )
    thin = jnp.concatenate(
        [
            half(grads[1]).reshape(count, rows, kv_width),
            half(grads[2]).reshape(count, rows, kv_width),
        ],
        axis=2,
    )
    own_wide = lax.psum_scatter(wide, axes, scatter_dimension=0).astype(jnp.float32)
    own_thin = lax.psum_scatter(thin, axes, scatter_dimension=0).astype(jnp.float32)
    grad_vector = lax.psum_scatter(grads[7], axes, scatter_dimension=0, tiled=True)
    owned = (
        own_wide[cuts[0] : cuts[1]],
        own_thin[:, :kv_width],
        own_thin[:, kv_width:],
        own_wide[cuts[1] : cuts[2]],
        own_wide[cuts[2] : cuts[3]],
        own_wide[cuts[3] : cuts[4]],
        own_wide[cuts[4] : cuts[5]],
    )
    priors = (
        query_prior,
        key_prior,
        value_prior,
        out_prior,
        gate_prior.T,
        up_prior.T,
        down_prior,
    )
    masters = (
        query_weight,
        key_weight,
        value_weight,
        out_weight,
        gate_weight,
        up_weight,
        down_weight,
    )
    shapes = ((D, D), (D, kv_width), (D, kv_width), (D, D), (D, FF), (D, FF), (FF, D))
    lefts = (False, False, False, False, True, True, False)
    momenta = tuple((MOMENTUM * priors[k] + owned[k] for k in range(7)))
    partial = [half(inner_rows(half(moment), half(moment))) for moment in momenta]
    big = lax.psum(jnp.stack([partial[k] for k in (0, 3, 4, 5, 6)]), axes).astype(jnp.float32)
    small = lax.psum(jnp.stack([partial[k] for k in (1, 2)]), axes).astype(jnp.float32)
    grams = (big[0], small[0], small[1], big[1], big[2], big[3], big[4])
    updated = []
    kept = []
    for k in range(7):
        gram = grams[k]
        norm = jnp.sqrt(jnp.trace(gram)) + 1e-07
        inverse = 1.0 / norm
        mixer = mixing(gram * inverse * inverse)
        current = momenta[k] * inverse
        current = NEWTON_A * NEWTON_A * current + product(half(current), mixer)
        factor = MUON_RATE * 0.2 * math.sqrt(max(shapes[k][0], shapes[k][1]))
        if lefts[k]:
            current = current.T
        updated.append(masters[k] * (1.0 - MUON_RATE * MUON_DECAY) - factor * current)
        kept.append(momenta[k].T if lefts[k] else momenta[k])
    vector_first = BETA_FIRST * first_prior + (1.0 - BETA_FIRST) * grad_vector
    vector_second = BETA_SECOND * second_prior + (1.0 - BETA_SECOND) * grad_vector * grad_vector
    first_hat = vector_first / (1.0 - BETA_FIRST**STEP)
    second_hat = vector_second / (1.0 - BETA_SECOND**STEP)
    vector_new = vectors * (1.0 - ADAM_RATE * ADAM_DECAY) - ADAM_RATE * first_hat / (
        jnp.sqrt(second_hat) + ADAM_EPSILON
    )
    return (
        block_output,
        input_grad,
        *kept,
        *updated,
        vector_first,
        vector_second,
        vector_new,
    )


def solution(mesh):
    placed = (
        P(None, ("dp", "narrow"), None, None),
        P(None, ("dp", "narrow"), None, None),
        P(),
        P(("dp", "narrow"), None),
        P(("dp", "narrow"), None),
        P(("dp", "narrow"), None),
        P(("dp", "narrow"), None),
        P(None, ("dp", "narrow")),
        P(None, ("dp", "narrow")),
        P(("dp", "narrow"), None),
        P(("dp", "narrow")),
        P(("dp", "narrow"), None),
        P(("dp", "narrow"), None),
        P(("dp", "narrow"), None),
        P(("dp", "narrow"), None),
        P(None, ("dp", "narrow")),
        P(None, ("dp", "narrow")),
        P(("dp", "narrow"), None),
        P(("dp", "narrow")),
        P(("dp", "narrow")),
    )
    return jax.shard_map(
        body,
        mesh=mesh,
        in_specs=placed,
        out_specs=(
            P(None, ("dp", "narrow"), None, None),
            P(None, ("dp", "narrow"), None, None),
            P(("dp", "narrow"), None),
            P(("dp", "narrow"), None),
            P(("dp", "narrow"), None),
            P(("dp", "narrow"), None),
            P(None, ("dp", "narrow")),
            P(None, ("dp", "narrow")),
            P(("dp", "narrow"), None),
            P(("dp", "narrow"), None),
            P(("dp", "narrow"), None),
            P(("dp", "narrow"), None),
            P(("dp", "narrow"), None),
            P(None, ("dp", "narrow")),
            P(None, ("dp", "narrow")),
            P(("dp", "narrow"), None),
            P(("dp", "narrow")),
            P(("dp", "narrow")),
            P(("dp", "narrow")),
        ),
        check_vma=False,
    )
```

time: 3030 us -> 1940 us (0.64)
  blocking collectives: 1130 us -> 174 us
  starting transfers between devices: 547 us -> 0.55 us
  waiting for transfers between devices: 729 us -> 1090 us
  local copies, waits for them, and re-layouts: 287 us -> 368 us
  matrix products: 252 us -> 220 us
    reduce_scatter x0 -> x2, waiting for transfers between devices: none -> 1020 us  [the longest x1 682 us: body(): lax.psum_scatter(wide, axes, scatter_dimension=0).astype(jnp.float32)]
    unnamed x2, blocking collectives: 802 us -> 135 us
    psum x2 -> x1, waiting for transfers between devices: 436 us -> 70.7 us  [body(): lax.psum(jnp.stack([partial[k] for k in (0, 3, 4, 5, 6)]), axes)]
    unnamed x82 -> x0, starting transfers between devices: 338 us -> none
    concatenate x0 -> x2, local copies, waits for them, and re-layouts: none -> 233 us  [the longest x1 226 us: body(): jnp.concatenate([half(grads[k]).reshape(count, -1, D) for k in (0, 3, 4,...]
    ppermute x48 -> x0, starting transfers between devices: 208 us -> none  [from_partner(): lax.ppermute(x, axis, [(i, i ^ 1 << distance) for i in range(lax.axis_siz...]
    all_gather x10 -> x1, waiting for transfers between devices: 188 us -> 0.01 us  [body(): gathered = lax.all_gather(packed, axes, axis=0)]
    while x300 -> x0, local copies, waits for them, and re-layouts: 138 us -> none
  transfers between devices with their start and end apart: 142 -> 4, of which waited for: 32 -> 3; matrix products, arithmetic and copies ran while one was open for 27% -> 17% of each run, Pallas kernels for 0% -> 0%
where the time goes in v1:
time: 1940 us; the launch traced here: 1920 us
  waiting for transfers between devices  1090 us (56%)
  local copies, waits for them, and re-layouts  368 us (19%)
  matrix products  220 us (11%)
  blocking collectives  174 us (9%)
  other arithmetic  48.3 us (2%)
  between operations  20.4 us (1%)
    reduce_scatter x1, waiting for transfers between devices, body(): lax.psum_scatter(wide, axes, scatter_dimension=0).astype(jnp.float32)  682 us
    reduce_scatter x1, waiting for transfers between devices, body(): lax.psum_scatter(thin, axes, scatter_dimension=0).astype(jnp.float32)  334 us
    concatenate x1, local copies, waits for them, and re-layouts, body(): jnp.concatenate([half(grads[k]).reshape(count, -1, D) for k in (0, 3, 4,...  226 us
    dot_general x42, matrix products, product(): return jnp.dot(left, right, preferred_element_type=jnp.float32)  138 us
    unnamed x2, blocking collectives  135 us
    psum x1, waiting for transfers between devices, body(): lax.psum(jnp.stack([partial[k] for k in (0, 3, 4, 5, 6)]), axes)  70.7 us
    reshape x5, local copies, waits for them, and re-layouts, body(): gathered[:, cuts[k]:cuts[k + 1]].reshape(count * (cuts[k + 1] - cuts[k]), D)  43.4 us
    reshape x5, local copies, waits for them, and re-layouts, body(): half(grads[k]).reshape(count, -1, D)  41.8 us
  transfers between devices with their start and end apart: 4, of which 3 were waited for; matrix products, arithmetic and copies ran while one was open for 17% of the time, Pallas kernels for 0%

profile of v1, /device:TPU:1, one launch (start us, length us, event | category | flops | bytes accessed | tf_op | source)
XLA Modules:
  0.0 1919.1 jit_solution(11857453849429309055)
XLA Ops:
  10.0 6.3 concatenate.90
  17.8 39.8 %all_gather.16 = bf16[128,7,256]{2,1,0:T(8,128)(2,1)S(1)} all-gather(bf16[1,7,256]{2,1,0:T(8,128)(2,1)S(1)} %pad_maximum_fusion.3), channel_id=1, replica_groups=mesh['dp'=64,'narrow'=2] {'dp','narrow'}, dimensions={0}, use_global_device_ids=true | all-gather | bytes 462336 | tf_op jit(solution)/shard_map/all_gather | solution.py:259
  58.0 65.4 %all-reduce = bf16[2944]{0:T(1024)(128)(2,1)S(1)} all-reduce(bf16[2944]{0:T(1024)(128)(2,1)S(1)} %dynamic-update-slice), channel_id=2, replica_groups=mesh['dp'=64,'narrow'=2] {'dp','narrow'}, use_global_device_ids=true, to_apply=%add | all-reduce | flops 2944 | bytes 11776
  129.8 4.4 fusion.282
  135.7 2.1 convolution_add_fusion.3
  140.0 27.2 %fusion.281 = (bf16[128,38,896]{2,1,0:T(8,128)(2,1)}, bf16[128,38,896]{2,1,0:T(8,128)(2,1)}, bf16[128,38,896]{2,1,0:T(8,128)(2,1)}) fusion(bf16[128,128,896]{2,1,0:T(8,128)(2,1)} %all-gather.3.cloned.1.call-done), kind=kLoop, calls=%fused_computation.373 | loop fusion | bytes 52297728 | tf_op jit(solution)/shard_map/slice | solution.py:263
  167.2 12.9 reshape.527
  181.4 2.8 reshape.524
  184.2 2.9 fusion.156
  187.0 3.0 fusion.288
  194.0 13.3 reshape.526
  207.3 12.9 reshape.525
  220.5 10.2 fusion.294
  230.6 9.9 fusion.293
  240.6 9.0 multiply_convert_fusion
  249.7 7.2 fusion.295
  257.0 3.5 multiply_reduce_fusion
  260.5 2.3 fusion.162
  265.0 2.5 reshape.558
  267.6 2.7 copy.92
  270.2 2.8 convert_reduce_fusion.1
  273.1 2.3 fusion.16
  279.8 2.6 fusion.18
  292.0 8.0 convolution_convert_fusion
  300.0 12.9 reshape.538
  312.9 7.8 convolution_convert_fusion.1
  320.8 12.9 reshape.537
  333.7 7.9 convolution_convert_fusion.2
  341.6 12.9 reshape.536
  354.5 226.5 %concatenate.96 = bf16[128,128,896]{2,1,0:T(8,128)(2,1)} concatenate(bf16[128,7,896]{2,1,0:T(8,128)(2,1)} %reshape.534, bf16[128,7,896]{2,1,0:T(8,128)(2,1)} %reshape.535, bf16[128,38,896]{2,1,0:T(8,128)(2,1)} %reshape.536, bf16[128,38,896]{2,1,0:T(8,128)(2,1)} %reshape.537, bf16[128,38,896]{2,1,0:T(8,128)(2,1)} %reshape.538), dimensions={1} | concatenate | bytes 58720256 | tf_op jit(solution)/shard_map/concatenate | solution.py:278
  581.3 334.1 %reduce-scatter.5.cloned.1.call-done = bf16[1,7,256]{2,1,0:T(8,128)(2,1)} async-done(((bf16[128,7,256]{2,1,0:T(8,128)(2,1)}), bf16[1,7,256]{2,1,0:T(8,128)(2,1)}) %reduce-scatter.5.cloned.1.call-update) | async-done | bytes 3600 | tf_op jit(solution)/shard_map/reduce_scatter | solution.py:293
  917.2 681.9 %reduce-scatter.3.cloned.1.call-done = bf16[1,128,896]{2,1,0:T(8,128)(2,1)} async-done(((bf16[128,128,896]{2,1,0:T(8,128)(2,1)}), bf16[1,128,896]{2,1,0:T(8,128)(2,1)}) %reduce-scatter.3.cloned.1.call-update) | async-done | bytes 229392 | tf_op jit(solution)/shard_map/reduce_scatter | solution.py:292
  1614.2 2.3 convert_reduce_fusion
  1621.9 69.2 %all-reduce.1 = f32[2944]{0:T(1024)S(1)} all-reduce(f32[2944]{0:T(1024)S(1)} %constant_dynamic-update-slice_fusion.1), channel_id=5, replica_groups=mesh['dp'=64,'narrow'=2] {'dp','narrow'}, use_global_device_ids=true, to_apply=%region_23.24.clone | all-reduce | flops 2944 | bytes 23552
  1691.7 2.3 add_convert_fusion.10
  1694.0 7.8 fusion.72
  1701.8 70.7 %all-reduce.5.cloned.1.call-done = (bf16[5,896,896]{2,1,0:T(8,128)(2,1)}, bf16[2,128,128]{2,1,0:T(8,128)(2,1)}) async-done(((bf16[5,896,896]{2,1,0:T(8,128)(2,1)}, bf16[2,128,128]{2,1,0:T(8,128)(2,1)}), (bf16[5,896,896]{2,1,0:T(8,128)(2,1)}, bf16[2,128,128]{2,1,0:T(8,128)(2,1)})) %all-reduce.5.cloned.1.call-update) | async-done | bytes 8093712 | tf_op jit(solution)/shard_map/psum | solution.py:326
  1778.4 9.9 convert_element_type.531
  1788.3 7.2 fusion.1
  1799.2 6.0 add_convert_fusion.1
  1805.2 7.8 add_convert_fusion.3
  1813.0 3.3 add_convert_fusion.5
  1816.4 3.3 add_convert_fusion.7
  1819.7 2.1 add_convert_fusion.9
  1821.9 2.0 fusion.28
  1823.9 2.3 add_add_fusion.4
  1826.2 3.7 multiply_add_fusion.4
  1829.9 6.7 fusion.146
  1836.6 4.5 fusion.26
  1841.2 4.1 add_add_fusion.3
  1845.3 3.7 multiply_add_fusion.3
  1849.0 6.7 fusion.137
  1855.7 4.7 fusion.24
  1860.4 4.1 add_add_fusion.2
  1864.5 3.7 multiply_add_fusion.2
  1868.3 6.8 fusion.113
  1875.1 4.5 fusion.22
  1879.6 4.1 add_add_fusion.1
  1883.7 3.7 multiply_add_fusion.1
  1887.4 7.1 fusion.101
  1894.5 3.9 fusion.20
  1898.4 4.1 add_add_fusion
  1902.5 3.7 multiply_add_fusion
  1906.2 6.0 fusion.89
  (286 shorter events, 63.2 us)
Async XLA Ops:
  7.2 119.1 %copy-start = (s32[2,128]{1,0:T(2,128)S(1)}, s32[2,128]{1,0:T(2,128)}, u32[]{:S(2)}) copy-start(s32[2,128]{1,0:T(2,128)} %param.22) | copy-start | bytes 3076
  7.2 116.2 %copy-start.3 = (bf16[2,1,128,896]{3,2,1,0:T(8,128)(2,1)S(1)}, bf16[2,1,128,896]{3,2,1,0:T(8,128)(2,1)}, u32[]{:S(2)}) copy-start(bf16[2,1,128,896]{3,2,1,0:T(8,128)(2,1)} %param.20) | copy-start | bytes 1376260
  7.2 122.6 %all-gather.3.cloned.1.call-start = ((), (), s32[]{:S(2)}) async-start(), calls=%async_computation.2 | async-start | bytes 29589504 | tf_op jit(solution)/shard_map/all_gather | solution.py:258
  16.4 899.0 %reduce-scatter.5.cloned.1.call-start = ((), (), s32[]{:S(2)}) async-start(), calls=%async_computation.4 | async-start | bytes 528384 | tf_op jit(solution)/shard_map/reduce_scatter | solution.py:293
  57.6 71.3 %copy-start.25 = (bf16[2,1,128,896]{3,2,1,0:T(8,128)(2,1)S(1)}, bf16[2,1,128,896]{3,2,1,0:T(8,128)(2,1)}, u32[]{:S(2)}) copy-start(bf16[2,1,128,896]{3,2,1,0:T(8,128)(2,1)} %param.21) | copy-start | bytes 1376260
  57.7 72.1 %copy-start.20 = (bf16[896,128]{1,0:T(8,128)(2,1)}, bf16[896,128]{1,0:T(8,128)(2,1)S(1)}, u32[]{:S(2)}) copy-start(bf16[896,128]{1,0:T(8,128)(2,1)S(1)} %reshape.519) | copy-start | bytes 688132
  125.2 4.6 copy-start.22
  127.3 56.8 %copy-start.35 = (f32[128,64]{0,1:T(8,128)}, f32[128,64]{0,1:T(8,128)S(1)}, u32[]{:S(2)}) copy-start(f32[128,64]{0,1:T(8,128)S(1)} %get-tuple-element.121) | copy-start | bytes 98308
  127.4 133.1 %copy-start.65 = (f32[256]{0:T(256)}, f32[256]{0:T(256)S(1)}, u32[]{:S(2)}) copy-start(f32[256]{0:T(256)S(1)} %get-tuple-element.133) | copy-start | bytes 3076
  180.2 4.0 copy-start.17
  194.0 62.9 %copy-start.4 = (f32[256,896]{1,0:T(8,128)}, f32[256,896]{1,0:T(8,128)S(1)}, u32[]{:S(2)}) copy-start(f32[256,896]{1,0:T(8,128)S(1)} %get-tuple-element.138) | copy-start | bytes 2752516
  220.4 10.2 copy-start.13
  220.4 20.1 %slice-start = ((s8[8716288]{0:T(1024)(128)(4,1)}), s8[4194304]{0:T(1024)(128)(4,1)S(1)}, s32[]{:S(2)}) async-start(s8[8716288]{0:T(1024)(128)(4,1)} %bitcast.417), calls=%async_computation.6 | async-start | bytes 8388608
  220.5 20.1 %slice-start.1 = ((s8[8716288]{0:T(1024)(128)(4,1)}), s8[4194304]{0:T(1024)(128)(4,1)S(1)}, s32[]{:S(2)}) async-start(s8[8716288]{0:T(1024)(128)(4,1)} %bitcast.417), calls=%async_computation.7 | async-start | bytes 8388608
  230.6 10.0 slice-start.2
  240.6 16.3 slice-start.3
  240.6 16.3 slice-start.4
  249.7 7.2 copy-start.15
  249.7 7.2 slice-start.5
  249.7 7.2 copy-start.16
  260.5 3.9 copy-start.11
  279.8 3.9 copy-start.27
  279.8 3.9 copy-start.45
  286.7 1312.4 %reduce-scatter.3.cloned.1.call-start = ((), (), s32[]{:S(2)}) async-start(), calls=%async_computation.3 | async-start | bytes 29589504 | tf_op jit(solution)/shard_map/reduce_scatter | solution.py:292
  300.0 13.0 copy-start.14
  581.0 335.1 %copy-start.68 = (f32[7,128]{1,0:T(8,128)S(1)}, f32[7,128]{1,0:T(8,128)}, u32[]{:S(2)}) copy-start(f32[7,128]{1,0:T(8,128)} %param.33) | copy-start | bytes 10756
  581.0 335.1 %copy-start.69 = (f32[7,128]{1,0:T(8,128)S(1)}, f32[7,128]{1,0:T(8,128)}, u32[]{:S(2)}) copy-start(f32[7,128]{1,0:T(8,128)} %param.32) | copy-start | bytes 10756
  581.0 1019.1 %copy-start.53 = (f32[7,896]{1,0:T(8,128)S(1)}, f32[7,896]{1,0:T(8,128)}, u32[]{:S(2)}) copy-start(f32[7,896]{1,0:T(8,128)} %param.34) | copy-start | bytes 75268
  581.0 1019.1 %copy-start.54 = (f32[7,896]{1,0:T(8,128)S(1)}, f32[7,896]{1,0:T(8,128)}, u32[]{:S(2)}) copy-start(f32[7,896]{1,0:T(8,128)} %param.31) | copy-start | bytes 75268
  581.0 1022.7 %copy-start.31 = (f32[896,38]{0,1:T(8,128)S(1)}, f32[896,38]{0,1:T(8,128)}, u32[]{:S(2)}) copy-start(f32[896,38]{0,1:T(8,128)} %param.35) | copy-start | bytes 408580
  581.0 1191.5 %all-reduce.5.cloned.1.call-start = ((), (), s32[]{:S(2)}) async-start(), calls=%async_computation.5 | async-start | bytes 16187392 | tf_op jit(solution)/shard_map/psum | solution.py:326
  916.1 860.1 %copy-start.52 = (f32[7,128]{1,0:T(8,128)}, f32[7,128]{1,0:T(8,128)S(1)}, u32[]{:S(2)}) copy-start(f32[7,128]{1,0:T(8,128)S(1)} %get-tuple-element.124) | copy-start | bytes 10756
  916.1 861.4 %copy-start.51 = (f32[7,128]{1,0:T(8,128)}, f32[7,128]{1,0:T(8,128)S(1)}, u32[]{:S(2)}) copy-start(f32[7,128]{1,0:T(8,128)S(1)} %get-tuple-element.123) | copy-start | bytes 10756
  916.5 689.1 %copy-start.33 = (f32[896,38]{0,1:T(8,128)S(1)}, f32[896,38]{0,1:T(8,128)}, u32[]{:S(2)}) copy-start(f32[896,38]{0,1:T(8,128)} %param.36) | copy-start | bytes 408580
  916.5 689.1 %copy-start.41 = (f32[38,896]{1,0:T(8,128)S(1)}, f32[38,896]{1,0:T(8,128)}, u32[]{:S(2)}) copy-start(f32[38,896]{1,0:T(8,128)} %param.37) | copy-start | bytes 408580
  1600.1 6.3 copy-start.18
  1600.1 6.3 copy-start.46
  1600.1 6.3 copy-start.57
  1610.1 4.1 copy-start.39
  1610.1 7.1 copy-start.6
  1613.0 6.1 copy-start.21
  1614.2 6.2 copy-start.23
  1614.2 6.3 copy-start.49
  1614.2 6.3 copy-start.64
  1617.3 4.5 copy-start.63
  1617.3 4.6 copy-start.67
  1617.3 4.6 copy-start.75
  1617.3 4.6 copy-start.74
  1619.1 72.0 %copy-start.70 = (f32[23]{0:T(128)S(1)}, f32[23]{0:T(128)}, u32[]{:S(2)}) copy-start(f32[23]{0:T(128)} %param.30) | copy-start | bytes 280
  1619.1 72.0 %copy-start.71 = (f32[23]{0:T(128)S(1)}, f32[23]{0:T(128)}, u32[]{:S(2)}) copy-start(f32[23]{0:T(128)} %param.39) | copy-start | bytes 280
  1619.1 72.0 %copy-start.72 = (f32[23]{0:T(128)S(1)}, f32[23]{0:T(128)}, u32[]{:S(2)}) copy-start(f32[23]{0:T(128)} %param.38) | copy-start | bytes 280
  1620.4 73.6 %copy-start.5 = (f32[256,896]{1,0:T(8,128)S(1)}, f32[256,896]{1,0:T(8,128)}, u32[]{:S(2)}) copy-start(f32[256,896]{1,0:T(8,128)} %copy-done.4) | copy-start | bytes 2752516
  1620.4 73.6 %copy-start.66 = (f32[256]{0:T(256)S(1)}, f32[256]{0:T(256)}, u32[]{:S(2)}) copy-start(f32[256]{0:T(256)} %copy-done.65) | copy-start | bytes 3076
  1694.0 82.2 %copy-start.61 = (f32[7,128]{1,0:T(8,128)S(1)}, f32[7,128]{1,0:T(8,128)}, u32[]{:S(2)}) copy-start(f32[7,128]{1,0:T(8,128)} %param.24) | copy-start | bytes 10756
  1694.0 83.5 %copy-start.62 = (f32[7,128]{1,0:T(8,128)S(1)}, f32[7,128]{1,0:T(8,128)}, u32[]{:S(2)}) copy-start(f32[7,128]{1,0:T(8,128)} %param.25) | copy-start | bytes 10756
  1799.2 13.9 copy-start.2
  1836.6 4.5 copy-start.78
  1855.7 4.7 copy-start.77
  1864.5 3.8 copy-start.19
  1864.5 3.7 copy-start.32
  1875.1 4.5 copy-start.76
  1883.7 3.7 copy-start.34
  1902.5 3.7 copy-start.30
  1902.5 9.8 copy-start.1
  (26 other events, 69.7 us)
Sparse Core Ops, SparseCore 0:
  16.5 104.6 all-gather.2
  286.8 628.5 reduce-scatter.4
  917.9 681.0 reduce-scatter.2
  1610.3 162.2 all-reduce.4

commit v2 on v1

--- a/solution.py
+++ b/solution.py
@@ -3,6 +3,8 @@
 import jax
 import jax.numpy as jnp
 from jax import lax
+from jax.experimental import pallas as pl
+from jax.experimental.pallas import tpu as pltpu
 from jax.sharding import PartitionSpec as P
 
 D = 896
@@ -75,20 +77,517 @@
     return scale * (grad - normed * jnp.mean(grad * normed, axis=-1, keepdims=True))
 
 
+MESH = pl.DeviceIdType.MESH
+ROWS = 144
+PART = 48
+GATHER_ORDERS = ((2, 1, 0), (1, 0, 2), (0, 2, 1))
+
+
+def my_coords():
+    dp = lax.axis_index("dp")
+    return (dp // 16, (dp // 4) % 4, dp % 4), lax.axis_index("narrow")
+
+
+def device_of(coords, core):
+    return (coords[0] * 16 + coords[1] * 4 + coords[2], core)
+
+
+def shifted(coords, axis, by):
+    out = list(coords)
+    out[axis] = (coords[axis] + by) % 4
+    return tuple(out)
+
+
+def ring_barrier(coords, core):
+    barrier = pltpu.get_barrier_semaphore()
+    for axis in range(3):
+        for by in (1, 3):
+            pl.semaphore_signal(
+                barrier, inc=1, device_id=device_of(shifted(coords, axis, by), core), device_id_type=MESH
+            )
+    pl.semaphore_signal(barrier, inc=1, device_id=device_of(coords, 1 - core), device_id_type=MESH)
+    pl.semaphore_wait(barrier, 7)
+
+
+def region(spec, part, rows=None):
+    index = []
+    for axis in range(2):
+        s = spec[axis]
+        index.append(pl.ds(*s) if isinstance(s, tuple) else s)
+    s = spec[2]
+    if isinstance(s, tuple):
+        index += [pl.ds(s[0] // 2, s[1] // 2), slice(None)]
+    else:
+        index += [s // 2, s % 2]
+    rows = (0, PART) if rows is None else rows
+    return (*index, pl.ds(part * PART + rows[0], rows[1]), slice(None))
+
+
+FULL = (0, 4)
+
+
+def halves(spec, split_axis):
+    if split_axis is None:
+        return [(spec, (0, 32)), (spec, (32, 16))]
+    out = []
+    for h in range(2):
+        s = list(spec)
+        s[split_axis] = (2 * h, 2)
+        out.append((tuple(s), None))
+    return out
+
+
+def gather_kernel(block_ref, out_ref, rest_ref, local_sem, send_sems, recv_sems, rest_sems):
+    coords, core = my_coords()
+    own = (coords[0], coords[1], coords[2])
+    local = pltpu.make_async_copy(
+        block_ref, out_ref.at[coords[0], coords[1], coords[2] // 2, coords[2] % 2], local_sem
+    )
+    local.start()
+    ring_barrier(coords, core)
+    local.wait()
+    sends = []
+
+    def send(part, phase, slot, piece, axis, by):
+        spec, rows = piece
+        ref = out_ref.at[region(spec, part, rows)]
+        copy = pltpu.make_async_remote_copy(
+            src_ref=ref,
+            dst_ref=ref,
+            send_sem=send_sems.at[part, phase, slot],
+            recv_sem=recv_sems.at[part, phase, slot],
+            device_id=device_of(shifted(coords, axis, by), core),
+            device_id_type=MESH,
+        )
+        copy.start()
+        sends.append(copy)
+
+    def wait(part, phase, slot, piece):
+        spec, rows = piece
+        ref = out_ref.at[region(spec, part, rows)]
+        pltpu.make_async_remote_copy(
+            src_ref=ref,
+            dst_ref=ref,
+            send_sem=send_sems.at[part, phase, slot],
+            recv_sem=recv_sems.at[part, phase, slot],
+            device_id=device_of(shifted(coords, 0, 1), core),
+            device_id_type=MESH,
+        ).wait_recv()
+
+    for phase in range(3):
+        specs = []
+        for part, order in enumerate(GATHER_ORDERS):
+            axis = order[phase]
+            split = order[phase - 1] if phase else None
+
+            def spec_at(by, order=order, axis=axis):
+                spec = [FULL if order.index(k) < phase else coords[k] for k in range(3)]
+                spec[axis] = (coords[axis] + by) % 4
+                return tuple(spec)
+
+            specs.append((axis, spec_at, split))
+        for part, (axis, spec_at, split) in enumerate(specs):
+            h0, h1 = halves(spec_at(0), split)
+            send(part, phase, 0, h0, axis, 1)
+            send(part, phase, 1, h1, axis, 3)
+            send(part, phase, 2, h1, axis, 1)
+            send(part, phase, 3, h0, axis, 3)
+        for part, (axis, spec_at, split) in enumerate(specs):
+            wait(part, phase, 0, halves(spec_at(3), split)[0])
+            send(part, phase, 4, halves(spec_at(3), split)[0], axis, 1)
+            wait(part, phase, 1, halves(spec_at(1), split)[1])
+            send(part, phase, 5, halves(spec_at(1), split)[1], axis, 3)
+        for part, (axis, spec_at, split) in enumerate(specs):
+            wait(part, phase, 2, halves(spec_at(3), split)[1])
+            wait(part, phase, 3, halves(spec_at(1), split)[0])
+            wait(part, phase, 4, halves(spec_at(2), split)[0])
+            wait(part, phase, 5, halves(spec_at(2), split)[1])
+    last = out_ref.at[:, :, :, 1, pl.ds(96, 48)]
+    keep = pltpu.make_async_copy(last, rest_ref.at[core], local_sem)
+    give = sibling_copy(last, rest_ref.at[core], rest_sems, 0, core)
+    keep.start()
+    give.start()
+    keep.wait()
+    give.wait()
+    for copy in sends:
+        copy.wait_send()
+
+
+def gather_blocks(block):
+    return pl.pallas_call(
+        gather_kernel,
+        out_shape=(
+            jax.ShapeDtypeStruct((4, 4, 2, 2, ROWS, D), jnp.bfloat16),
+            jax.ShapeDtypeStruct((2, 4, 4, 2, 48, D), jnp.bfloat16),
+        ),
+        in_specs=[pl.BlockSpec(memory_space=pl.ANY)],
+        out_specs=(pl.BlockSpec(memory_space=pl.ANY),) * 2,
+        scratch_shapes=[
+            pltpu.SemaphoreType.DMA,
+            pltpu.SemaphoreType.DMA((3, 3, 6)),
+            pltpu.SemaphoreType.DMA((3, 3, 6)),
+            pltpu.SemaphoreType.DMA((2, 1)),
+        ],
+        compiler_params=pltpu.CompilerParams(collective_id=0, has_side_effects=True),
+    )(block)
+
+
+def region_shape(spec, rows):
+    shape = []
+    for axis in range(2):
+        if isinstance(spec[axis], tuple):
+            shape.append(spec[axis][1])
+    if isinstance(spec[2], tuple):
+        shape += [spec[2][1] // 2, 2]
+    return (*shape, PART if rows is None else rows[1], D)
+
+
+SCATTER_ORDERS = tuple(order[::-1] for order in GATHER_ORDERS)
+
+
+def static_specs(order, phase):
+    spec = [FULL if order.index(k) > phase else 0 for k in range(3)]
+    split = order[phase + 1] if phase < 2 else None
+    return [region_shape(*piece) for piece in halves(tuple(spec), split)]
+
+
+def each_block(shape, body):
+    lead = shape[:-2]
+    count = 1
+    for n in lead:
+        count *= n
+    if count == 1:
+        body((0,) * len(lead))
+        return
+
+    def step(k, carry):
+        index = []
+        for n in reversed(lead):
+            index.append(k % n)
+            k = k // n
+        body(tuple(reversed(index)))
+        return carry
+
+    lax.fori_loop(0, count, step, 0)
+
+
+def scatter_kernel(mlp_ref, rest_ref, out_ref, *scratch):
+    buffers = scratch[:54]
+    total, sibling, load_sems, send_sems, recv_sems, rest_sems = scratch[54:]
+    coords, core = my_coords()
+    loads = [
+        pltpu.make_async_copy(
+            mlp_ref.at[:, :, :, pl.ds(0, ROWS)], total.at[:, :, :, 0], load_sems.at[0]
+        ),
+        pltpu.make_async_copy(
+            mlp_ref.at[:, :, :, pl.ds(ROWS, 96)], total.at[:, :, :, 1, pl.ds(0, 96)], load_sems.at[1]
+        ),
+        pltpu.make_async_copy(rest_ref.at[core], total.at[:, :, :, 1, pl.ds(96, 48)], load_sems.at[2]),
+    ]
+    for copy in loads:
+        copy.start()
+    ring_barrier(coords, core)
+    give = sibling_copy(rest_ref.at[1 - core], sibling, rest_sems, 0, core)
+    give.start()
+    for copy in loads:
+        copy.wait()
+    give.wait()
+
+    def join(index):
+        place = (*index, 1, pl.ds(96, 48), slice(None))
+        total[place] = half(total[place].astype(jnp.float32) + sibling[index].astype(jnp.float32))
+
+    each_block((4, 4, 2, 48, D), join)
+    sends = []
+
+    def copy_of(part, phase, slot, piece, dst, axis, by):
+        spec, rows = piece
+        return pltpu.make_async_remote_copy(
+            src_ref=total.at[region(spec, part, rows)],
+            dst_ref=dst,
+            send_sem=send_sems.at[part, phase, slot],
+            recv_sem=recv_sems.at[part, phase, slot],
+            device_id=device_of(shifted(coords, axis, by), core),
+            device_id_type=MESH,
+        )
+
+    def send(*args):
+        copy = copy_of(*args)
+        copy.start()
+        sends.append(copy)
+
+    def add_piece(part, piece, *sources):
+        spec, rows = piece
+        shape = region_shape(spec, rows)
+        base = region(spec, part, rows)
+
+        def one(index):
+            place = []
+            position = 0
+            for entry in base[:4]:
+                if isinstance(entry, slice):
+                    place.append(index[position])
+                    position += 1
+                elif isinstance(entry, pl.Slice):
+                    place.append(entry.start + index[position])
+                    position += 1
+                else:
+                    place.append(entry)
+            place = (*place, base[4], slice(None))
+            value = total[place].astype(jnp.float32)
+            for source in sources:
+                value = value + source[(*index, slice(None), slice(None))].astype(jnp.float32)
+            total[place] = value.astype(jnp.bfloat16)
+
+        each_block(shape, one)
+
+    for phase in range(3):
+        plans = []
+        for part, order in enumerate(SCATTER_ORDERS):
+            axis = order[phase]
+            split = order[phase + 1] if phase < 2 else None
+
+            def pieces_at(by, order=order, axis=axis, split=split):
+                spec = [FULL if order.index(k) > phase else coords[k] for k in range(3)]
+                spec[axis] = (coords[axis] + by) % 4
+                return halves(tuple(spec), split)
+
+            base = (part * 3 + phase) * 6
+            bufs = buffers[base : base + 6]
+            plans.append((axis, pieces_at, (bufs[0], bufs[1], bufs[2:4], bufs[4:6])))
+        for part, (axis, pieces_at, bufs) in enumerate(plans):
+            far_left, far_right, near_left, near_right = bufs
+            send(part, phase, 0, pieces_at(2)[0], far_left, axis, 1)
+            send(part, phase, 1, pieces_at(2)[1], far_right, axis, 3)
+            send(part, phase, 2, pieces_at(1)[1], near_left[1], axis, 1)
+            send(part, phase, 3, pieces_at(3)[0], near_right[0], axis, 3)
+        for part, (axis, pieces_at, bufs) in enumerate(plans):
+            far_left, far_right, near_left, near_right = bufs
+            copy_of(part, phase, 0, pieces_at(2)[0], far_left, axis, 1).wait_recv()
+            add_piece(part, pieces_at(1)[0], far_left)
+            send(part, phase, 4, pieces_at(1)[0], near_left[0], axis, 1)
+            copy_of(part, phase, 1, pieces_at(2)[1], far_right, axis, 3).wait_recv()
+            add_piece(part, pieces_at(3)[1], far_right)
+            send(part, phase, 5, pieces_at(3)[1], near_right[1], axis, 3)
+        for part, (axis, pieces_at, bufs) in enumerate(plans):
+            far_left, far_right, near_left, near_right = bufs
+            copy_of(part, phase, 3, pieces_at(3)[0], near_right[0], axis, 3).wait_recv()
+            copy_of(part, phase, 4, pieces_at(1)[0], near_left[0], axis, 1).wait_recv()
+            add_piece(part, pieces_at(0)[0], near_left[0], near_right[0])
+            copy_of(part, phase, 2, pieces_at(1)[1], near_left[1], axis, 1).wait_recv()
+            copy_of(part, phase, 5, pieces_at(3)[1], near_right[1], axis, 3).wait_recv()
+            add_piece(part, pieces_at(0)[1], near_left[1], near_right[1])
+    for copy in sends:
+        copy.wait_send()
+    out_ref[...] = total[coords[0], coords[1], coords[2] // 2, coords[2] % 2]
+
+
+def scatter_blocks(mlp, rest):
+    scratch = []
+    for order in SCATTER_ORDERS:
+        for phase in range(3):
+            h0, h1 = static_specs(order, phase)
+            scratch += [pltpu.VMEM(shape, jnp.bfloat16) for shape in (h0, h1, h0, h1, h0, h1)]
+    scratch += [
+        pltpu.VMEM((4, 4, 2, 2, ROWS, D), jnp.bfloat16),
+        pltpu.VMEM((4, 4, 2, 48, D), jnp.bfloat16),
+        pltpu.SemaphoreType.DMA((3,)),
+        pltpu.SemaphoreType.DMA((3, 3, 6)),
+        pltpu.SemaphoreType.DMA((3, 3, 6)),
+        pltpu.SemaphoreType.DMA((2, 1)),
+    ]
+    return pl.pallas_call(
+        scatter_kernel,
+        out_shape=jax.ShapeDtypeStruct((ROWS, D), jnp.bfloat16),
+        in_specs=[pl.BlockSpec(memory_space=pl.ANY)] * 2,
+        out_specs=pl.BlockSpec(memory_space=pltpu.VMEM),
+        scratch_shapes=scratch,
+        compiler_params=pltpu.CompilerParams(
+            collective_id=1, has_side_effects=True, vmem_limit_bytes=56 * 2**20
+        ),
+    )(mlp, rest)
+
+
+UNITS = 80
+TILE_PAIRS = 8
+TILE = TILE_PAIRS * UNITS
+TILES = 32 // TILE_PAIRS
+TOKENS = 256
+
+
+def sibling_copy(src, dst, sems, slot, core):
+    return pltpu.make_async_remote_copy(
+        src_ref=src,
+        dst_ref=dst,
+        send_sem=sems.at[0, slot],
+        recv_sem=sems.at[1, slot],
+        device_id=(lax.axis_index("dp"), 1 - core),
+        device_id_type=MESH,
+    )
+
+
+def mlp_kernel(
+    h_ref, e_ref, gate_ref, up_ref, down_ref, out_ref, back_ref, grad_ref,
+    h_all, e_all, out_acc, back_acc, parcel, arrived, sems,
+):
+    core = lax.axis_index("narrow")
+    step = pl.program_id(0)
+
+    @pl.when(step == 0)
+    def _():
+        barrier = pltpu.get_barrier_semaphore()
+        pl.semaphore_signal(
+            barrier, inc=1, device_id=(lax.axis_index("dp"), 1 - core), device_id_type=MESH
+        )
+        pl.semaphore_wait(barrier, 1)
+        h_copy = sibling_copy(h_ref, h_all.at[core], sems, 0, core)
+        e_copy = sibling_copy(e_ref, e_all.at[core], sems, 1, core)
+        h_copy.start()
+        e_copy.start()
+        h_all[core] = h_ref[...]
+        e_all[core] = e_ref[...]
+        out_acc[...] = jnp.zeros_like(out_acc)
+        back_acc[...] = jnp.zeros_like(back_acc)
+        h_copy.wait()
+        e_copy.wait()
+
+    h = h_all[...].reshape(2 * TOKENS, D)
+    e = e_all[...].reshape(2 * TOKENS, D)
+    gate_w = gate_ref[...].reshape(TILE, D)
+    up_w = up_ref[...].reshape(TILE, D)
+    down_w = down_ref[...].reshape(TILE, D)
+    gate = outer_cols(h, gate_w)
+    up = outer_cols(h, up_w)
+    sigma = jax.nn.sigmoid(gate)
+    silu = gate * sigma
+    hidden = half(silu * up)
+    grad_hidden = outer_cols(e, down_w)
+    out_acc[...] += product(hidden, down_w).reshape(2, TOKENS, D)
+    grad_gate = half(grad_hidden * up * sigma * (1.0 + gate * (1.0 - sigma)))
+    grad_up = half(grad_hidden * silu)
+    back_acc[...] += (product(grad_gate, gate_w) + product(grad_up, up_w)).reshape(2, TOKENS, D)
+    grad_ref[:, 0:UNITS] = half(inner_rows(grad_gate, h)).reshape(TILE_PAIRS, UNITS, D)
+    grad_ref[:, UNITS : 2 * UNITS] = half(inner_rows(grad_up, h)).reshape(TILE_PAIRS, UNITS, D)
+    grad_ref[:, 2 * UNITS :] = half(inner_rows(hidden, e)).reshape(TILE_PAIRS, UNITS, D)
+
+    @pl.when(step == TILES - 1)
+    def _():
+        parcel[0] = half(out_acc[1 - core])
+        parcel[1] = half(back_acc[1 - core])
+        copy = sibling_copy(parcel, arrived, sems, 2, core)
+        copy.start()
+        copy.wait()
+        out_ref[...] = out_acc[core] + arrived[0].astype(jnp.float32)
+        back_ref[...] = back_acc[core] + arrived[1].astype(jnp.float32)
+
+
+def mlp(normed_two, back_half, weights):
+    whole = pl.BlockSpec((TOKENS, D), lambda i: (0, 0))
+    return pl.pallas_call(
+        mlp_kernel,
+        grid=(TILES,),
+        out_shape=(
+            jax.ShapeDtypeStruct((TOKENS, D), jnp.float32),
+            jax.ShapeDtypeStruct((TOKENS, D), jnp.float32),
+            jax.ShapeDtypeStruct((32, 3 * UNITS, D), jnp.bfloat16),
+        ),
+        in_specs=[
+            whole,
+            whole,
+            pl.BlockSpec((TILE_PAIRS, UNITS, D), lambda i: (i, 0, 0)),
+            pl.BlockSpec((TILE_PAIRS, UNITS, D), lambda i: (i, 1, 0)),
+            pl.BlockSpec((TILE_PAIRS, UNITS, D), lambda i: (i, 2, 0)),
+        ],
+        out_specs=(whole, whole, pl.BlockSpec((TILE_PAIRS, 3 * UNITS, D), lambda i: (i, 0, 0))),
+        scratch_shapes=[
+            pltpu.VMEM((2, TOKENS, D), jnp.bfloat16),
+            pltpu.VMEM((2, TOKENS, D), jnp.bfloat16),
+            pltpu.VMEM((2, TOKENS, D), jnp.float32),
+            pltpu.VMEM((2, TOKENS, D), jnp.float32),
+            pltpu.VMEM((2, TOKENS, D), jnp.bfloat16),
+            pltpu.VMEM((2, TOKENS, D), jnp.bfloat16),
+            pltpu.SemaphoreType.DMA((2, 3)),
+        ],
+        compiler_params=pltpu.CompilerParams(
+            collective_id=2, has_side_effects=True, vmem_limit_bytes=58 * 2**20
+        ),
+    )(normed_two, back_half, weights, weights, weights)
+
+
+def placement():
+    row = lax.broadcasted_iota(jnp.int32, (1024, D), 0)
+    feature = lax.broadcasted_iota(jnp.int32, (1024, D), 1)
+    core, pair, slot = row // 512, (row // 16) % 32, row % 16
+    source = 7 * (2 * (2 * pair + slot // 7) + core) + slot % 7
+    return half(((source == feature) & (slot < 14)).astype(jnp.float32))
+
+
+def swap_pair(value):
+    return lax.ppermute(value, "dp", [(i, i ^ 1) for i in range(64)])
+
+
+def pack_pair(pieces, parity):
+    wide, narrow, vector = pieces
+    extra = jnp.concatenate([narrow.reshape(2, D), jnp.pad(vector, (0, D - 23))[None]])
+    own = half(jnp.concatenate([wide, extra]))
+    other = swap_pair(own)
+    even = jnp.where(parity == 0, own, other).astype(jnp.float32)
+    odd = jnp.where(parity == 0, other, own).astype(jnp.float32)
+
+    def two(start, size, pad):
+        return [even[start : start + size], odd[start : start + size], jnp.zeros((pad, D), jnp.float32)]
+
+    rows = [
+        *two(0, 38, 4),
+        *two(38, 38, 4),
+        *two(76, 38, 4),
+        *two(114, 7, 2),
+        *two(121, 7, 2),
+        *two(128, 3, 10),
+    ]
+    block = half(jnp.concatenate(rows))
+    return jnp.where(parity == 0, block[:ROWS], block[ROWS:])
+
+
+def unpack_rest(rest):
+    rest = rest.reshape(2, 32, 48, D)
+    place = placement()
+    query = half(inner_rows(place, rest[:, :, 0:16].reshape(1024, D)))
+    out = half(inner_rows(place, rest[:, :, 16:32].reshape(1024, D)))
+    misc = rest[:, :, 32:38].reshape(2, 32, 2, 3, D)
+    narrow = misc[:, :, :, :2].reshape(2, 32, 14, 256)
+    narrow = jnp.pad(narrow, ((0, 0), (0, 0), (0, 2), (0, 0))).reshape(1024, 256)
+    narrow = half(inner_rows(place, narrow))
+    vectors = misc[:, :, :, 2, :23].transpose(1, 2, 0, 3).reshape(-1)
+    return query, out, narrow, vectors
+
+
+def pack_rest(query, out, narrow, vectors):
+    vectors = vectors.reshape(32, 2, 2, 1, 23).transpose(2, 0, 1, 3, 4)
+    vectors = jnp.pad(vectors, ((0, 0),) * 4 + ((0, D - 23),))
+    narrow = narrow.reshape(2, 32, 16, 256)[:, :, :14].reshape(2, 32, 2, 2, D)
+    misc = jnp.concatenate([narrow, vectors], axis=3).reshape(2, 32, 6, D)
+    misc = jnp.pad(misc, ((0, 0), (0, 0), (0, 10), (0, 0)))
+    rest = jnp.concatenate(
+        [half(query).reshape(2, 32, 16, D), half(out).reshape(2, 32, 16, D), half(misc)], axis=2
+    )
+    return rest.reshape(2, 4, 4, 2, 48, D)
+
+
 def slot_pass(full, tokens, cotangent, lengths):
     (
         query_weight,
-        key_weight,
-        value_weight,
         out_weight,
-        gate_rows,
-        up_rows,
-        down_weight,
+        narrow_weight,
+        mlp_weights,
         vectors,
     ) = full
     batch, rows = tokens.shape[0], tokens.shape[1]
     count = batch * rows
-    kv_width = key_weight.shape[1]
+    kv_width = KV_HEADS * HEAD
+    key_weight = narrow_weight[:, :kv_width]
+    value_weight = narrow_weight[:, kv_width:]
+    place = placement()
     group = HEADS // KV_HEADS
     gains = vectors.astype(jnp.float32)
     first_gain = gains[:D]
@@ -129,24 +628,14 @@
     second_scale = lax.rsqrt(jnp.mean(middle * middle, axis=-1, keepdims=True) + NORM_EPSILON)
     second_normed = middle * second_scale
     normed_two = (second_normed * second_gain).astype(jnp.bfloat16)
-    gate = outer_cols(normed_two, gate_rows)
-    up = outer_cols(normed_two, up_rows)
-    sigma = jax.nn.sigmoid(gate)
-    hidden = (gate * sigma * up).astype(jnp.bfloat16)
-    result = ((middle + product(hidden, down_weight)) * live).astype(jnp.bfloat16)
     back = cotangent.astype(jnp.float32).reshape(count, D) * live
     back_half = back.astype(jnp.bfloat16)
-    grad_down_w = inner_rows(hidden, back_half)
-    grad_hidden = outer_cols(back_half, down_weight)
-    grad_gate = (grad_hidden * up * sigma * (1.0 + gate * (1.0 - sigma))).astype(jnp.bfloat16)
-    grad_up = (grad_hidden * gate * sigma).astype(jnp.bfloat16)
-    grad_gate_w = inner_rows(grad_gate, normed_two)
-    grad_up_w = inner_rows(grad_up, normed_two)
-    grad_normed_two = product(grad_gate, gate_rows) + product(grad_up, up_rows)
+    fed, grad_normed_two, grad_mlp = mlp(normed_two, back_half, mlp_weights)
+    result = ((middle + fed) * live).astype(jnp.bfloat16)
     second_gain_grad = jnp.sum(grad_normed_two * second_normed, axis=0)
     grad_middle = back + norm_back(grad_normed_two * second_gain, second_normed, second_scale)
     branch_grad = grad_middle.astype(jnp.bfloat16)
-    grad_out_w = inner_rows(mixed, branch_grad)
+    grad_out_w = inner_rows(half(outer_cols(mixed, place)), branch_grad)
     grad_mixed = outer_cols(branch_grad, out_weight).astype(jnp.bfloat16)
     grad_mixed = grad_mixed.reshape(batch, rows, KV_HEADS, group, HEAD)
     grad_probs = jnp.einsum(
@@ -173,9 +662,9 @@
     query_bias_grad = jnp.sum(grad_query.astype(jnp.float32), axis=0)
     key_bias_grad = jnp.sum(grad_key.astype(jnp.float32), axis=0)
     value_bias_grad = jnp.sum(grad_value.astype(jnp.float32), axis=0)
-    grad_query_w = inner_rows(normed, grad_query)
-    grad_key_w = inner_rows(normed, grad_key)
-    grad_value_w = inner_rows(normed, grad_value)
+    placed = half(outer_cols(normed, place))
+    grad_query_w = inner_rows(placed, grad_query)
+    grad_narrow_w = inner_rows(placed, jnp.concatenate([grad_key, grad_value], axis=1))
     grad_normed = (
         outer_cols(grad_query, query_weight)
         + outer_cols(grad_key, key_weight)
@@ -188,16 +677,7 @@
     vector_grad = jnp.concatenate(
         [first_gain_grad, second_gain_grad, query_bias_grad, key_bias_grad, value_bias_grad]
     )
-    grads = (
-        grad_query_w,
-        grad_key_w,
-        grad_value_w,
-        grad_out_w,
-        grad_gate_w,
-        grad_up_w,
-        grad_down_w,
-        vector_grad,
-    )
+    grads = (grad_mlp, pack_rest(grad_query_w, grad_out_w, grad_narrow_w, vector_grad))
     return (
         result.reshape(batch, 1, rows, D),
         grad_inputs.reshape(batch, 1, rows, D),
@@ -246,60 +726,43 @@
     second_prior,
 ):
     axes = ("dp", "narrow")
-    count = lax.axis_size("dp") * lax.axis_size("narrow")
-    index = lax.axis_index("dp") * lax.axis_size("narrow") + lax.axis_index("narrow")
-    rows = query_weight.shape[0]
-    units = down_weight.shape[0]
+    chip = lax.axis_index("dp")
+    core = lax.axis_index("narrow")
+    parity = chip % 2
     kv_width = key_weight.shape[1]
-    packed = half(
-        jnp.concatenate([query_weight, out_weight, gate_weight.T, up_weight.T, down_weight])
-    )
-    narrow = half(jnp.concatenate([key_weight, value_weight], axis=1))
-    gathered = lax.all_gather(packed, axes, axis=0)
-    gathered_narrow = lax.all_gather(narrow, axes, axis=0)
-    gathered_vectors = lax.all_gather(half(vectors), axes, axis=0)
-    cuts = (0, rows, 2 * rows, 2 * rows + units, 2 * rows + 2 * units, 2 * rows + 3 * units)
-    pieces = [
-        gathered[:, cuts[k] : cuts[k + 1]].reshape(count * (cuts[k + 1] - cuts[k]), D)
-        for k in range(5)
-    ]
-    full = (
-        pieces[0],
-        gathered_narrow[:, :, :kv_width].reshape(D, kv_width),
-        gathered_narrow[:, :, kv_width:].reshape(D, kv_width),
-        pieces[1],
-        pieces[2],
-        pieces[3],
-        pieces[4],
-        gathered_vectors.reshape(-1),
-    )
-    own_lengths = lax.dynamic_slice_in_dim(lengths, index, 1, axis=1)[:, 0]
+    own = pack_pair(
+        (
+            jnp.concatenate([gate_weight.T, up_weight.T, down_weight, query_weight, out_weight]),
+            jnp.concatenate([key_weight, value_weight], axis=1),
+            vectors,
+        ),
+        parity,
+    )
+    gathered, rest = gather_blocks(own)
+    query, out, narrow, gathered_vectors = unpack_rest(rest)
+    full = (query, out, narrow, gathered.reshape(32, 2 * ROWS, D), gathered_vectors)
+    own_lengths = lax.dynamic_slice_in_dim(lengths, chip * 2 + core, 1, axis=1)[:, 0]
     block_output, input_grad, grads = slot_pass(full, inputs[:, 0], cotangent[:, 0], own_lengths)
-    wide = jnp.concatenate(
-        [
-            half(grads[k]).reshape(count, -1, D)
-            for k in (0, 3, 4, 5, 6)
-        ],
-        axis=1,
-    )
-    thin = jnp.concatenate(
-        [
-            half(grads[1]).reshape(count, rows, kv_width),
-            half(grads[2]).reshape(count, rows, kv_width),
-        ],
-        axis=2,
-    )
-    own_wide = lax.psum_scatter(wide, axes, scatter_dimension=0).astype(jnp.float32)
-    own_thin = lax.psum_scatter(thin, axes, scatter_dimension=0).astype(jnp.float32)
-    grad_vector = lax.psum_scatter(grads[7], axes, scatter_dimension=0, tiled=True)
+    reduced = scatter_blocks(grads[0].reshape(4, 4, 2, 3 * UNITS, D), grads[1])
+    partner = swap_pair(reduced)
+    both = jnp.where(
+        parity == 0, jnp.concatenate([reduced, partner]), jnp.concatenate([partner, reduced])
+    ).astype(jnp.float32)
+
+    def mine(start, size):
+        return lax.dynamic_slice_in_dim(both, start + parity * size, size, axis=0)
+
+    tail = mine(272, 3)
+    own_narrow = tail[:2].reshape(7, 2 * kv_width)
+    grad_vector = tail[2, :23]
     owned = (
-        own_wide[cuts[0] : cuts[1]],
-        own_thin[:, :kv_width],
-        own_thin[:, kv_width:],
-        own_wide[cuts[1] : cuts[2]],
-        own_wide[cuts[2] : cuts[3]],
-        own_wide[cuts[3] : cuts[4]],
-        own_wide[cuts[4] : cuts[5]],
+        mine(240, 7),
+        own_narrow[:, :kv_width],
+        own_narrow[:, kv_width:],
+        mine(256, 7),
+        mine(0, 38),
+        mine(80, 38),
+        mine(160, 38),
     )
     priors = (
         query_prior,

time: 1940 us -> 723 us (0.37)
  waiting for transfers between devices: 1090 us -> 164 us
  local copies, waits for them, and re-layouts: 368 us -> 29 us
  Pallas kernels: 0 us -> 281 us
  blocking collectives: 174 us -> 0 us
  matrix products: 220 us -> 166 us
    reduce_scatter x2 -> x0, waiting for transfers between devices: 1020 us -> none  [the longest x1 682 us: body(): lax.psum_scatter(wide, axes, scatter_dimension=0).astype(jnp.float32)]
    pallas_call x0 -> x3, Pallas kernels: none -> 281 us  [the longest x1 160 us: gather_blocks(): pl.pallas_call(gather_kernel, out_shape=(jax.ShapeDtypeStruct((4, 4, 2, 2...]
    concatenate x2 -> x4, local copies, waits for them, and re-layouts: 233 us -> 2.66 us  [the longest x2 1.94 us: pack_pair(): block = half(jnp.concatenate(rows))]
    unnamed x2 -> x0, blocking collectives: 135 us -> none
    psum x1, waiting for transfers between devices: 70.7 us -> 159 us  [body(): lax.psum(jnp.stack([partial[k] for k in (0, 3, 4, 5, 6)]), axes)]
    reshape x14 -> x6, local copies, waits for them, and re-layouts: 87.2 us -> 2.7 us  [the longest x1 2.09 us: pack_rest(): narrow = narrow.reshape(2, 32, 16, 256)[:, :, :14].reshape(2, 32, 2, 2, D)]
    all_gather x1 -> x0, blocking collectives: 39.8 us -> none  [body(): gathered_narrow = lax.all_gather(narrow, axes, axis=0)]
    dot_general x7 -> x5, matrix products: 35.1 us -> 7.19 us  [outer_cols(): lax.dot_general(left, right, (((1,), (1,)), ((), ())), preferred_element_...]
  transfers between devices with their start and end apart: 4 -> 3, of which waited for: 3 -> 2; matrix products, arithmetic and copies ran while one was open for 17% -> 1% of each run, Pallas kernels for 0% -> 0%
where the time goes in v2:
time: 723 us; the launch traced here: 719 us
  Pallas kernels  281 us (39%)
  matrix products  166 us (23%)
  waiting for transfers between devices  164 us (23%)
  other arithmetic  56 us (8%)
  local copies, waits for them, and re-layouts  29 us (4%)
  between operations  20.8 us (3%)
    pallas_call x1, Pallas kernels, gather_blocks(): pl.pallas_call(gather_kernel, out_shape=(jax.ShapeDtypeStruct((4, 4, 2, 2...  160 us
    psum x1, waiting for transfers between devices, body(): lax.psum(jnp.stack([partial[k] for k in (0, 3, 4, 5, 6)]), axes)  159 us
    dot_general x39, matrix products, product(): return jnp.dot(left, right, preferred_element_type=jnp.float32)  128 us
    pallas_call x1, Pallas kernels, scatter_blocks(): pl.pallas_call(scatter_kernel, out_shape=jax.ShapeDtypeStruct((ROWS, D),...  78.2 us
    pallas_call x1, Pallas kernels, mlp(): pl.pallas_call(mlp_kernel, grid=(TILES,), out_shape=(jax.ShapeDtypeStruct...  42.9 us
    dot_general x13, matrix products, inner_rows(): lax.dot_general(left, right, (((0,), (0,)), ((), ())), preferred_element_...  24.1 us
  transfers between devices with their start and end apart: 3, of which 2 were waited for; matrix products, arithmetic and copies ran while one was open for 1% of the time, Pallas kernels for 0%

profile of v2, /device:TPU:1, one launch (start us, length us, event | category | flops | bytes accessed | tf_op | source)
XLA Modules:
  0.0 718.9 jit_solution(11210288774316060663)
XLA Ops:
  13.4 2.1 collective-permute-start
  17.3 1.9 fusion.186.e_ref
  19.2 4.1 convert_convert_fusion.20
  24.9 1.4 concatenate.83
  27.1 159.7 %shard_map.339 = (bf16[4,4,2,2,144,896]{5,4,3,2,1,0:T(8,128)(2,1)}, bf16[2,4,4,2,48,896]{5,4,3,2,1,0:T(8,128)(2,1)}) custom-call(bf16[144,896]{1,0:T(8,128)(2,1)} %slice_select_fusion.block_ref), custom_call_target="tpu_custom_call" | custom-call | tf_op jit(solution)/shard_map/pallas_call | solution.py:217
  186.8 1.3 slice.213
  189.7 3.6 fusion.311
  193.3 2.8 fusion.41
  199.5 1.4 copy.58
  201.3 2.1 fusion.97
  205.7 1.4 fusion.142
  208.9 1.4 fusion.183
  210.3 1.8 fusion.320
  212.1 1.2 copy-done.5
  214.9 2.8 fusion.42
  219.5 42.9 %shard_map.340 = (f32[256,896]{1,0:T(8,128)}, f32[256,896]{1,0:T(8,128)}, bf16[32,240,896]{2,1,0:T(8,128)(2,1)}) custom-call(bf16[256,896]{1,0:T(8,128)(2,1)} %multiply_convert_fusion.6.h_ref, bf16[256,896]{1,0:T(8,128)(2,1)} %fusion.186.e_ref, bf16[32,288,896]{2,1,0:T(8,128)(2,1)} %bitcast.353, bf16[32,288,896]{2,1,0:T(8,128)(2,1)} %bitcast.354, ...), custom_call_target="tpu_custom_call" | custom-call | tf_op jit(solution)/shard_map/pallas_call | solution.py:486
  262.4 2.1 multiply_reduce_fusion
  264.6 2.7 fusion.185
  268.0 4.9 convolution_convert_fusion
  274.5 2.1 fusion.37
  277.7 1.2 broadcast_multiply_fusion
  284.3 1.7 fusion.326
  288.7 2.1 reshape.339
  290.8 1.7 fusion.196
  292.6 1.6 convolution_add_fusion.1
  294.3 2.4 multiply_reduce_fusion.1
  298.5 1.6 fusion.180
  301.6 4.8 pad_maximum_fusion.rest_ref
  306.4 78.2 %shard_map.341 = bf16[144,896]{1,0:T(8,128)(2,1)} custom-call(bf16[4,4,2,240,896]{4,3,2,1,0:T(8,128)(2,1)} %bitcast.356, bf16[2,4,4,2,48,896]{5,4,3,2,1,0:T(8,128)(2,1)} %pad_maximum_fusion.rest_ref), custom_call_target="tpu_custom_call" | custom-call | tf_op jit(solution)/shard_map/pallas_call | solution.py:399
  385.0 5.1 collective-permute-done.1
  391.9 1.8 bitcast_dynamic-update-slice_fusion.4
  394.4 1.8 bitcast_dynamic-update-slice_fusion.3
  396.3 1.8 bitcast_dynamic-update-slice_fusion.2
  398.1 1.8 bitcast_dynamic-update-slice_fusion.1
  399.9 1.9 bitcast_dynamic-update-slice_fusion
  404.0 1.2 divide_subtract_fusion
  405.2 158.9 %all-reduce.7.cloned.1.call-done = (bf16[5,896,896]{2,1,0:T(8,128)(2,1)}, bf16[2,128,128]{2,1,0:T(8,128)(2,1)}) async-done(((bf16[5,896,896]{2,1,0:T(8,128)(2,1)}, bf16[2,128,128]{2,1,0:T(8,128)(2,1)}), (bf16[5,896,896]{2,1,0:T(8,128)(2,1)}, bf16[2,128,128]{2,1,0:T(8,128)(2,1)})) %all-reduce.7.cloned.1.call-update) | async-done | bytes 8093712 | tf_op jit(solution)/shard_map/psum | solution.py:789
  564.1 9.9 %convert_element_type.495 = f32[5,896,896]{2,1,0:T(8,128)} convert(bf16[5,896,896]{2,1,0:T(8,128)(2,1)} %get-tuple-element.78) | non-fusion elementwise | flops 4014080 | bytes 24084480 | tf_op jit(solution)/shard_map/convert_element_type | solution.py:789
  574.1 7.1 fusion.22
  581.9 5.9 add_convert_fusion.1
  587.8 3.9 fusion.44
  591.7 4.1 add_add_fusion
  595.8 3.7 multiply_add_fusion
  599.5 5.9 fusion.114
  606.1 6.2 add_convert_fusion.3
  612.3 4.1 fusion.46
  616.4 4.1 add_add_fusion.1
  620.5 3.7 multiply_add_fusion.1
  624.3 6.0 fusion.126
  631.0 6.0 add_convert_fusion.5
  637.0 3.9 fusion.48
  640.9 4.1 add_add_fusion.2
  645.1 4.1 multiply_add_fusion.2
  649.2 6.0 fusion.138
  656.0 6.0 add_convert_fusion.7
  662.0 4.5 fusion.50
  666.5 4.1 add_add_fusion.3
  670.6 3.7 multiply_add_fusion.3
  674.3 6.7 fusion.162
  686.8 6.1 add_convert_fusion.9
  692.9 4.5 fusion.52
  697.4 4.1 add_add_fusion.4
  701.5 3.7 multiply_add_fusion.4
  705.2 6.7 fusion.171
  (273 shorter events, 45.8 us)
Async XLA Ops:
  7.2 9.9 %copy-start = (s32[2,128]{1,0:T(2,128)S(1)}, s32[2,128]{1,0:T(2,128)}, u32[]{:S(2)}) copy-start(s32[2,128]{1,0:T(2,128)} %param.22) | copy-start | bytes 3076
  7.2 556.9 %all-reduce.7.cloned.1.call-start = ((), (), s32[]{:S(2)}) async-start(), calls=%async_computation | async-start | bytes 16187392 | tf_op jit(solution)/shard_map/psum | solution.py:789
  13.4 10.7 %collective-permute-start = (bf16[131,896]{1,0:T(8,128)(2,1)S(1)}, bf16[131,896]{1,0:T(8,128)(2,1)S(1)}, u32[]{:S(2)}, u32[]{:S(2)}) collective-permute-start(bf16[131,896]{1,0:T(8,128)(2,1)S(1)} %concatenate.81), channel_id=1, source_target_pairs={{0,2},{2,0},{4,6},{6,4},{8,10},{10,8},{12,14},{14,12},{16,18},{18,... | collective-permute-start | bytes 704264 | tf_op jit(solution)/shard_map/ppermute | solution.py:526
  15.5 185.7 %copy-start.38 = (s32[1024]{0:T(1024)}, s32[1024]{0:T(1024)S(1)}, u32[]{:S(2)}) copy-start(s32[1024]{0:T(1024)S(1)} %get-tuple-element.143) | copy-start | bytes 12292
  15.5 177.8 %copy-start.40 = (s32[1024]{0:T(1024)}, s32[1024]{0:T(1024)S(1)}, u32[]{:S(2)}) copy-start(s32[1024]{0:T(1024)S(1)} %get-tuple-element.144) | copy-start | bytes 12292
  15.5 177.7 %copy-start.43 = (s32[1024]{0:T(1024)}, s32[1024]{0:T(1024)S(1)}, u32[]{:S(2)}) copy-start(s32[1024]{0:T(1024)S(1)} %get-tuple-element.145) | copy-start | bytes 12292
  15.6 177.7 %copy-start.46 = (s32[1024]{0:T(1024)}, s32[1024]{0:T(1024)S(1)}, u32[]{:S(2)}) copy-start(s32[1024]{0:T(1024)S(1)} %get-tuple-element.148) | copy-start | bytes 12292
  15.6 177.7 %copy-start.49 = (s32[1024]{0:T(1024)}, s32[1024]{0:T(1024)S(1)}, u32[]{:S(2)}) copy-start(s32[1024]{0:T(1024)S(1)} %get-tuple-element.149) | copy-start | bytes 12292
  15.6 177.7 %copy-start.58 = (pred[1024]{0:T(1024)(128)(4,1)}, pred[1024]{0:T(1024)(128)(4,1)S(1)}, u32[]{:S(2)}) copy-start(pred[1024]{0:T(1024)(128)(4,1)S(1)} %get-tuple-element.146) | copy-start | bytes 3076
  15.6 177.7 %copy-start.61 = (pred[1024]{0:T(1024)(128)(4,1)}, pred[1024]{0:T(1024)(128)(4,1)S(1)}, u32[]{:S(2)}) copy-start(pred[1024]{0:T(1024)(128)(4,1)S(1)} %get-tuple-element.147) | copy-start | bytes 3076
  15.6 177.7 %copy-start.66 = (pred[1024]{0:T(1024)(128)(4,1)}, pred[1024]{0:T(1024)(128)(4,1)S(1)}, u32[]{:S(2)}) copy-start(pred[1024]{0:T(1024)(128)(4,1)S(1)} %fusion.283) | copy-start | bytes 3076
  17.3 7.5 %copy-start.54 = (f32[256]{0:T(256)}, f32[256]{0:T(256)S(1)}, u32[]{:S(2)}) copy-start(f32[256]{0:T(256)S(1)} %get-tuple-element.125) | copy-start | bytes 3076
  193.3 2.8 copy-start.2
  198.4 2.8 copy-start.41
  198.5 2.8 copy-start.44
  198.5 2.8 copy-start.47
  198.5 2.8 copy-start.50
  198.5 2.8 copy-start.59
  198.5 2.8 copy-start.62
  198.5 2.8 copy-start.67
  201.3 2.9 copy-start.10
  208.9 4.5 copy-start.30
  213.3 1.5 copy-start.4
  213.3 1.5 copy-start.39
  213.3 1.5 copy-start.42
  213.3 1.5 copy-start.45
  219.5 45.1 %copy-start.12 = (bf16[2,1,128,896]{3,2,1,0:T(8,128)(2,1)S(1)}, bf16[2,1,128,896]{3,2,1,0:T(8,128)(2,1)}, u32[]{:S(2)}) copy-start(bf16[2,1,128,896]{3,2,1,0:T(8,128)(2,1)} %param.21) | copy-start | bytes 1376260
  219.5 45.1 %copy-start.55 = (f32[256]{0:T(256)S(1)}, f32[256]{0:T(256)}, u32[]{:S(2)}) copy-start(f32[256]{0:T(256)} %copy-done.54) | copy-start | bytes 3076
  274.5 2.1 copy-start.6
  280.4 2.5 copy-start.8
  280.4 2.5 copy-start.11
  284.3 2.6 copy-start.7
  290.8 6.0 copy-start.57
  290.8 6.1 copy-start.56
  300.1 1.5 copy-start.13
  306.4 85.0 %copy-start.64 = (f32[7,128]{1,0:T(8,128)S(1)}, f32[7,128]{1,0:T(8,128)}, u32[]{:S(2)}) copy-start(f32[7,128]{1,0:T(8,128)} %param.33) | copy-start | bytes 10756
  306.4 85.0 %copy-start.65 = (f32[7,128]{1,0:T(8,128)S(1)}, f32[7,128]{1,0:T(8,128)}, u32[]{:S(2)}) copy-start(f32[7,128]{1,0:T(8,128)} %param.32) | copy-start | bytes 10756
  306.4 85.5 %copy-start.35 = (f32[7,896]{1,0:T(8,128)S(1)}, f32[7,896]{1,0:T(8,128)}, u32[]{:S(2)}) copy-start(f32[7,896]{1,0:T(8,128)} %param.34) | copy-start | bytes 75268
  306.4 85.5 %copy-start.36 = (f32[7,896]{1,0:T(8,128)S(1)}, f32[7,896]{1,0:T(8,128)}, u32[]{:S(2)}) copy-start(f32[7,896]{1,0:T(8,128)} %param.31) | copy-start | bytes 75268
  384.6 11.5 %copy-start.25 = (f32[38,896]{1,0:T(8,128)S(1)}, f32[38,896]{1,0:T(8,128)}, u32[]{:S(2)}) copy-start(f32[38,896]{1,0:T(8,128)} %param.37) | copy-start | bytes 408580
  384.6 11.5 %copy-start.26 = (f32[896,38]{0,1:T(8,128)S(1)}, f32[896,38]{0,1:T(8,128)}, u32[]{:S(2)}) copy-start(f32[896,38]{0,1:T(8,128)} %param.36) | copy-start | bytes 408580
  384.7 11.5 %copy-start.27 = (f32[896,38]{0,1:T(8,128)S(1)}, f32[896,38]{0,1:T(8,128)}, u32[]{:S(2)}) copy-start(f32[896,38]{0,1:T(8,128)} %param.35) | copy-start | bytes 408580
  384.7 5.5 collective-permute-start.1
  391.4 291.6 %copy-start.31 = (f32[7,128]{1,0:T(8,128)}, f32[7,128]{1,0:T(8,128)S(1)}, u32[]{:S(2)}) copy-start(f32[7,128]{1,0:T(8,128)S(1)} %get-tuple-element.123) | copy-start | bytes 10756
  391.4 293.8 %copy-start.32 = (f32[7,128]{1,0:T(8,128)}, f32[7,128]{1,0:T(8,128)S(1)}, u32[]{:S(2)}) copy-start(f32[7,128]{1,0:T(8,128)S(1)} %get-tuple-element.124) | copy-start | bytes 10756
  391.9 282.4 %copy-start.28 = (f32[7,896]{1,0:T(8,128)}, f32[7,896]{1,0:T(8,128)S(1)}, u32[]{:S(2)}) copy-start(f32[7,896]{1,0:T(8,128)S(1)} %get-tuple-element.90) | copy-start | bytes 75268
  391.9 313.3 %copy-start.37 = (f32[7,896]{1,0:T(8,128)}, f32[7,896]{1,0:T(8,128)S(1)}, u32[]{:S(2)}) copy-start(f32[7,896]{1,0:T(8,128)S(1)} %get-tuple-element.91) | copy-start | bytes 75268
  396.3 5.5 copy-start.18
  396.3 5.5 copy-start.20
  396.3 203.2 %copy-start.17 = (f32[38,896]{1,0:T(8,128)}, f32[38,896]{1,0:T(8,128)S(1)}, u32[]{:S(2)}) copy-start(f32[38,896]{1,0:T(8,128)S(1)} %get-tuple-element.87) | copy-start | bytes 408580
  401.8 2.2 copy-start.69
  595.7 3.7 copy-start.22
  620.5 3.7 copy-start.19
  620.5 3.7 copy-start.23
  645.0 4.2 copy-start.21
  645.0 4.1 copy-start.24
  662.0 4.5 copy-start.71
  670.6 3.7 copy-start.33
  674.3 6.8 copy-start.29
  674.3 8.7 %copy-start.52 = (f32[7,128]{1,0:T(8,128)S(1)}, f32[7,128]{1,0:T(8,128)}, u32[]{:S(2)}) copy-start(f32[7,128]{1,0:T(8,128)} %param.25) | copy-start | bytes 10756
  674.3 10.9 %copy-start.53 = (f32[7,128]{1,0:T(8,128)S(1)}, f32[7,128]{1,0:T(8,128)}, u32[]{:S(2)}) copy-start(f32[7,128]{1,0:T(8,128)} %param.24) | copy-start | bytes 10756
  692.9 4.5 copy-start.70
  701.5 3.7 copy-start.34
  701.5 10.4 %copy-start.1 = (s32[2,128]{1,0:T(2,128)S(1)}, s32[2,128]{1,0:T(2,128)}, u32[]{:S(2)}) copy-start(s32[2,128]{1,0:T(2,128)} %param.22) | copy-start | bytes 3076
  (11 other events, 14.3 us)
Sparse Core Ops, SparseCore 0:
  401.9 162.1 all-reduce.6

commit v3 on v2

--- a/solution.py
+++ b/solution.py
@@ -137,21 +137,22 @@
     return out
 
 
-def gather_kernel(block_ref, out_ref, rest_ref, local_sem, send_sems, recv_sems, rest_sems):
+def gather_kernel(
+    block_ref, out_ref, rest_ref, held, local_sem, send_sems, recv_sems, rest_sems, store_sems
+):
     coords, core = my_coords()
-    own = (coords[0], coords[1], coords[2])
     local = pltpu.make_async_copy(
-        block_ref, out_ref.at[coords[0], coords[1], coords[2] // 2, coords[2] % 2], local_sem
+        block_ref, held.at[coords[0], coords[1], coords[2] // 2, coords[2] % 2], local_sem
     )
     local.start()
     ring_barrier(coords, core)
     local.wait()
     sends = []
-
-    def send(part, phase, slot, piece, axis, by):
-        spec, rows = piece
-        ref = out_ref.at[region(spec, part, rows)]
-        copy = pltpu.make_async_remote_copy(
+    stores = []
+
+    def copy_of(part, phase, slot, piece, axis, by):
+        ref = held.at[region(piece[0], part, piece[1])]
+        return pltpu.make_async_remote_copy(
             src_ref=ref,
             dst_ref=ref,
             send_sem=send_sems.at[part, phase, slot],
@@ -159,56 +160,63 @@
             device_id=device_of(shifted(coords, axis, by), core),
             device_id_type=MESH,
         )
+
+    def send(*args):
+        copy = copy_of(*args)
         copy.start()
         sends.append(copy)
 
-    def wait(part, phase, slot, piece):
-        spec, rows = piece
-        ref = out_ref.at[region(spec, part, rows)]
-        pltpu.make_async_remote_copy(
-            src_ref=ref,
-            dst_ref=ref,
-            send_sem=send_sems.at[part, phase, slot],
-            recv_sem=recv_sems.at[part, phase, slot],
-            device_id=device_of(shifted(coords, 0, 1), core),
-            device_id_type=MESH,
-        ).wait_recv()
+    def store(part, slot, piece):
+        place = region(piece[0], part, piece[1])
+        copy = pltpu.make_async_copy(held.at[place], out_ref.at[place], store_sems.at[part, slot])
+        copy.start()
+        stores.append(copy)
 
     for phase in range(3):
-        specs = []
+        plans = []
         for part, order in enumerate(GATHER_ORDERS):
             axis = order[phase]
             split = order[phase - 1] if phase else None
 
-            def spec_at(by, order=order, axis=axis):
+            def pieces_at(by, order=order, axis=axis, split=split):
                 spec = [FULL if order.index(k) < phase else coords[k] for k in range(3)]
                 spec[axis] = (coords[axis] + by) % 4
-                return tuple(spec)
-
-            specs.append((axis, spec_at, split))
-        for part, (axis, spec_at, split) in enumerate(specs):
-            h0, h1 = halves(spec_at(0), split)
+                return halves(tuple(spec), split)
+
+            plans.append((axis, pieces_at))
+        for part, (axis, pieces_at) in enumerate(plans):
+            h0, h1 = pieces_at(0)
             send(part, phase, 0, h0, axis, 1)
             send(part, phase, 1, h1, axis, 3)
             send(part, phase, 2, h1, axis, 1)
             send(part, phase, 3, h0, axis, 3)
-        for part, (axis, spec_at, split) in enumerate(specs):
-            wait(part, phase, 0, halves(spec_at(3), split)[0])
-            send(part, phase, 4, halves(spec_at(3), split)[0], axis, 1)
-            wait(part, phase, 1, halves(spec_at(1), split)[1])
-            send(part, phase, 5, halves(spec_at(1), split)[1], axis, 3)
-        for part, (axis, spec_at, split) in enumerate(specs):
-            wait(part, phase, 2, halves(spec_at(3), split)[1])
-            wait(part, phase, 3, halves(spec_at(1), split)[0])
-            wait(part, phase, 4, halves(spec_at(2), split)[0])
-            wait(part, phase, 5, halves(spec_at(2), split)[1])
-    last = out_ref.at[:, :, :, 1, pl.ds(96, 48)]
+            if phase == 2:
+                store(part, 0, h0)
+                store(part, 1, h1)
+        for part, (axis, pieces_at) in enumerate(plans):
+            first, second = pieces_at(3)[0], pieces_at(1)[1]
+            copy_of(part, phase, 0, first, axis, 1).wait_recv()
+            send(part, phase, 4, first, axis, 1)
+            copy_of(part, phase, 1, second, axis, 3).wait_recv()
+            send(part, phase, 5, second, axis, 3)
+            if phase == 2:
+                store(part, 2, first)
+                store(part, 3, second)
+        for part, (axis, pieces_at) in enumerate(plans):
+            last = (pieces_at(3)[1], pieces_at(1)[0], pieces_at(2)[0], pieces_at(2)[1])
+            for slot, piece in enumerate(last):
+                copy_of(part, phase, 2 + slot, piece, axis, 1 if slot % 2 == 0 else 3).wait_recv()
+                if phase == 2:
+                    store(part, 4 + slot, piece)
+    last = held.at[:, :, :, 1, pl.ds(96, 48)]
     keep = pltpu.make_async_copy(last, rest_ref.at[core], local_sem)
     give = sibling_copy(last, rest_ref.at[core], rest_sems, 0, core)
     keep.start()
     give.start()
     keep.wait()
     give.wait()
+    for copy in stores:
+        copy.wait()
     for copy in sends:
         copy.wait_send()
 
@@ -223,12 +231,16 @@
         in_specs=[pl.BlockSpec(memory_space=pl.ANY)],
         out_specs=(pl.BlockSpec(memory_space=pl.ANY),) * 2,
         scratch_shapes=[
+            pltpu.VMEM((4, 4, 2, 2, ROWS, D), jnp.bfloat16),
             pltpu.SemaphoreType.DMA,
             pltpu.SemaphoreType.DMA((3, 3, 6)),
             pltpu.SemaphoreType.DMA((3, 3, 6)),
             pltpu.SemaphoreType.DMA((2, 1)),
+            pltpu.SemaphoreType.DMA((3, 8)),
         ],
-        compiler_params=pltpu.CompilerParams(collective_id=0, has_side_effects=True),
+        compiler_params=pltpu.CompilerParams(
+            collective_id=0, has_side_effects=True, vmem_limit_bytes=40 * 2**20
+        ),
     )(block)
 
 
@@ -701,6 +713,246 @@
     return half(
         NEWTON_A * (first.astype(jnp.float32) + second) + product(first, half(second))
     )
+
+
+BLOCKS = [(i, j) for i in range(7) for j in range(i, 7)]
+
+
+def muon_kernel(
+    sent_ref, big_ref, square_ref, narrow_ref,
+    rows, job, gram_out, gram_in, gram_all, gram, back, narrow_back, big_got, square_got, narrow_got,
+    job_sems, sum_sems, all_sems, back_send, back_recv,
+):
+    coords, core = my_coords()
+    z, y, x = coords
+    me = y * 4 + x
+
+    def plane(peer):
+        return device_of((z, peer // 4, peer % 4), core)
+
+    def line(other, other_core):
+        return device_of((other, y, x), other_core)
+
+    barrier = pltpu.get_barrier_semaphore()
+    for k in range(1, 8):
+        t = (z * 2 + core + k) % 8
+        pl.semaphore_signal(barrier, inc=1, device_id=line(t // 2, t % 2), device_id_type=MESH)
+    for k in range(1, 16):
+        pl.semaphore_signal(barrier, inc=1, device_id=plane((me + k) % 16), device_id_type=MESH)
+    pl.semaphore_wait(barrier, 22)
+
+    def returned(src, dst, send_slot, slot, device):
+        return pltpu.make_async_remote_copy(
+            src_ref=src,
+            dst_ref=dst,
+            send_sem=back_send.at[send_slot],
+            recv_sem=back_recv.at[slot],
+            device_id=device,
+            device_id_type=MESH,
+        )
+
+    def remote(src, dst, sems, slot, device):
+        return pltpu.make_async_remote_copy(
+            src_ref=src,
+            dst_ref=dst,
+            send_sem=sems.at[0, slot],
+            recv_sem=sems.at[1, slot],
+            device_id=device,
+            device_id_type=MESH,
+        )
+
+    own = z * 2 + core
+
+    def job_copy(k):
+        t = (own + k) % 8
+        return remote(sent_ref.at[t // 2], rows.at[own], job_sems, k, line(t // 2, t % 2))
+
+    def job_arrival(k):
+        t = (own + 8 - k) % 8
+        return remote(sent_ref.at[0], rows.at[t], job_sems, k, line(t // 2, t % 2))
+
+    for k in range(1, 8):
+        job_copy(k).start()
+    rows[own] = sent_ref[z]
+    for k in range(1, 8):
+        job_arrival(k).wait_recv()
+
+    @pl.when(z < 3)
+    def _():
+        job[...] = rows[...]
+
+    for job_core in range(2):
+
+        @pl.when((z == 3) & (core == job_core))
+        def _():
+            job[:, 0:16] = rows[:, 16 * job_core : 16 * job_core + 16]
+            job[:, 16:48] = jnp.zeros((8, 32, D), jnp.bfloat16)
+
+    flat = job[...].reshape(384, D)
+    narrow = rows[:, 32:48, 0:256].reshape(128, 256)
+    gram[...] = inner_rows(flat, flat)
+    for index, (i, j) in enumerate(BLOCKS):
+        gram_out[index // 2, index % 2] = half(
+            gram[128 * i : 128 * i + 128, 128 * j : 128 * j + 128]
+        )
+    for t in range(2):
+        part = narrow[:, 128 * t : 128 * t + 128]
+        gram_out[14, t] = half(inner_rows(part, part))
+        gram_out[15, t] = jnp.zeros((128, 128), jnp.bfloat16)
+
+    def sum_copy(k):
+        peer = (me + k) % 16
+        return remote(gram_out.at[peer], gram_in.at[me], sum_sems, k, plane(peer))
+
+    def sum_arrival(k):
+        peer = (me + 16 - k) % 16
+        return remote(gram_out.at[0], gram_in.at[peer], sum_sems, k, plane(peer))
+
+    for k in range(1, 16):
+        sum_copy(k).start()
+    gram_in[me] = gram_out[me]
+    for k in range(1, 16):
+        sum_arrival(k).wait_recv()
+    for t in range(2):
+        value = gram_in[0, t].astype(jnp.float32)
+        for s in range(1, 16):
+            value = value + gram_in[s, t].astype(jnp.float32)
+        gram_all[me, t] = half(value)
+
+    def all_copy(k, peer):
+        return remote(gram_all.at[peer], gram_all.at[peer], all_sems, k, plane((me + k) % 16))
+
+    for k in range(1, 16):
+        all_copy(k, me).start()
+    for k in range(1, 16):
+        all_copy(k, (me + 16 - k) % 16).wait_recv()
+
+    eye = lax.broadcasted_iota(jnp.int32, (128, 128), 0) == lax.broadcasted_iota(
+        jnp.int32, (128, 128), 1
+    )
+
+    def diagonal(block):
+        return jnp.sum(jnp.where(eye, block, 0.0))
+
+    trace = 0.0
+    for index, (i, j) in enumerate(BLOCKS):
+        block = gram_all[index // 2, index % 2].astype(jnp.float32)
+        gram[128 * i : 128 * i + 128, 128 * j : 128 * j + 128] = block
+        if i == j:
+            trace = trace + diagonal(block)
+        else:
+            gram[128 * j : 128 * j + 128, 128 * i : 128 * i + 128] = block.T
+
+    def finish(total, matrix, values):
+        inverse = 1.0 / (jnp.sqrt(jnp.full((1, 1), total)) + 1e-07)
+        mixer = mixing(matrix * (inverse * inverse))
+        scaled = values.astype(jnp.float32) * inverse
+        return half(NEWTON_A * NEWTON_A * scaled + product(half(scaled), mixer))
+
+    back[...] = finish(trace, gram[...], flat).reshape(8, 48, D)
+    for t in range(2):
+        matrix = gram_all[14, t].astype(jnp.float32)
+        part = narrow[:, 128 * t : 128 * t + 128]
+        narrow_back[t] = finish(diagonal(matrix), matrix, part).reshape(8, 16, 128)
+
+    @pl.when(z < 3)
+    def _():
+        copies = []
+        for k in range(1, 4):
+            other = (z + k) % 4
+            copies.append(
+                returned(
+                    back.at[other * 2 + core], big_got.at[z], k, z, line(other, core)
+                )
+            )
+        for copy in copies:
+            copy.start()
+        big_got[z] = back[own]
+        for copy in copies:
+            copy.wait_send()
+
+    @pl.when(z == 3)
+    def _():
+        copies = []
+        for k in range(1, 8):
+            t = (own + k) % 8
+            device = line(t // 2, t % 2)
+            copies.append(
+                returned(back.at[t, pl.ds(0, 16)], square_got.at[core], k, 3 + core, device)
+            )
+            copies.append(
+                returned(narrow_back.at[core, t], narrow_got.at[core], 8 + k, 5 + core, device)
+            )
+        for copy in copies:
+            copy.start()
+        square_got[core] = back[own, 0:16]
+        narrow_got[core] = narrow_back[core, own]
+        for copy in copies:
+            copy.wait_send()
+
+    for plane_z in range(3):
+
+        @pl.when(z != plane_z)
+        def _():
+            returned(
+                back.at[0], big_got.at[plane_z], 0, plane_z, line(plane_z, core)
+            ).wait_recv()
+
+    for job_core in range(2):
+
+        @pl.when((z != 3) | (core != job_core))
+        def _():
+            device = line(3, job_core)
+            returned(
+                back.at[0, pl.ds(0, 16)], square_got.at[job_core], 0, 3 + job_core, device
+            ).wait_recv()
+            returned(
+                narrow_back.at[0, 0], narrow_got.at[job_core], 0, 5 + job_core, device
+            ).wait_recv()
+
+    for k in range(1, 8):
+        job_copy(k).wait_send()
+    for k in range(1, 16):
+        sum_copy(k).wait_send()
+        all_copy(k, me).wait_send()
+    big_ref[...] = big_got[...]
+    square_ref[...] = square_got[...]
+    narrow_ref[...] = narrow_got[...]
+
+
+def muon(sent):
+    vmem = pl.BlockSpec(memory_space=pltpu.VMEM)
+    return pl.pallas_call(
+        muon_kernel,
+        out_shape=(
+            jax.ShapeDtypeStruct((3, 48, D), jnp.bfloat16),
+            jax.ShapeDtypeStruct((2, 16, D), jnp.bfloat16),
+            jax.ShapeDtypeStruct((2, 16, 128), jnp.bfloat16),
+        ),
+        in_specs=[vmem],
+        out_specs=(vmem,) * 3,
+        scratch_shapes=[
+            pltpu.VMEM((8, 48, D), jnp.bfloat16),
+            pltpu.VMEM((8, 48, D), jnp.bfloat16),
+            pltpu.VMEM((16, 2, 128, 128), jnp.bfloat16),
+            pltpu.VMEM((16, 2, 128, 128), jnp.bfloat16),
+            pltpu.VMEM((16, 2, 128, 128), jnp.bfloat16),
+            pltpu.VMEM((D, D), jnp.float32),
+            pltpu.VMEM((8, 48, D), jnp.bfloat16),
+            pltpu.VMEM((2, 8, 16, 128), jnp.bfloat16),
+            pltpu.VMEM((3, 48, D), jnp.bfloat16),
+            pltpu.VMEM((2, 16, D), jnp.bfloat16),
+            pltpu.VMEM((2, 16, 128), jnp.bfloat16),
+            pltpu.SemaphoreType.DMA((2, 8)),
+            pltpu.SemaphoreType.DMA((2, 16)),
+            pltpu.SemaphoreType.DMA((2, 16)),
+            pltpu.SemaphoreType.DMA((16,)),
+            pltpu.SemaphoreType.DMA((7,)),
+        ],
+        compiler_params=pltpu.CompilerParams(
+            collective_id=3, has_side_effects=True, vmem_limit_bytes=58 * 2**20
+        ),
+    )(sent)
 
 
 def body(
@@ -785,19 +1037,23 @@
     shapes = ((D, D), (D, kv_width), (D, kv_width), (D, D), (D, FF), (D, FF), (FF, D))
     lefts = (False, False, False, False, True, True, False)
     momenta = tuple((MOMENTUM * priors[k] + owned[k] for k in range(7)))
-    partial = [half(inner_rows(half(moment), half(moment))) for moment in momenta]
-    big = lax.psum(jnp.stack([partial[k] for k in (0, 3, 4, 5, 6)]), axes).astype(jnp.float32)
-    small = lax.psum(jnp.stack([partial[k] for k in (1, 2)]), axes).astype(jnp.float32)
-    grams = (big[0], small[0], small[1], big[1], big[2], big[3], big[4])
+
+    def padded(value, count):
+        return jnp.pad(value, ((0, count - value.shape[0]), (0, D - value.shape[1])))
+
+    narrow_rows = jnp.concatenate([momenta[1], momenta[2]], axis=1)
+    last = jnp.concatenate(
+        [padded(momenta[0], 16), padded(momenta[3], 16), padded(narrow_rows, 16)]
+    )
+    sent = jnp.stack([padded(momenta[4], 48), padded(momenta[5], 48), padded(momenta[6], 48), last])
+    big, square, thin = muon(half(sent))
+    finals = (
+        square[0, :7], thin[0, :7], thin[1, :7], square[1, :7], big[0, :38], big[1, :38], big[2, :38],
+    )
     updated = []
     kept = []
     for k in range(7):
-        gram = grams[k]
-        norm = jnp.sqrt(jnp.trace(gram)) + 1e-07
-        inverse = 1.0 / norm
-        mixer = mixing(gram * inverse * inverse)
-        current = momenta[k] * inverse
-        current = NEWTON_A * NEWTON_A * current + product(half(current), mixer)
+        current = finals[k].astype(jnp.float32)
         factor = MUON_RATE * 0.2 * math.sqrt(max(shapes[k][0], shapes[k][1]))
         if lefts[k]:
             current = current.T

time: 723 us -> 377 us (0.52)
  waiting for transfers between devices: 164 us -> 3.72 us
  matrix products: 166 us -> 31.4 us
  Pallas kernels: 281 us -> 261 us
  between operations: 20.8 us -> 2.15 us
  other arithmetic: 56 us -> 45.1 us
    psum x1 -> x0, waiting for transfers between devices: 159 us -> none  [body(): lax.psum(jnp.stack([partial[k] for k in (0, 3, 4, 5, 6)]), axes)]
    dot_general x39 -> x4, matrix products: 128 us -> 3.19 us  [product(): return jnp.dot(left, right, preferred_element_type=jnp.float32)]
    pallas_call x1, Pallas kernels: 160 us -> 77.4 us  [gather_blocks(): pl.pallas_call(gather_kernel, out_shape=(jax.ShapeDtypeStruct((4, 4, 2, 2...]
    pallas_call x0 -> x1, Pallas kernels: none -> 67.2 us  [muon(): pl.pallas_call(muon_kernel, out_shape=(jax.ShapeDtypeStruct((3, 48, D), j...]
    convert_element_type x2 -> x0, other arithmetic: 9.94 us -> none  [the longest x1 9.93 us: body(): lax.psum(jnp.stack([partial[k] for k in (0, 3, 4, 5, 6)]), axes)]
    dot_general x13 -> x6, matrix products: 24.1 us -> 14.7 us  [inner_rows(): lax.dot_general(left, right, (((0,), (0,)), ((), ())), preferred_element_...]
    reduce_sum x2 -> x0, other arithmetic: 7.68 us -> none  [body(): norm = jnp.sqrt(jnp.trace(gram)) + 1e-07]
  transfers between devices with their start and end apart: 3 -> 2, of which waited for: 2 -> 1; matrix products, arithmetic and copies ran while one was open for 1% -> 3% of each run, Pallas kernels for 0% -> 0%
where the time goes in v3:
time: 377 us; the launch traced here: 374 us
  Pallas kernels  261 us (69%)
  other arithmetic  45.1 us (12%)
  matrix products  31.4 us (8%)
  local copies, waits for them, and re-layouts  27.2 us (7%)
    pallas_call x1, Pallas kernels, scatter_blocks(): pl.pallas_call(scatter_kernel, out_shape=jax.ShapeDtypeStruct((ROWS, D),...  78.2 us
    pallas_call x1, Pallas kernels, gather_blocks(): pl.pallas_call(gather_kernel, out_shape=(jax.ShapeDtypeStruct((4, 4, 2, 2...  77.4 us
    pallas_call x1, Pallas kernels, muon(): pl.pallas_call(muon_kernel, out_shape=(jax.ShapeDtypeStruct((3, 48, D), j...  67.2 us
    pallas_call x1, Pallas kernels, mlp(): pl.pallas_call(mlp_kernel, grid=(TILES,), out_shape=(jax.ShapeDtypeStruct...  38.5 us
    dot_general x6, matrix products, inner_rows(): lax.dot_general(left, right, (((0,), (0,)), ((), ())), preferred_element_...  14.7 us
  transfers between devices with their start and end apart: 2, of which 1 were waited for; matrix products, arithmetic and copies ran while one was open for 3% of the time, Pallas kernels for 0%

profile of v3, /device:TPU:1, one launch (start us, length us, event | category | flops | bytes accessed | tf_op | source)
XLA Modules:
  0.0 373.7 jit_solution(894680048529512159)
XLA Ops:
  0.7 0.9 convert.146
  1.6 0.8 convert.147
  2.4 0.8 convert.148
  3.1 0.7 convert.149
  3.8 0.7 convert.150
  5.2 1.0 convert_bitcast_fusion
  6.8 2.1 collective-permute-start
  9.1 1.2 multiply_reduce_fusion.5
  10.7 1.9 fusion.42.e_ref
  12.7 4.1 %convert_convert_fusion.20 = bf16[1024,896]{1,0:T(8,128)(2,1)} fusion(s32[1024]{0:T(1024)S(1)} %get-tuple-element.160, s32[1024]{0:T(1024)S(1)} %get-tuple-element.166, pred[1024]{0:T(1024)(128)(4,1)S(1)} %fusion.111, s32[1024]{0:T(1024)S(1)} %get-tuple-element.162, s32[1024]{0:T(1024)S(1)} %get-tuple-element.163, ...), kind=kLoop, calls=%fused_computation.25.clone.1.clone.clone.clone.1 | loop fusion | flops 33947648 | bytes 1862656 | tf_op jit(solution)/shard_map/dot_general | solution.py:45
  16.8 0.7 broadcast_and_fusion
  18.3 0.9 concatenate.91
  19.3 77.4 %shard_map.339 = (bf16[4,4,2,2,144,896]{5,4,3,2,1,0:T(8,128)(2,1)}, bf16[2,4,4,2,48,896]{5,4,3,2,1,0:T(8,128)(2,1)S(1)}) custom-call(bf16[144,896]{1,0:T(8,128)(2,1)S(1)} %slice_select_fusion.block_ref), custom_call_target="tpu_custom_call" | custom-call | tf_op jit(solution)/shard_map/pallas_call | solution.py:225
  96.8 2.4 copy-done.2
  99.3 0.8 slice.216
  100.9 3.6 fusion.133
  104.6 2.8 fusion.26
  107.6 0.9 copy-done.15
  108.7 0.7 convolution_add_fusion.3
  110.7 1.4 copy.58
  112.6 2.1 fusion.31
  114.7 0.8 copy-done.17
  116.9 1.4 fusion.34
  119.1 1.0 fusion.81
  120.2 1.4 fusion.39
  121.6 1.8 fusion.142
  123.5 1.1 copy-done.6
  125.6 2.8 fusion.27
  128.4 0.8 multiply_reduce_fusion.4
  129.3 0.9 multiply_convert_fusion.1.h_ref
  130.2 38.5 %shard_map.340 = (f32[256,896]{1,0:T(8,128)}, f32[256,896]{1,0:T(8,128)}, bf16[32,240,896]{2,1,0:T(8,128)(2,1)}) custom-call(bf16[256,896]{1,0:T(8,128)(2,1)} %multiply_convert_fusion.1.h_ref, bf16[256,896]{1,0:T(8,128)(2,1)} %fusion.42.e_ref, bf16[32,288,896]{2,1,0:T(8,128)(2,1)} %bitcast.229, bf16[32,288,896]{2,1,0:T(8,128)(2,1)} %bitcast.230, ...), custom_call_target="tpu_custom_call" | custom-call | tf_op jit(solution)/shard_map/pallas_call | solution.py:498
  168.7 2.1 multiply_reduce_fusion
  170.8 2.7 fusion.41
  173.5 0.7 convolution_convert_fusion.4
  174.2 5.0 %convolution_convert_fusion = bf16[1024,896]{1,0:T(8,128)(2,1)} fusion(bf16[112,8,2,128]{3,2,1,0:T(2,128)(2,1)S(1)} %bitcast.249, f32[256,896]{1,0:T(8,128)S(1)} %get-tuple-element.104, s32[1024]{0:T(1024)S(1)} %get-tuple-element.160, s32[1024]{0:T(1024)S(1)} %copy-done.39, s32[1024]{0:T(1024)S(1)} %copy-done.33, s32[1024]{0:T(1024)S(1)} %copy-done.36, ...), kind=kOutput, calls=%fused_computation.43 | convolution fusion | flops 974880768 | bytes 3238912 | tf_op jit(solution)/shard_map/dot_general | solution.py:39
  179.2 0.7 reshape.361
  180.0 0.8 copy.70
  180.8 2.1 fusion.22
  184.0 1.3 broadcast_multiply_fusion
  185.2 0.7 copy.73
  186.0 0.7 copy_multiply_fusion
  187.0 0.8 copy.81
  188.3 0.8 copy.82
  189.1 0.7 fusion.29
  190.5 1.7 fusion.148
  192.2 0.8 convolution_convert_fusion.1
  193.8 1.2 convolution_convert_fusion.2
  195.0 2.1 reshape.346
  197.1 1.7 fusion.52
  198.9 1.6 convolution_add_fusion.1
  200.5 2.3 multiply_reduce_fusion.1
  204.7 1.7 fusion.36
  207.0 4.8 %pad_maximum_fusion.rest_ref = bf16[2,4,4,2,48,896]{5,4,3,2,1,0:T(8,128)(2,1)} fusion(bf16[2,4,4,2,16,896]{5,4,3,2,1,0:T(8,128)(2,1)S(1)} %bitcast.236, bf16[2,4,4,2,16,896]{5,4,3,2,1,0:T(8,128)(2,1)S(1)} %bitcast.252, bf16[2,4,4,2,16,896]{5,4,3,2,1,0:T(8,128)(2,1)S(1)} %bitcast.235), kind=kLoop, calls=%fused_computation.12 | loop fusion | flops 16515072 | bytes 11010048 | tf_op jit(solution)/shard_map/concatenate | solution.py:583
  211.8 78.2 %shard_map.341 = bf16[144,896]{1,0:T(8,128)(2,1)} custom-call(bf16[4,4,2,240,896]{4,3,2,1,0:T(8,128)(2,1)} %bitcast.232, bf16[2,4,4,2,48,896]{5,4,3,2,1,0:T(8,128)(2,1)} %pad_maximum_fusion.rest_ref), custom_call_target="tpu_custom_call" | custom-call | tf_op jit(solution)/shard_map/pallas_call | solution.py:411
  290.8 1.1 add_convert_fusion
  291.9 3.7 collective-permute-done.1
  295.6 1.2 fusion.46
  296.8 0.8 fusion.96
  299.0 0.8 pad_maximum_fusion.2.sent_ref
  299.8 67.2 %shard_map.342 = (bf16[3,48,896]{2,1,0:T(8,128)(2,1)}, bf16[2,16,896]{2,1,0:T(8,128)(2,1)}, bf16[2,16,128]{2,1,0:T(8,128)(2,1)}) custom-call(bf16[4,48,896]{2,1,0:T(8,128)(2,1)} %pad_maximum_fusion.2.sent_ref), custom_call_target="tpu_custom_call" | custom-call | tf_op jit(solution)/shard_map/pallas_call | solution.py:925
  367.0 1.7 bitcast_subtract_fusion.1
  368.7 1.6 bitcast_subtract_fusion.3
  370.3 1.4 bitcast_subtract_fusion.4
  371.6 1.3 bitcast_subtract_fusion.6
  (216 shorter events, 17.0 us)
Async XLA Ops:
  0.7 9.8 %copy-start = (s32[2,128]{1,0:T(2,128)S(1)}, s32[2,128]{1,0:T(2,128)}, u32[]{:S(2)}) copy-start(s32[2,128]{1,0:T(2,128)} %param.22) | copy-start | bytes 3076
  6.8 10.7 %collective-permute-start = (bf16[131,896]{1,0:T(8,128)(2,1)S(1)}, bf16[131,896]{1,0:T(8,128)(2,1)S(1)}, u32[]{:S(2)}, u32[]{:S(2)}) collective-permute-start(bf16[131,896]{1,0:T(8,128)(2,1)S(1)} %concatenate.89), channel_id=1, source_target_pairs={{0,2},{2,0},{4,6},{6,4},{8,10},{10,8},{12,14},{14,12},{16,18},{18,... | collective-permute-start | bytes 704264 | tf_op jit(solution)/shard_map/ppermute | solution.py:538
  9.0 103.5 %copy-start.29 = (s32[1024]{0:T(1024)}, s32[1024]{0:T(1024)S(1)}, u32[]{:S(2)}) copy-start(s32[1024]{0:T(1024)S(1)} %get-tuple-element.161) | copy-start | bytes 12292
  9.0 95.6 %copy-start.31 = (s32[1024]{0:T(1024)}, s32[1024]{0:T(1024)S(1)}, u32[]{:S(2)}) copy-start(s32[1024]{0:T(1024)S(1)} %get-tuple-element.162) | copy-start | bytes 12292
  9.0 95.6 %copy-start.34 = (s32[1024]{0:T(1024)}, s32[1024]{0:T(1024)S(1)}, u32[]{:S(2)}) copy-start(s32[1024]{0:T(1024)S(1)} %get-tuple-element.163) | copy-start | bytes 12292
  9.0 95.5 %copy-start.37 = (s32[1024]{0:T(1024)}, s32[1024]{0:T(1024)S(1)}, u32[]{:S(2)}) copy-start(s32[1024]{0:T(1024)S(1)} %get-tuple-element.166) | copy-start | bytes 12292
  9.0 95.5 %copy-start.40 = (s32[1024]{0:T(1024)}, s32[1024]{0:T(1024)S(1)}, u32[]{:S(2)}) copy-start(s32[1024]{0:T(1024)S(1)} %get-tuple-element.167) | copy-start | bytes 12292
  9.0 95.5 %copy-start.49 = (pred[1024]{0:T(1024)(128)(4,1)}, pred[1024]{0:T(1024)(128)(4,1)S(1)}, u32[]{:S(2)}) copy-start(pred[1024]{0:T(1024)(128)(4,1)S(1)} %get-tuple-element.164) | copy-start | bytes 3076
  9.0 95.5 %copy-start.52 = (pred[1024]{0:T(1024)(128)(4,1)}, pred[1024]{0:T(1024)(128)(4,1)S(1)}, u32[]{:S(2)}) copy-start(pred[1024]{0:T(1024)(128)(4,1)S(1)} %get-tuple-element.165) | copy-start | bytes 3076
  9.1 95.5 %copy-start.57 = (pred[1024]{0:T(1024)(128)(4,1)}, pred[1024]{0:T(1024)(128)(4,1)S(1)}, u32[]{:S(2)}) copy-start(pred[1024]{0:T(1024)(128)(4,1)S(1)} %fusion.111) | copy-start | bytes 3076
  10.7 7.5 %copy-start.45 = (f32[256]{0:T(256)}, f32[256]{0:T(256)S(1)}, u32[]{:S(2)}) copy-start(f32[256]{0:T(256)S(1)} %get-tuple-element.143) | copy-start | bytes 3076
  96.8 2.4 copy-start.2
  104.6 2.8 copy-start.3
  107.4 1.1 copy-start.15
  107.6 1.1 copy-start.10
  109.7 2.8 copy-start.32
  109.7 2.8 copy-start.35
  109.7 2.8 copy-start.38
  109.7 2.8 copy-start.41
  109.7 2.8 copy-start.50
  109.7 2.8 copy-start.53
  109.8 2.8 copy-start.58
  112.6 2.9 copy-start.11
  120.2 4.4 %copy-start.26 = (bf16[2,128,2,64]{1,0,3,2:T(2,128)(2,1)S(1)}, bf16[2,128,2,64]{1,0,3,2:T(2,128)(2,1)}, u32[]{:S(2)}) copy-start(bf16[2,128,2,64]{1,0,3,2:T(2,128)(2,1)} %reshape.330) | copy-start | bytes 196612
  123.3 1.2 copy-start.6
  123.3 2.2 copy-start.5
  123.4 2.2 copy-start.30
  123.4 2.2 copy-start.33
  123.4 2.2 copy-start.36
  123.4 2.2 copy-start.39
  123.4 2.2 copy-start.42
  123.4 2.2 copy-start.51
  123.4 2.2 copy-start.54
  123.4 2.2 copy-start.59
  130.2 40.6 %copy-start.13 = (bf16[2,1,128,896]{3,2,1,0:T(8,128)(2,1)S(1)}, bf16[2,1,128,896]{3,2,1,0:T(8,128)(2,1)}, u32[]{:S(2)}) copy-start(bf16[2,1,128,896]{3,2,1,0:T(8,128)(2,1)} %param.21) | copy-start | bytes 1376260
  130.2 40.6 %copy-start.46 = (f32[256]{0:T(256)S(1)}, f32[256]{0:T(256)}, u32[]{:S(2)}) copy-start(f32[256]{0:T(256)} %copy-done.45) | copy-start | bytes 3076
  180.8 2.1 copy-start.7
  186.0 3.2 copy-start.9
  186.0 3.1 copy-start.12
  189.1 1.4 copy-start.16
  190.5 2.6 copy-start.8
  195.0 8.0 %copy-start.48 = (bf16[2944]{0:T(1024)(128)(2,1)S(1)}, bf16[2944]{0:T(1024)(128)(2,1)}, u32[]{:S(2)}) copy-start(bf16[2944]{0:T(1024)(128)(2,1)} %custom-call) | copy-start | bytes 17668
  195.0 8.2 %copy-start.47 = (bf16[896]{0:T(1024)(128)(2,1)S(1)}, bf16[896]{0:T(1024)(128)(2,1)}, u32[]{:S(2)}) copy-start(bf16[896]{0:T(1024)(128)(2,1)} %get-tuple-element.73) | copy-start | bytes 5380
  204.7 2.3 copy-start.14
  211.8 79.0 %copy-start.4 = (f32[256,896]{1,0:T(8,128)S(1)}, f32[256,896]{1,0:T(8,128)}, u32[]{:S(2)}) copy-start(f32[256,896]{1,0:T(8,128)} %get-tuple-element.155) | copy-start | bytes 2752516
  290.0 6.8 %copy-start.21 = (f32[896,38]{0,1:T(8,128)S(1)}, f32[896,38]{0,1:T(8,128)}, u32[]{:S(2)}) copy-start(f32[896,38]{0,1:T(8,128)} %param.35) | copy-start | bytes 408580
  290.0 6.8 %copy-start.22 = (f32[896,38]{0,1:T(8,128)S(1)}, f32[896,38]{0,1:T(8,128)}, u32[]{:S(2)}) copy-start(f32[896,38]{0,1:T(8,128)} %param.36) | copy-start | bytes 408580
  290.0 6.8 %copy-start.23 = (f32[38,896]{1,0:T(8,128)S(1)}, f32[38,896]{1,0:T(8,128)}, u32[]{:S(2)}) copy-start(f32[38,896]{1,0:T(8,128)} %param.37) | copy-start | bytes 408580
  290.1 7.6 %copy-start.55 = (f32[7,128]{1,0:T(8,128)S(1)}, f32[7,128]{1,0:T(8,128)}, u32[]{:S(2)}) copy-start(f32[7,128]{1,0:T(8,128)} %param.33) | copy-start | bytes 10756
  290.1 7.6 %copy-start.56 = (f32[7,128]{1,0:T(8,128)S(1)}, f32[7,128]{1,0:T(8,128)}, u32[]{:S(2)}) copy-start(f32[7,128]{1,0:T(8,128)} %param.32) | copy-start | bytes 10756
  290.1 8.2 %copy-start.27 = (f32[7,896]{1,0:T(8,128)S(1)}, f32[7,896]{1,0:T(8,128)}, u32[]{:S(2)}) copy-start(f32[7,896]{1,0:T(8,128)} %param.34) | copy-start | bytes 75268
  290.1 8.2 %copy-start.28 = (f32[7,896]{1,0:T(8,128)S(1)}, f32[7,896]{1,0:T(8,128)}, u32[]{:S(2)}) copy-start(f32[7,896]{1,0:T(8,128)} %param.31) | copy-start | bytes 75268
  290.1 5.5 %collective-permute-start.1 = (bf16[144,896]{1,0:T(8,128)(2,1)}, bf16[144,896]{1,0:T(8,128)(2,1)S(1)}, u32[]{:S(2)}, u32[]{:S(2)}) collective-permute-start(bf16[144,896]{1,0:T(8,128)(2,1)} %shard_map.341), channel_id=1, source_target_pairs={{0,2},{2,0},{4,6},{6,4},{8,10},{10,8},{12,14},{14,12},{16,18},{18,... | collective-permute-start | bytes 774152 | tf_op jit(solution)/shard_map/ppermute | solution.py:538
  290.7 76.3 %copy-start.19 = (f32[896,38]{0,1:T(8,128)S(1)}, f32[896,38]{0,1:T(8,128)}, u32[]{:S(2)}) copy-start(f32[896,38]{0,1:T(8,128)} %param.28) | copy-start | bytes 408580
  290.7 76.3 %copy-start.20 = (f32[896,38]{0,1:T(8,128)S(1)}, f32[896,38]{0,1:T(8,128)}, u32[]{:S(2)}) copy-start(f32[896,38]{0,1:T(8,128)} %param.27) | copy-start | bytes 408580
  290.7 78.0 %copy-start.18 = (f32[38,896]{1,0:T(8,128)S(1)}, f32[38,896]{1,0:T(8,128)}, u32[]{:S(2)}) copy-start(f32[38,896]{1,0:T(8,128)} %param.29) | copy-start | bytes 408580
  290.7 82.7 %copy-start.1 = (s32[2,128]{1,0:T(2,128)S(1)}, s32[2,128]{1,0:T(2,128)}, u32[]{:S(2)}) copy-start(s32[2,128]{1,0:T(2,128)} %param.22) | copy-start | bytes 3076
  291.8 78.5 %copy-start.24 = (f32[7,896]{1,0:T(8,128)S(1)}, f32[7,896]{1,0:T(8,128)}, u32[]{:S(2)}) copy-start(f32[7,896]{1,0:T(8,128)} %param.23) | copy-start | bytes 75268
  291.8 78.5 %copy-start.25 = (f32[7,896]{1,0:T(8,128)S(1)}, f32[7,896]{1,0:T(8,128)}, u32[]{:S(2)}) copy-start(f32[7,896]{1,0:T(8,128)} %param.26) | copy-start | bytes 75268
  291.8 79.8 %copy-start.43 = (f32[7,128]{1,0:T(8,128)S(1)}, f32[7,128]{1,0:T(8,128)}, u32[]{:S(2)}) copy-start(f32[7,128]{1,0:T(8,128)} %param.25) | copy-start | bytes 10756
  291.8 79.8 %copy-start.44 = (f32[7,128]{1,0:T(8,128)S(1)}, f32[7,128]{1,0:T(8,128)}, u32[]{:S(2)}) copy-start(f32[7,128]{1,0:T(8,128)} %param.24) | copy-start | bytes 10756
  291.8 81.1 %copy-start.60 = (f32[23]{0:T(128)S(1)}, f32[23]{0:T(128)}, u32[]{:S(2)}) copy-start(f32[23]{0:T(128)} %param.30) | copy-start | bytes 280
  291.8 81.1 %copy-start.61 = (f32[23]{0:T(128)S(1)}, f32[23]{0:T(128)}, u32[]{:S(2)}) copy-start(f32[23]{0:T(128)} %param.39) | copy-start | bytes 280
  291.8 81.1 %copy-start.62 = (f32[23]{0:T(128)S(1)}, f32[23]{0:T(128)}, u32[]{:S(2)}) copy-start(f32[23]{0:T(128)} %param.38) | copy-start | bytes 280
  (1 other events, 0.8 us)

commit v4 on v1

v4 whole, which is shorter than its diff:
```python
import math

import jax
import jax.numpy as jnp
from jax import lax
from jax.experimental import pallas as pl
from jax.experimental.pallas import tpu as pltpu
from jax.sharding import PartitionSpec as P

D = 896
FF = 4864
HEADS = 14
KV_HEADS = 2
HEAD = 64
STEP = 10


NORM_EPSILON = 1e-06
ROPE_BASE = 1000000.0
MOMENTUM = 0.95
NEWTON_A = 3.4445
NEWTON_B = -4.775
NEWTON_C = 2.0315
MUON_RATE = 0.4
MUON_DECAY = 0.1
ADAM_RATE = 0.5
ADAM_DECAY = 0.01
BETA_FIRST = 0.9
BETA_SECOND = 0.999
ADAM_EPSILON = 1e-08
MASKED = -1e30


def product(left, right):
    return jnp.dot(left, right, preferred_element_type=jnp.float32)


def inner_rows(left, right):
    return lax.dot_general(
        left, right, (((0,), (0,)), ((), ())), preferred_element_type=jnp.float32
    )


def outer_cols(left, right):
    return lax.dot_general(
        left, right, (((1,), (1,)), ((), ())), preferred_element_type=jnp.float32
    )


def rotary_tables(length):
    half = HEAD // 2
    freqs = ROPE_BASE ** (-jnp.arange(half, dtype=jnp.float32) * 2.0 / HEAD)
    angles = jnp.arange(length, dtype=jnp.float32)[:, None] * freqs[None, :]
    angles = jnp.concatenate([angles, angles], axis=-1)
    return (jnp.cos(angles), jnp.sin(angles))


def norm_back(grad, normed, scale):
    return scale * (grad - normed * jnp.mean(grad * normed, axis=-1, keepdims=True))


def half(value):
    return value.astype(jnp.bfloat16)


MESH = pl.DeviceIdType.MESH
TOKENS = 256
FULL = (0, 4)
BF16 = jnp.bfloat16
F32 = jnp.float32
CHUNK = 48
PARTS = (
    (0, 0, CHUNK, (2, 1, 0), False),
    (0, CHUNK, CHUNK, (1, 0, 2), False),
    (1, 0, CHUNK, (0, 2, 1), True),
    (2, 0, 16, (2, 1, 0), True),
    (2, 16, 16, (1, 0, 2), True),
    (2, 32, 16, (0, 2, 1), True),
)
WIDE = (0, 1, 2)
THIN = (3, 4, 5)


def my_coords():
    dp = lax.axis_index("dp")
    return (dp // 16, (dp // 4) % 4, dp % 4), lax.axis_index("narrow")


def device_of(coords, core):
    return (coords[0] * 16 + coords[1] * 4 + coords[2], core)


def shifted(coords, axis, by):
    out = list(coords)
    out[axis] = (coords[axis] + by) % 4
    return tuple(out)


def facing(coords):
    return (coords[0], coords[1], 3 - coords[2])


def greet(coords, core):
    barrier = pltpu.get_barrier_semaphore()
    for axis in range(3):
        for by in (1, 3):
            pl.semaphore_signal(
                barrier, inc=1, device_id=device_of(shifted(coords, axis, by), core), device_id_type=MESH
            )
    pl.semaphore_signal(barrier, inc=1, device_id=device_of(coords, 1 - core), device_id_type=MESH)
    pl.semaphore_wait(barrier, 7)


def remote(src, dst, send_sem, recv_sem, device):
    return pltpu.make_async_remote_copy(
        src_ref=src,
        dst_ref=dst,
        send_sem=send_sem,
        recv_sem=recv_sem,
        device_id=device,
        device_id_type=MESH,
    )


def place_of(part, piece):
    spec, columns = piece
    _, first, rows, _, shared = PARTS[part]
    index = [pl.ds(*s) if isinstance(s, tuple) else s for s in spec[:2]]
    s = spec[2]
    if isinstance(s, tuple):
        index.append(pl.ds(s[0] // 2, s[1] // 2))
        index += [] if shared else [pl.ds(0, 2)]
    else:
        index.append(s // 2)
        index += [] if shared else [s % 2]
    columns = (0, D) if columns is None else columns
    return (*index, pl.ds(first, rows), pl.ds(*columns))


def shape_of(part, piece):
    return tuple(entry.size for entry in place_of(part, piece) if isinstance(entry, pl.Slice))


def halves(spec, axis):
    if axis is None:
        return [(spec, (0, 512)), (spec, (512, 384))]
    out = []
    for h in range(2):
        s = list(spec)
        s[axis] = (2 * h, 2)
        out.append((tuple(s), None))
    return out


class Plan:
    def __init__(self, part, coords, axis, spec, split):
        self.coords, self.axis, self.spec, self.split = coords, axis, spec, split
        self.exchange = PARTS[part][4] and axis == 2

    def pieces(self, by):
        spec = list(self.spec)
        spec[self.axis] = (self.coords[self.axis] + by) % 4
        return halves(tuple(spec), self.split)

    def facing(self):
        return ((*self.spec[:2], 3 - self.coords[2]), None)

    def own(self):
        return (self.spec, None)


def plan_of(part, stage, coords):
    order = PARTS[part][3]
    spec = tuple(FULL if k in order[:stage] else coords[k] for k in range(3))
    return Plan(part, coords, order[stage], spec, order[stage - 1] if stage else None)


class Gather:
    def __init__(self, arrays, coords, core, send_sems, recv_sems):
        self.arrays, self.coords, self.core = arrays, coords, core
        self.send_sems, self.recv_sems = send_sems, recv_sems

    def copy(self, part, phase, slot, piece, coords):
        array, prefix = self.arrays[PARTS[part][0]]
        ref = array.at[(*prefix, *place_of(part, piece))]
        sems = (self.send_sems.at[part, phase, slot], self.recv_sems.at[part, phase, slot])
        return remote(ref, ref, *sems, device_of(coords, self.core))

    def send(self, *args):
        self.copy(*args).start()

    def neighbours(self, plan):
        return shifted(self.coords, plan.axis, 1), shifted(self.coords, plan.axis, 3)

    def start(self, parts, phase):
        for part in parts:
            plan = plan_of(part, phase, self.coords)
            if plan.exchange:
                self.send(part, phase, 0, plan.own(), facing(self.coords))
                continue
            right, left = self.neighbours(plan)
            first, second = plan.pieces(0)
            self.send(part, phase, 0, first, right)
            self.send(part, phase, 1, second, left)
            self.send(part, phase, 2, second, right)
            self.send(part, phase, 3, first, left)

    def forward(self, parts, phase):
        for part in parts:
            plan = plan_of(part, phase, self.coords)
            if plan.exchange:
                continue
            right, left = self.neighbours(plan)
            piece = plan.pieces(3)[0]
            self.copy(part, phase, 0, piece, right).wait_recv()
            self.send(part, phase, 4, piece, right)
            piece = plan.pieces(1)[1]
            self.copy(part, phase, 1, piece, left).wait_recv()
            self.send(part, phase, 5, piece, left)

    def near(self, parts, phase):
        for part in parts:
            plan = plan_of(part, phase, self.coords)
            if plan.exchange:
                self.copy(part, phase, 0, plan.facing(), facing(self.coords)).wait_recv()
                continue
            right, left = self.neighbours(plan)
            self.copy(part, phase, 2, plan.pieces(3)[1], right).wait_recv()
            self.copy(part, phase, 3, plan.pieces(1)[0], left).wait_recv()

    def far(self, parts, phase):
        for part in parts:
            plan = plan_of(part, phase, self.coords)
            if plan.exchange:
                continue
            right, left = self.neighbours(plan)
            self.copy(part, phase, 4, plan.pieces(2)[0], right).wait_recv()
            self.copy(part, phase, 5, plan.pieces(2)[1], left).wait_recv()

    def finish(self, parts, phase):
        self.near(parts, phase)
        self.far(parts, phase)

    def drain(self):
        for part in range(6):
            for phase in range(3):
                plan = plan_of(part, phase, self.coords)
                if plan.exchange:
                    self.copy(part, phase, 0, plan.own(), facing(self.coords)).wait_send()
                    continue
                right, _ = self.neighbours(plan)
                for slot, which in enumerate((0, 1, 1, 0, 0, 1)):
                    self.copy(part, phase, slot, plan.pieces(0)[which], right).wait_send()


def each_block(shape, body):
    lead = shape[:-2]
    count = math.prod(lead)
    if count == 1:
        body((0,) * len(lead))
        return

    def step(k, carry):
        index = []
        for n in reversed(lead):
            index.append(k % n)
            k = k // n
        body(tuple(reversed(index)))
        return carry

    lax.fori_loop(0, count, step, 0)


class Scatter:
    def __init__(self, arrays, coords, core, buffers, send_sems, recv_sems):
        self.arrays, self.coords, self.core = arrays, coords, core
        self.buffers, self.send_sems, self.recv_sems = buffers, send_sems, recv_sems

    def copy(self, part, phase, slot, piece, coords):
        array, prefix = self.arrays[PARTS[part][0]]
        ref = array.at[(*prefix, *place_of(part, piece))]
        sems = (self.send_sems.at[part, phase, slot], self.recv_sems.at[part, phase, slot])
        return remote(ref, self.buffers[part, phase][slot], *sems, device_of(coords, self.core))

    def send(self, *args):
        self.copy(*args).start()

    def arrive(self, *args):
        self.copy(*args).wait_recv()

    def add(self, part, phase, piece, *slots):
        sources = [self.buffers[part, phase][slot] for slot in slots]
        base = place_of(part, piece)
        array, prefix = self.arrays[PARTS[part][0]]

        def one(index):
            spot, position = [], 0
            for entry in base[:-2]:
                if isinstance(entry, pl.Slice):
                    spot.append(entry.start + index[position])
                    position += 1
                else:
                    spot.append(entry)
            spot = (*prefix, *spot, *base[-2:])
            value = array[spot].astype(F32)
            for source in sources:
                value = value + source[(*index, slice(None), slice(None))].astype(F32)
            array[spot] = half(value)

        each_block(shape_of(part, piece), one)

    def neighbours(self, plan):
        return shifted(self.coords, plan.axis, 1), shifted(self.coords, plan.axis, 3)

    def start_far(self, parts, phase):
        for part in parts:
            plan = plan_of(part, phase, self.coords)
            if plan.exchange:
                continue
            right, left = self.neighbours(plan)
            self.send(part, phase, 0, plan.pieces(2)[0], right)
            self.send(part, phase, 1, plan.pieces(2)[1], left)

    def start_near(self, parts, phase):
        for part in parts:
            plan = plan_of(part, phase, self.coords)
            if plan.exchange:
                self.send(part, phase, 0, plan.facing(), facing(self.coords))
                continue
            right, left = self.neighbours(plan)
            self.send(part, phase, 2, plan.pieces(1)[1], right)
            self.send(part, phase, 3, plan.pieces(3)[0], left)

    def start(self, parts, phase):
        self.start_far(parts, phase)
        self.start_near(parts, phase)

    def forward(self, parts, phase):
        for part in parts:
            plan = plan_of(part, phase, self.coords)
            if plan.exchange:
                continue
            right, left = self.neighbours(plan)
            self.arrive(part, phase, 0, plan.pieces(2)[0], right)
            self.add(part, phase, plan.pieces(1)[0], 0)
            self.send(part, phase, 4, plan.pieces(1)[0], right)
            self.arrive(part, phase, 1, plan.pieces(2)[1], left)
            self.add(part, phase, plan.pieces(3)[1], 1)
            self.send(part, phase, 5, plan.pieces(3)[1], left)

    def finish(self, parts, phase):
        for part in parts:
            plan = plan_of(part, phase, self.coords)
            if plan.exchange:
                self.arrive(part, phase, 0, plan.facing(), facing(self.coords))
                self.add(part, phase, plan.own(), 0)
                continue
            right, left = self.neighbours(plan)
            self.arrive(part, phase, 3, plan.pieces(3)[0], left)
            self.arrive(part, phase, 4, plan.pieces(1)[0], right)
            self.add(part, phase, plan.pieces(0)[0], 4, 3)
            self.arrive(part, phase, 2, plan.pieces(1)[1], right)
            self.arrive(part, phase, 5, plan.pieces(3)[1], left)
            self.add(part, phase, plan.pieces(0)[1], 2, 5)

    def drain(self):
        for part in range(6):
            for phase in range(3):
                plan = plan_of(part, phase, self.coords)
                if plan.exchange:
                    self.copy(part, phase, 0, plan.own(), facing(self.coords)).wait_send()
                    continue
                right, _ = self.neighbours(plan)
                for slot, which in enumerate((0, 1, 1, 0, 0, 1)):
                    self.copy(part, phase, slot, plan.pieces(0)[which], right).wait_send()


def scatter_buffer_shapes():
    out = []
    for part in range(6):
        for phase in range(3):
            plan = plan_of(part, phase, (0, 0, 0))
            if plan.exchange:
                shapes = [shape_of(part, plan.own())]
            else:
                first, second = (shape_of(part, piece) for piece in plan.pieces(0))
                shapes = [first, second, second, first, first, second]
            out.append(((part, phase), shapes))
    return out


SCALE = HEAD ** (-0.5)


def turn(values, sign):
    lane = lax.broadcasted_iota(jnp.int32, values.shape, 1)
    ahead = pltpu.roll(values, 96, 1)
    behind = pltpu.roll(values, 32, 1)
    return jnp.where(lane & 32 == 0, sign * ahead, -sign * behind)


def tiles_of(values):
    return [values[:, 128 * t : 128 * t + 128] for t in range(values.shape[1] // 128)]


def rotated(values, cosine, sine):
    return jnp.concatenate(
        [tile * cosine + turn(tile, -1.0) * sine for tile in tiles_of(values)], axis=1
    )


def rotated_back(values, cosine, sine):
    return jnp.concatenate(
        [tile * cosine + turn(tile * sine, 1.0) for tile in tiles_of(values)], axis=1
    )


def low_lanes(shape):
    return lax.broadcasted_iota(jnp.int32, shape, 1) < HEAD


def paired(both):
    swapped = pltpu.roll(both, 64, 1)
    low = low_lanes(both.shape)
    even = [half(jnp.where(low, v, 0.0)) for v in (both, swapped)]
    odd = [half(jnp.where(low, 0.0, v)) for v in (swapped, both)]
    kinds = [jnp.concatenate([even[a], odd[b]]) for a, b in ((0, 0), (0, 1), (1, 1))]
    return [kinds[0]] * 3 + [kinds[1]] + [kinds[2]] * 3


def gathered_place():
    row = lax.broadcasted_iota(jnp.int32, (1024, D), 0)
    feature = lax.broadcasted_iota(jnp.int32, (1024, D), 1)
    slot = row & 15
    odd = (slot >= 7).astype(jnp.int32)
    device = (((row >> 4) & 31) * 2 + odd) * 2 + (row >> 9)
    source = jnp.where(slot < 14, 7 * device + slot - 7 * odd, -1)
    return half((source == feature).astype(jnp.float32))


def vector_maps():
    device = lax.broadcasted_iota(jnp.int32, (128, 1024), 0)
    row = lax.broadcasted_iota(jnp.int32, (128, 1024), 1)
    target = (device & 1) * 512 + (device >> 2) * 16 + ((device >> 1) & 1) * 7
    pick = half((row == target).astype(jnp.float32))
    start = lax.broadcasted_iota(jnp.int32, (128, 2944), 0) * 23
    entry = lax.broadcasted_iota(jnp.int32, (128, 2944), 1)
    owner = half(((entry >= start) & (entry < start + 23)).astype(jnp.float32))
    return pick, owner


def slot_mask(slots):
    return lax.broadcasted_iota(jnp.int32, (128, 2944), 0) == slots


def attention_forward(
    x_ref, rest_ref, len_ref, cos_ref, sin_ref, slot_ref,
    middle_ref, h1p_ref, q_ref, k_ref, v_ref, mixed_ref, probs_ref, vector_ref,
):
    place = gathered_place()
    pick, owner = vector_maps()
    stored = rest_ref[:, :, :, :, 32:48, 256:384].reshape(1024, 128)
    by_device = half(product(pick, stored))
    spread = inner_rows(by_device, owner)
    vector = jnp.sum(jnp.where(slot_mask(slot_ref[...]), spread, 0.0), axis=0, keepdims=True)
    vector_ref[...] = vector
    first_gain, second_gain = vector[:, :D], vector[:, D : 2 * D]
    query_bias, narrow_bias = vector[:, 2 * D : 3 * D], vector[:, 3 * D :]
    cosine, sine = cos_ref[...], sin_ref[...]
    inputs = x_ref[...].astype(jnp.float32)
    first_scale = lax.rsqrt(jnp.mean(inputs * inputs, axis=-1, keepdims=True) + NORM_EPSILON)
    normed = half(inputs * first_scale * first_gain)
    placed = half(outer_cols(normed, place))
    h1p_ref[...] = placed
    queries = product(placed, rest_ref[:, :, :, :, 0:16, :].reshape(1024, D)) + query_bias
    narrow = product(placed, rest_ref[:, :, :, :, 32:48, 0:256].reshape(1024, 256)) + narrow_bias
    q_ref[...] = half(rotated(queries, cosine, sine))
    keys = rotated(narrow[:, 0:128], cosine, sine)
    k_ref[...] = half(keys)
    values = narrow[:, 128:256]
    v_ref[...] = half(values)
    position = lax.broadcasted_iota(jnp.int32, (128, 256), 0)
    other = lax.broadcasted_iota(jnp.int32, (128, 256), 1) & 127
    causal = other <= position
    rows = []
    for b in range(2):
        here = slice(128 * b, 128 * b + 128)
        allowed = causal & (other < len_ref[here, :])
        key_tiles = paired(keys[here])
        value_tiles = paired(values[here])
        tiles = []
        for t in range(7):
            scores = outer_cols(q_ref[here, 128 * t : 128 * t + 128], key_tiles[t])
            scores = jnp.where(allowed, scores * SCALE, MASKED)
            parts = []
            for part in tiles_of(scores):
                shifted = jnp.exp(part - jnp.max(part, axis=-1, keepdims=True))
                parts.append(shifted / jnp.sum(shifted, axis=-1, keepdims=True))
            probs = jnp.concatenate(parts, axis=1)
            probs_ref[b, t] = probs
            tiles.append(half(product(half(probs), value_tiles[t])))
        rows.append(jnp.concatenate(tiles, axis=1))
    mixed = half(outer_cols(jnp.concatenate(rows), place))
    mixed_ref[...] = mixed
    middle = inputs + product(mixed, rest_ref[:, :, :, :, 16:32, :].reshape(1024, D))
    middle_ref[...] = middle
    second_scale = lax.rsqrt(jnp.mean(middle * middle, axis=-1, keepdims=True) + NORM_EPSILON)
    return half(middle * second_scale * second_gain)


def mlp_tile(weights, h, e, out_acc, back_acc):
    lead = weights.shape[:-2]
    units = 16 * math.prod(lead)
    gate_w, up_w, down_w = (
        weights[..., 16 * k : 16 * k + 16, :].reshape(units, D) for k in range(3)
    )
    gate = outer_cols(h, gate_w)
    up = outer_cols(h, up_w)
    sigma = jax.nn.sigmoid(gate)
    silu = gate * sigma
    hidden = half(silu * up)
    grad_hidden = outer_cols(e, down_w)
    out_acc[...] += product(hidden, down_w).reshape(2, TOKENS, D)
    grad_gate = half(grad_hidden * up * sigma * (1.0 + gate * (1.0 - sigma)))
    grad_up = half(grad_hidden * silu)
    back_acc[...] += (product(grad_gate, gate_w) + product(grad_up, up_w)).reshape(2, TOKENS, D)
    grads = (inner_rows(grad_gate, h), inner_rows(grad_up, h), inner_rows(hidden, e))
    return [half(grad).reshape(*lead, 16, D) for grad in grads]


def gather_kernel(
    wide_ref, tail_ref, x_ref, cot_ref, len_ref, cos_ref, sin_ref, slot_ref,
    middle_ref, e_ref, h1p_ref, q_ref, k_ref, v_ref, mixed_ref, probs_ref, vector_ref,
    output_ref, dh2_ref, grad_wide_ref, grad_shared_ref, rest_ref,
    wide, shared, rest, stage0, stage1, stage2, h_all, e_all, out_acc, back_acc, parcel, arrived, tail,
    local_sems, send_sems, recv_sems, twin_sems, store_sems,
):
    coords, core = my_coords()
    z, y, x = coords
    pair, odd = x // 2, x % 2
    load = pltpu.make_async_copy(wide_ref, wide.at[z, y, pair, odd], local_sems.at[0])
    load.start()
    greet(coords, core)
    twin = device_of(coords, 1 - core)

    def to_twin(src, dst, slot):
        return remote(src, dst, twin_sems.at[0, slot], twin_sems.at[1, slot], twin)

    gather = Gather(((wide, ()), (shared, ()), (rest, (core,))), coords, core, send_sems, recv_sems)
    partner = device_of((z, y, x + 1 - 2 * odd), core)
    tail_copy = remote(tail_ref, tail, twin_sems.at[0, 4], twin_sems.at[1, 4], partner)
    tail_copy.start()
    load.wait()
    gather.start((0, 1), 0)
    token = lax.broadcasted_iota(jnp.int32, (TOKENS, 1), 0) & 127
    live = (token < len_ref[...]).astype(F32)
    e_ref[...] = half(cot_ref[...].astype(F32) * live)
    e_all[core] = e_ref[...]
    e_copy = to_twin(e_ref, e_all.at[core], 0)
    e_copy.start()
    tail_copy.wait()
    both = half(tail_ref[...].astype(F32) + tail[...].astype(F32))
    shared[z, y, pair] = both[:CHUNK]
    rest[core, z, y, pair] = both[CHUNK:]
    gather.start(THIN, 0)
    gather.start((2,), 0)
    gather.forward(THIN, 0)
    gather.finish(THIN, 0)
    gather.start(THIN, 1)
    gather.forward(WIDE, 0)
    gather.forward(THIN, 1)
    gather.finish(THIN, 1)
    gather.start(THIN, 2)
    gather.finish(WIDE, 0)
    gather.start(WIDE, 1)
    gather.forward(THIN, 2)
    gather.finish(THIN, 2)
    rest_copy = to_twin(rest.at[core], rest.at[core], 1)
    rest_copy.start()
    gather.forward(WIDE, 1)
    gather.finish(WIDE, 1)
    gather.start(WIDE, 2)
    rest_copy.wait()
    rest_store = pltpu.make_async_copy(rest, rest_ref, local_sems.at[0])
    rest_store.start()
    h_all[core] = attention_forward(
        x_ref, rest, len_ref, cos_ref, sin_ref, slot_ref,
        middle_ref, h1p_ref, q_ref, k_ref, v_ref, mixed_ref, probs_ref, vector_ref,
    )
    h_copy = to_twin(h_all.at[core], h_all.at[core], 2)
    h_copy.start()
    out_acc[...] = jnp.zeros_like(out_acc)
    back_acc[...] = jnp.zeros_like(back_acc)
    e_copy.wait()
    h_copy.wait()
    stages = (stage0, stage1, stage2)

    def tile_places(j):
        return (
            (wide, grad_wide_ref, (j, slice(None), slice(None), slice(None), pl.ds(0, CHUNK))),
            (wide, grad_wide_ref, (slice(None), slice(None), j // 2, j % 2, pl.ds(CHUNK, CHUNK))),
            (shared, grad_shared_ref, (slice(None), j, slice(None), pl.ds(0, CHUNK))),
        )

    def step(k, carry):
        @pl.when(k == 1)
        def _():
            gather.near(WIDE, 2)

        @pl.when(k == 3)
        def _():
            gather.far(WIDE, 2)

        offset = jnp.where(k < 2, k, 5 - k)
        h = h_all[...].reshape(2 * TOKENS, D)
        e = e_all[...].reshape(2 * TOKENS, D)
        for t, axis in enumerate((0, 2, 1)):
            j = (coords[axis] + offset) % 4
            source, target, index = tile_places(j)[t]
            grads = mlp_tile(source[(*index, slice(None))], h, e, out_acc, back_acc)
            copy = pltpu.make_async_copy(
                stages[t], target.at[(*index, slice(None))], store_sems.at[t]
            )

            @pl.when(k > 0)
            def _():
                copy.wait()

            for place, grad in enumerate(grads):
                stages[t][..., 16 * place : 16 * place + 16, :] = grad
            copy.start()

        @pl.when(k == 0)
        def _():
            gather.forward(WIDE, 2)

        return carry

    lax.fori_loop(0, 4, step, 0)
    parcel[0] = half(out_acc[1 - core])
    parcel[1] = half(back_acc[1 - core])
    parcel_copy = to_twin(parcel, arrived, 3)
    parcel_copy.start()
    parcel_copy.wait()
    output_ref[...] = half(
        (middle_ref[...] + (out_acc[core] + arrived[0].astype(F32))) * live
    )
    dh2_ref[...] = back_acc[core] + arrived[1].astype(F32)
    for t in range(3):
        _, target, index = tile_places(0)[t]
        pltpu.make_async_copy(
            stages[t], target.at[(*index, slice(None))], store_sems.at[t]
        ).wait()
    rest_store.wait()
    gather.drain()


def attention_backward(
    between, x_ref, e_ref, rest_ref, cos_ref, sin_ref, slot_ref,
    middle_ref, h1p_ref, q_ref, k_ref, v_ref, mixed_ref, probs_ref, vector_ref, dh2_ref,
    input_grad_ref, grad_ref,
):
    place = gathered_place()
    pick, owner = vector_maps()
    vector = vector_ref[...]
    first_gain, second_gain = vector[:, :D], vector[:, D : 2 * D]
    cosine, sine = cos_ref[...], sin_ref[...]
    middle = middle_ref[...]
    second_scale = lax.rsqrt(jnp.mean(middle * middle, axis=-1, keepdims=True) + NORM_EPSILON)
    second_normed = middle * second_scale
    dh2 = dh2_ref[...]
    second_gain_grad = jnp.sum(dh2 * second_normed, axis=0, keepdims=True)
    grad_middle = e_ref[...].astype(jnp.float32) + norm_back(
        dh2 * second_gain, second_normed, second_scale
    )
    branch = half(grad_middle)
    wide = rest_ref[:, :, :, :, 16:32, :].reshape(1024, D)
    grad_ref[:, :, :, :, 16:32, :] = half(inner_rows(mixed_ref[...], branch)).reshape(2, 4, 4, 2, 16, D)
    grad_mixed = half(product(half(outer_cols(branch, wide)), place))
    low = low_lanes((128, 128))
    query_rows, key_rows, value_rows = [], [], []
    for b in range(2):
        if b == 1:
            between()
        here = slice(128 * b, 128 * b + 128)
        key_tiles = paired(k_ref[here, :].astype(jnp.float32))
        value_tiles = paired(v_ref[here, :].astype(jnp.float32))
        tiles = []
        sums = [[jnp.zeros((128, 128), jnp.float32) for _ in range(4)] for _ in range(2)]
        for t in range(7):
            head = grad_mixed[here, 128 * t : 128 * t + 128]
            grad_probs = outer_cols(head, value_tiles[t])
            probs = probs_ref[b, t]
            parts = []
            for p, g in zip(tiles_of(probs), tiles_of(grad_probs)):
                parts.append(half(p * (g - jnp.sum(p * g, axis=-1, keepdims=True))))
            grad_scores = jnp.concatenate(parts, axis=1)
            tiles.append(product(grad_scores, key_tiles[t]) * SCALE)
            for which, (left, right) in enumerate(
                ((grad_scores, q_ref[here, 128 * t : 128 * t + 128]), (half(probs), head))
            ):
                both = inner_rows(left, right)
                even, odd = (2 * t) // 7, (2 * t + 1) // 7
                sums[which][even] += both[0:128]
                sums[which][2 + odd] += both[128:256]
        query_rows.append(jnp.concatenate(tiles, axis=1))
        joined = []
        for which in range(2):
            even0, even1, odd0, odd1 = sums[which]
            joined.append(
                jnp.where(low, even0 + pltpu.roll(odd0, 64, 1), odd1 + pltpu.roll(even1, 64, 1))
            )
        key_rows.append(joined[0] * SCALE)
        value_rows.append(joined[1])
    grad_query = half(rotated_back(jnp.concatenate(query_rows), cosine, sine))
    grad_key = half(rotated_back(jnp.concatenate(key_rows), cosine, sine))
    grad_narrow = jnp.concatenate([grad_key, half(jnp.concatenate(value_rows))], axis=1)
    placed = h1p_ref[...]
    grad_ref[:, :, :, :, 0:16, :] = half(inner_rows(placed, grad_query)).reshape(2, 4, 4, 2, 16, D)
    grad_ref[:, :, :, :, 32:48, 0:256] = half(inner_rows(placed, grad_narrow)).reshape(2, 4, 4, 2, 16, 256)
    bias_grad = jnp.sum(
        jnp.concatenate([grad_query, grad_narrow], axis=1).astype(jnp.float32), axis=0, keepdims=True
    )
    grad_placed = outer_cols(grad_query, rest_ref[:, :, :, :, 0:16, :].reshape(1024, D)) + outer_cols(
        grad_narrow, rest_ref[:, :, :, :, 32:48, 0:256].reshape(1024, 256)
    )
    high = half(grad_placed)
    remainder = half(grad_placed - high.astype(jnp.float32))
    grad_normed = product(high, place) + product(remainder, place)
    inputs = x_ref[...].astype(jnp.float32)
    first_scale = lax.rsqrt(jnp.mean(inputs * inputs, axis=-1, keepdims=True) + NORM_EPSILON)
    first_normed = inputs * first_scale
    first_gain_grad = jnp.sum(grad_normed * first_normed, axis=0, keepdims=True)
    input_grad_ref[...] = half(
        grad_middle + norm_back(grad_normed * first_gain, first_normed, first_scale)
    )
    vector_grad = jnp.concatenate([first_gain_grad, second_gain_grad, bias_grad], axis=1)
    spread = half(jnp.where(slot_mask(slot_ref[...]), vector_grad, 0.0))
    by_device = half(outer_cols(owner, spread))
    stored = half(inner_rows(pick, by_device))
    grad_ref[:, :, :, :, 32:48, 256:384] = stored.reshape(2, 4, 4, 2, 16, 128)
    grad_ref[:, :, :, :, 32:48, 384:] = jnp.zeros((2, 4, 4, 2, 16, D - 384), jnp.bfloat16)


def scatter_kernel(
    grad_wide_ref, grad_shared_ref, x_ref, e_ref, rest_ref, cos_ref, sin_ref, slot_ref,
    middle_ref, h1p_ref, q_ref, k_ref, v_ref, mixed_ref, probs_ref, vector_ref, dh2_ref,
    input_grad_ref, out_ref,
    wide, shared, thin, joined, mine, theirs, load_sems, send_sems, recv_sems, twin_sems, pair_sems,
    *buffers,
):
    coords, core = my_coords()
    z, y, x = coords
    pair, odd = x // 2, x % 2
    named, position = {}, 0
    for key, shapes in scatter_buffer_shapes():
        named[key] = buffers[position : position + len(shapes)]
        position += len(shapes)
    scatter = Scatter(((wide, ()), (shared, ()), (thin, (core,))), coords, core, named, send_sems, recv_sems)

    def load(part, by):
        spec = [FULL] * 3
        axis = PARTS[part][3][2]
        spec[axis] = (coords[axis] + by) % 4
        place = place_of(part, (tuple(spec), None))
        source = (grad_wide_ref, grad_shared_ref)[PARTS[part][0]]
        target = (wide, shared)[PARTS[part][0]]
        return pltpu.make_async_copy(source.at[place], target.at[place], load_sems.at[part, by])

    for by in (2, 1, 3, 0):
        for part in WIDE:
            load(part, by).start()
    greet(coords, core)

    for part in WIDE:
        load(part, 2).wait()
        scatter.start_far((part,), 2)
    for part in WIDE:
        load(part, 1).wait()
        load(part, 3).wait()
        scatter.start_near((part,), 2)

    def between():
        scatter.forward(WIDE, 2)

    attention_backward(
        between, x_ref, e_ref, rest_ref, cos_ref, sin_ref, slot_ref,
        middle_ref, h1p_ref, q_ref, k_ref, v_ref, mixed_ref, probs_ref, vector_ref, dh2_ref,
        input_grad_ref, thin,
    )
    twin_copy = remote(
        thin.at[1 - core], joined, twin_sems.at[0], twin_sems.at[1], device_of(coords, 1 - core)
    )
    twin_copy.start()
    for part in WIDE:
        load(part, 0).wait()
    twin_copy.wait()

    def join(index):
        thin[(core, *index)] = half(thin[(core, *index)].astype(F32) + joined[index].astype(F32))

    each_block((4, 4, 2, CHUNK, D), join)
    scatter.start(THIN, 2)
    for part in WIDE:
        scatter.finish((part,), 2)
        scatter.start((part,), 1)
    scatter.forward(THIN, 2)
    scatter.finish(THIN, 2)
    scatter.start(THIN, 1)
    scatter.forward(WIDE, 1)
    scatter.forward(THIN, 1)
    for part in WIDE:
        scatter.finish((part,), 1)
        scatter.start((part,), 0)
    scatter.finish(THIN, 1)
    scatter.start(THIN, 0)
    scatter.forward(WIDE, 0)
    scatter.forward(THIN, 0)
    scatter.finish(WIDE, 0)
    scatter.finish(THIN, 0)
    mine[0] = shared[z, y, pair]
    mine[1] = thin[core, z, y, pair]
    partner = device_of((z, y, x + 1 - 2 * odd), core)
    pair_copy = remote(mine, theirs, pair_sems.at[0], pair_sems.at[1], partner)
    pair_copy.start()
    pair_copy.wait()
    out_ref[0] = wide[z, y, pair, odd, 0:CHUNK].astype(F32)
    out_ref[1] = wide[z, y, pair, odd, CHUNK : 2 * CHUNK].astype(F32)
    out_ref[2] = mine[0].astype(F32) + theirs[0].astype(F32)
    out_ref[3] = mine[1].astype(F32) + theirs[1].astype(F32)
    scatter.drain()


def layer(blocks, tokens, cotangent, lengths):
    vmem = pl.BlockSpec(memory_space=pltpu.VMEM)
    anywhere = pl.BlockSpec(memory_space=pl.ANY)
    x = tokens.reshape(TOKENS, D)
    rows = jnp.repeat(lengths, 128)[:, None]
    cosine, sine = rotary_tables(128)
    tables = (
        jnp.tile(cosine, (2, 2)),
        jnp.tile(sine, (2, 2)),
        (jnp.arange(2944, dtype=jnp.int32) % 23)[None],
    )

    def shapes(*pairs):
        return [jax.ShapeDtypeStruct(shape, dtype) for shape, dtype in pairs]

    kept = pl.pallas_call(
        gather_kernel,
        out_shape=shapes(
            ((TOKENS, D), F32),
            ((TOKENS, D), BF16),
            ((TOKENS, 1024), BF16),
            ((TOKENS, D), BF16),
            ((TOKENS, 128), BF16),
            ((TOKENS, 128), BF16),
            ((TOKENS, 1024), BF16),
            ((2, 7, 128, 256), F32),
            ((1, 2944), F32),
            ((TOKENS, D), BF16),
            ((TOKENS, D), F32),
            ((4, 4, 2, 2, 2 * CHUNK, D), BF16),
            ((4, 4, 2, CHUNK, D), BF16),
            ((2, 4, 4, 2, CHUNK, D), BF16),
        ),
        in_specs=[anywhere] + [vmem] * 7,
        out_specs=[vmem] * 11 + [anywhere] * 3,
        scratch_shapes=[
            pltpu.VMEM((4, 4, 2, 2, 2 * CHUNK, D), BF16),
            pltpu.VMEM((4, 4, 2, CHUNK, D), BF16),
            pltpu.VMEM((2, 4, 4, 2, CHUNK, D), BF16),
            pltpu.VMEM((4, 2, 2, CHUNK, D), BF16),
            pltpu.VMEM((4, 4, CHUNK, D), BF16),
            pltpu.VMEM((4, 2, CHUNK, D), BF16),
            pltpu.VMEM((2, TOKENS, D), BF16),
            pltpu.VMEM((2, TOKENS, D), BF16),
            pltpu.VMEM((2, TOKENS, D), F32),
            pltpu.VMEM((2, TOKENS, D), F32),
            pltpu.VMEM((2, TOKENS, D), BF16),
            pltpu.VMEM((2, TOKENS, D), BF16),
            pltpu.VMEM((2 * CHUNK, D), BF16),
            pltpu.SemaphoreType.DMA((3,)),
            pltpu.SemaphoreType.DMA((6, 3, 6)),
            pltpu.SemaphoreType.DMA((6, 3, 6)),
            pltpu.SemaphoreType.DMA((2, 5)),
            pltpu.SemaphoreType.DMA((3,)),
        ],
        compiler_params=pltpu.CompilerParams(
            collective_id=0, has_side_effects=True, vmem_limit_bytes=60 * 2**20
        ),
    )(*blocks, x, cotangent.reshape(TOKENS, D), rows, *tables)
    (middle, e, h1p, q, k, v, mixed, probs, vector, output, dh2, grad_wide, grad_shared, rest) = kept
    input_grad, grads = pl.pallas_call(
        scatter_kernel,
        out_shape=shapes(((TOKENS, D), BF16), ((4, CHUNK, D), F32)),
        in_specs=[anywhere] * 2 + [vmem] * 15,
        out_specs=[vmem] * 2,
        scratch_shapes=[
            pltpu.VMEM((4, 4, 2, 2, 2 * CHUNK, D), BF16),
            pltpu.VMEM((4, 4, 2, CHUNK, D), BF16),
            pltpu.VMEM((2, 4, 4, 2, CHUNK, D), BF16),
            pltpu.VMEM((4, 4, 2, CHUNK, D), BF16),
            pltpu.VMEM((2, CHUNK, D), BF16),
            pltpu.VMEM((2, CHUNK, D), BF16),
            pltpu.SemaphoreType.DMA((3, 4)),
            pltpu.SemaphoreType.DMA((6, 3, 6)),
            pltpu.SemaphoreType.DMA((6, 3, 6)),
            pltpu.SemaphoreType.DMA((2,)),
            pltpu.SemaphoreType.DMA((2,)),
        ]
        + [pltpu.VMEM(shape, BF16) for _, group in scatter_buffer_shapes() for shape in group],
        compiler_params=pltpu.CompilerParams(
            collective_id=1, has_side_effects=True, vmem_limit_bytes=62 * 2**20
        ),
    )(grad_wide, grad_shared, x, e, rest, *tables, middle, h1p, q, k, v, mixed, probs, vector, dh2)
    return output.reshape(2, 1, 128, D), input_grad.reshape(2, 1, 128, D), grads


def pack(units, query, out, narrow, vector, parity):
    wide = jnp.concatenate(
        [half(rows[16 * k : 16 * k + 16]) for k in range(2) for rows in units]
    )
    narrow = jnp.concatenate(
        [narrow, jnp.pad(vector[None], ((0, 6), (0, D - 256 - vector.shape[0])))], axis=1
    )

    def placed(rows, size):
        low = jnp.pad(rows, ((0, 16 - size), (0, 0)))
        high = jnp.pad(rows, ((size, 16 - 2 * size), (0, 0)))
        return jnp.where(parity == 0, low, high)

    shared = [placed(rows[32:38], 6) for rows in units] + [
        placed(rows, 7) for rows in (query, out, narrow)
    ]
    return wide, half(jnp.concatenate(shared))


def newton_schulz(gram, values):
    gram_half = half(gram)
    first = half(NEWTON_B * gram + NEWTON_C * product(gram_half, gram_half))
    cross = product(gram_half, first)
    after = NEWTON_A * NEWTON_A * gram + 2.0 * NEWTON_A * cross + product(half(cross), first)
    after_half = half(after)
    second = half(NEWTON_B * after + NEWTON_C * product(after_half, after_half))
    values = half(NEWTON_A * values + product(half(values), first))
    return half(NEWTON_A * values.astype(F32) + product(values, second))


BLOCKS = [(i, j) for i in range(7) for j in range(i, 7)]
JOB_ROWS = (48, 48, 48, 16, 16, 16, 16)


def muon_kernel(
    tall_ref, short_ref, tall_out_ref, short_out_ref,
    rows, gram_out, gram_twin, gram_half_sum, gram_in, gram_all, gram, back, tall_got, short_got,
    job_sems, twin_sems, sum_sems, all_sems, back_sems,
):
    coords, core = my_coords()
    z, y, x = coords
    job = z * 2 + y // 2
    source = z * 2 + y // 2
    member = (y % 2) * 4 + x
    twin = device_of(coords, 1 - core)

    def group(peer):
        return device_of((z, (y // 2) * 2 + peer // 4, peer % 4), core)

    def square(k):
        return device_of((k // 2, (k % 2) * 2 + y % 2, x), core)

    barrier = pltpu.get_barrier_semaphore()
    for k in range(1, 8):
        for device in (group((member + k) % 8), square((source + k) % 8)):
            pl.semaphore_signal(barrier, inc=1, device_id=device, device_id_type=MESH)
    pl.semaphore_signal(barrier, inc=1, device_id=twin, device_id_type=MESH)
    pl.semaphore_wait(barrier, 15)

    def copy(src, dst, sems, slot, device):
        return remote(src, dst, sems.at[0, slot], sems.at[1, slot], device)

    def mine(m, tall, short):
        return tall.at[m] if m < 3 else short.at[m - 3]

    def job_copy(m):
        return remote(
            mine(m, tall_ref, short_ref),
            rows.at[source, pl.ds(0, JOB_ROWS[m])],
            job_sems.at[0, m],
            job_sems.at[1, source],
            square(m),
        )

    for m in range(7):

        @pl.when(job != m)
        def _():
            job_copy(m).start()

    for kind in range(2):
        count = (48, 16)[kind]

        @pl.when((job >= 3 * kind) & (job < 3 + 4 * kind))
        def _():
            if kind == 1:
                rows[:, 16:48] = jnp.zeros((8, 32, D), BF16)
                rows[source, 0:16] = short_ref[job - 3]
            else:
                rows[source] = tall_ref[job]
            for k in range(1, 8):
                other = (source + k) % 8
                arrival = rows.at[other, pl.ds(0, count)]
                remote(
                    arrival, arrival, job_sems.at[0, 0], job_sems.at[1, other], square(other)
                ).wait_recv()

    @pl.when(job < 7)
    def _():
        flat = rows[...].reshape(384, D)
        gram[...] = inner_rows(flat, flat)
        for index, (i, j) in enumerate(BLOCKS):
            gram_out[index // 16, index % 16] = half(
                gram[128 * i : 128 * i + 128, 128 * j : 128 * j + 128]
            )
        gram_out[1, 12:16] = jnp.zeros((4, 128, 128), BF16)
        twin_copy = copy(gram_out.at[1 - core], gram_twin, twin_sems, 0, twin)
        twin_copy.start()
        twin_copy.wait()
        gram_half_sum[...] = half(gram_out[core].astype(F32) + gram_twin[...].astype(F32))

        def sum_copy(k):
            peer = (member + k) % 8
            return copy(
                gram_half_sum.at[pl.ds(2 * peer, 2)], gram_in.at[k], sum_sems, k, group(peer)
            )

        for k in range(1, 8):
            sum_copy(k).start()
        total = gram_half_sum[pl.ds(2 * member, 2)].astype(F32)
        for k in range(1, 8):
            sum_copy(k).wait_recv()
            total = total + gram_in[k].astype(F32)
        gram_all[core, pl.ds(2 * member, 2)] = half(total)

        def all_copy(k, owner):
            ref = gram_all.at[core, pl.ds(2 * owner, 2)]
            return copy(ref, ref, all_sems, k, group((member + k) % 8))

        for k in range(1, 8):
            all_copy(k, member).start()
        for k in range(1, 8):
            all_copy(k, (member + 8 - k) % 8).wait_recv()
        last_copy = copy(gram_all.at[core], gram_all.at[core], twin_sems, 1, twin)
        last_copy.start()
        last_copy.wait()

        eye = lax.broadcasted_iota(jnp.int32, (128, 128), 0) == lax.broadcasted_iota(
            jnp.int32, (128, 128), 1
        )
        trace = 0.0
        for index, (i, j) in enumerate(BLOCKS):
            block = gram_all[index // 16, index % 16].astype(F32)
            gram[128 * i : 128 * i + 128, 128 * j : 128 * j + 128] = block
            if i == j:
                trace = trace + jnp.sum(jnp.where(eye, block, 0.0))
            else:
                gram[128 * j : 128 * j + 128, 128 * i : 128 * i + 128] = block.T
        inverse = 1.0 / (jnp.sqrt(jnp.full((1, 1), trace)) + 1e-07)
        moved = newton_schulz(
            gram[...] * (inverse * inverse), rows[...].reshape(384, D).astype(F32) * inverse
        )
        back[...] = moved.reshape(8, 48, D)
        for k in range(1, 8):
            sum_copy(k).wait_send()
            all_copy(k, member).wait_send()

    for m in range(7):

        @pl.when(job == m)
        def _():
            copies = []
            for k in range(1, 8):
                other = (source + k) % 8
                copies.append(
                    remote(
                        back.at[other, pl.ds(0, JOB_ROWS[m])],
                        mine(m, tall_got, short_got),
                        back_sems.at[0, k],
                        back_sems.at[1, m],
                        square(other),
                    )
                )
            for item in copies:
                item.start()
            if m < 3:
                tall_got[m] = back[source]
            else:
                short_got[m - 3] = back[source, 0:16]
            for item in copies:
                item.wait_send()

    for m in range(7):

        @pl.when(job != m)
        def _():
            arrival = mine(m, tall_got, short_got)
            remote(arrival, arrival, back_sems.at[0, 0], back_sems.at[1, m], square(m)).wait_recv()
            job_copy(m).wait_send()

    tall_out_ref[...] = tall_got[...]
    short_out_ref[...] = short_got[...]


def muon(tall, short):
    vmem = pl.BlockSpec(memory_space=pltpu.VMEM)
    return pl.pallas_call(
        muon_kernel,
        out_shape=(
            jax.ShapeDtypeStruct((3, 48, D), BF16),
            jax.ShapeDtypeStruct((4, 16, D), BF16),
        ),
        in_specs=[vmem] * 2,
        out_specs=(vmem,) * 2,
        scratch_shapes=[
            pltpu.VMEM((8, 48, D), BF16),
            pltpu.VMEM((2, 16, 128, 128), BF16),
            pltpu.VMEM((16, 128, 128), BF16),
            pltpu.VMEM((16, 128, 128), BF16),
            pltpu.VMEM((8, 2, 128, 128), BF16),
            pltpu.VMEM((2, 16, 128, 128), BF16),
            pltpu.VMEM((D, D), F32),
            pltpu.VMEM((8, 48, D), BF16),
            pltpu.VMEM((3, 48, D), BF16),
            pltpu.VMEM((4, 16, D), BF16),
            pltpu.SemaphoreType.DMA((2, 8)),
            pltpu.SemaphoreType.DMA((2, 2)),
            pltpu.SemaphoreType.DMA((2, 8)),
            pltpu.SemaphoreType.DMA((2, 8)),
            pltpu.SemaphoreType.DMA((2, 8)),
        ],
        compiler_params=pltpu.CompilerParams(
            collective_id=3, has_side_effects=True, vmem_limit_bytes=58 * 2**20
        ),
    )(tall, short)


def body(
    inputs,
    cotangent,
    lengths,
    query_weight,
    key_weight,
    value_weight,
    out_weight,
    gate_weight,
    up_weight,
    down_weight,
    vectors,
    query_prior,
    key_prior,
    value_prior,
    out_prior,
    gate_prior,
    up_prior,
    down_prior,
    first_prior,
    second_prior,
):
    chip = lax.axis_index("dp")
    core = lax.axis_index("narrow")
    parity = chip % 2
    kv_width = key_weight.shape[1]
    blocks = pack(
        (gate_weight.T, up_weight.T, down_weight),
        query_weight,
        out_weight,
        jnp.concatenate([key_weight, value_weight], axis=1),
        vectors,
        parity,
    )
    own_lengths = lax.dynamic_slice_in_dim(lengths, chip * 2 + core, 1, axis=1)[:, 0]
    block_output, input_grad, grads = layer(blocks, inputs[:, 0], cotangent[:, 0], own_lengths)
    units = grads[:3].reshape(3, 3, 16, D)
    thin = grads[3]

    def mine(which, size):
        if size == 7:
            return lax.dynamic_slice_in_dim(thin, 16 * which + parity * 7, 7, axis=0)
        last = lax.dynamic_slice_in_dim(units[2, which], parity * 6, 6, axis=0)
        return jnp.concatenate([units[0, which], units[1, which], last])

    own_narrow = mine(2, 7)
    grad_vector = own_narrow[0, 2 * kv_width : 2 * kv_width + 23]
    owned = (
        mine(0, 7),
        own_narrow[:, :kv_width],
        own_narrow[:, kv_width : 2 * kv_width],
        mine(1, 7),
        mine(0, 38),
        mine(1, 38),
        mine(2, 38),
    )
    priors = (
        query_prior,
        key_prior,
        value_prior,
        out_prior,
        gate_prior.T,
        up_prior.T,
        down_prior,
    )
    masters = (
        query_weight,
        key_weight,
        value_weight,
        out_weight,
        gate_weight,
        up_weight,
        down_weight,
    )
    shapes = ((D, D), (D, kv_width), (D, kv_width), (D, D), (D, FF), (D, FF), (FF, D))
    lefts = (False, False, False, False, True, True, False)
    momenta = tuple((MOMENTUM * priors[k] + owned[k] for k in range(7)))

    def padded(value, count):
        return jnp.pad(value, ((0, count - value.shape[0]), (0, D - value.shape[1])))

    tall, short = muon(
        half(jnp.stack([padded(momenta[k], 48) for k in (4, 5, 6)])),
        half(jnp.stack([padded(momenta[k], 16) for k in (0, 3, 1, 2)])),
    )
    finals = (
        short[0, :7], short[2, :7, :128], short[3, :7, :128], short[1, :7], tall[0, :38], tall[1, :38],
        tall[2, :38],
    )
    updated = []
    kept = []
    for k in range(7):
        current = finals[k].astype(jnp.float32)
        factor = MUON_RATE * 0.2 * math.sqrt(max(shapes[k][0], shapes[k][1]))
        if lefts[k]:
            current = current.T
        updated.append(masters[k] * (1.0 - MUON_RATE * MUON_DECAY) - factor * current)
        kept.append(momenta[k].T if lefts[k] else momenta[k])
    vector_first = BETA_FIRST * first_prior + (1.0 - BETA_FIRST) * grad_vector
    vector_second = BETA_SECOND * second_prior + (1.0 - BETA_SECOND) * grad_vector * grad_vector
    first_hat = vector_first / (1.0 - BETA_FIRST**STEP)
    second_hat = vector_second / (1.0 - BETA_SECOND**STEP)
    vector_new = vectors * (1.0 - ADAM_RATE * ADAM_DECAY) - ADAM_RATE * first_hat / (
        jnp.sqrt(second_hat) + ADAM_EPSILON
    )
    return (
        block_output,
        input_grad,
        *kept,
        *updated,
        vector_first,
        vector_second,
        vector_new,
    )


def solution(mesh):
    placed = (
        P(None, ("dp", "narrow"), None, None),
        P(None, ("dp", "narrow"), None, None),
        P(),
        P(("dp", "narrow"), None),
        P(("dp", "narrow"), None),
        P(("dp", "narrow"), None),
        P(("dp", "narrow"), None),
        P(None, ("dp", "narrow")),
        P(None, ("dp", "narrow")),
        P(("dp", "narrow"), None),
        P(("dp", "narrow")),
        P(("dp", "narrow"), None),
        P(("dp", "narrow"), None),
        P(("dp", "narrow"), None),
        P(("dp", "narrow"), None),
        P(None, ("dp", "narrow")),
        P(None, ("dp", "narrow")),
        P(("dp", "narrow"), None),
        P(("dp", "narrow")),
        P(("dp", "narrow")),
    )
    return jax.shard_map(
        body,
        mesh=mesh,
        in_specs=placed,
        out_specs=(
            P(None, ("dp", "narrow"), None, None),
            P(None, ("dp", "narrow"), None, None),
            P(("dp", "narrow"), None),
            P(("dp", "narrow"), None),
            P(("dp", "narrow"), None),
            P(("dp", "narrow"), None),
            P(None, ("dp", "narrow")),
            P(None, ("dp", "narrow")),
            P(("dp", "narrow"), None),
            P(("dp", "narrow"), None),
            P(("dp", "narrow"), None),
            P(("dp", "narrow"), None),
            P(("dp", "narrow"), None),
            P(None, ("dp", "narrow")),
            P(None, ("dp", "narrow")),
            P(("dp", "narrow"), None),
            P(("dp", "narrow")),
            P(("dp", "narrow")),
            P(("dp", "narrow")),
        ),
        check_vma=False,
    )
```

time: 1940 us -> 296 us (0.15)
  waiting for transfers between devices: 1090 us -> 0 us
  local copies, waits for them, and re-layouts: 368 us -> 8.96 us
  Pallas kernels: 0 us -> 263 us
  matrix products: 220 us -> 0 us
  blocking collectives: 174 us -> 0 us
  other arithmetic: 48.3 us -> 17.2 us
    reduce_scatter x2 -> x0, waiting for transfers between devices: 1020 us -> none  [the longest x1 682 us: body(): lax.psum_scatter(wide, axes, scatter_dimension=0).astype(jnp.float32)]
    pallas_call x0 -> x3, Pallas kernels: none -> 263 us  [the longest x1 114 us: layer(): pl.pallas_call(gather_kernel, out_shape=shapes(((TOKENS, D), F32), ((TOKE...]
    concatenate x3 -> x0, local copies, waits for them, and re-layouts: 233 us -> none  [the longest x1 226 us: body(): jnp.concatenate([half(grads[k]).reshape(count, -1, D) for k in (0, 3, 4,...]
    dot_general x68 -> x0, matrix products: 217 us -> none  [the longest x42 138 us: product(): return jnp.dot(left, right, preferred_element_type=jnp.float32)]
    unnamed x2 -> x0, blocking collectives: 135 us -> none
    reshape x20 -> x0, local copies, waits for them, and re-layouts: 95 us -> none  [the longest x5 43.4 us: body(): gathered[:, cuts[k]:cuts[k + 1]].reshape(count * (cuts[k + 1] - cuts[k]), D)]
    psum x1 -> x0, waiting for transfers between devices: 70.7 us -> none  [body(): lax.psum(jnp.stack([partial[k] for k in (0, 3, 4, 5, 6)]), axes)]
    all_gather x1 -> x0, blocking collectives: 39.8 us -> none  [body(): gathered_narrow = lax.all_gather(narrow, axes, axis=0)]
  transfers between devices with their start and end apart: 4 -> 0, of which waited for: 3 -> 0; matrix products, arithmetic and copies ran while one was open for 17% -> 0% of each run, Pallas kernels for 0% -> 0%
where the time goes in v4:
time: 296 us; the launch traced here: 291 us
  Pallas kernels  263 us (89%)
  other arithmetic  17.2 us (6%)
  local copies, waits for them, and re-layouts  8.96 us (3%)
    pallas_call x1, Pallas kernels, layer(): pl.pallas_call(gather_kernel, out_shape=shapes(((TOKENS, D), F32), ((TOKE...  114 us
    pallas_call x1, Pallas kernels, layer(): pl.pallas_call(scatter_kernel, out_shape=shapes(((TOKENS, D), BF16), ((4,...  91.2 us
    pallas_call x1, Pallas kernels, muon(): pl.pallas_call(muon_kernel, out_shape=(jax.ShapeDtypeStruct((3, 48, D), B...  58.1 us
    another operation x8, other arithmetic  6.06 us

profile of v4, /device:TPU:1, one launch (start us, length us, event | category | flops | bytes accessed | tf_op | source)
XLA Modules:
  0.0 290.5 jit_solution(2036430882289658359)
XLA Ops:
  0.7 0.0 copy-start
  0.7 0.8 slice.132
  1.4 0.8 slice.133
  2.2 0.8 slice.104
  3.0 0.8 fusion.5
  3.8 0.8 fusion.6
  4.7 0.7 select_maximum_fusion
  5.4 0.9 bitcast_convert_fusion.1
  6.3 0.9 bitcast_convert_fusion
  7.3 0.9 convert.74
  8.3 0.0 copy-start.6
  8.3 0.0 copy-start.7
  8.3 0.0 copy-done
  8.3 0.2 fusion.12
  8.5 0.1 broadcast_in_dim.10
  8.6 0.8 copy.41.len_ref
  9.4 0.1 iota_multiply_fusion
  9.5 0.1 fusion
  9.6 0.8 copy.42.cos_ref
  10.4 0.8 copy.43.sin_ref
  11.2 0.6 and_select_fusion.slot_ref
  11.8 113.8 %shard_map.339 = (f32[256,896]{1,0:T(8,128)}, bf16[256,896]{1,0:T(8,128)(2,1)}, bf16[256,1024]{1,0:T(8,128)(2,1)}, bf16[256,896]{1,0:T(8,128)(2,1)}, bf16[256,12...) custom-call(bf16[96,896]{1,0:T(8,128)(2,1)} %copy-done.6, ...), custom_call_target="tpu_custom_call" | custom-call | tf_op jit(solution)/shard_map/pallas_call | solution.py:849
  125.7 0.0 copy-start.13
  125.7 0.0 copy-start.14
  125.7 0.0 copy-start.17
  125.7 0.0 copy-start.18
  125.7 0.0 copy-start.8
  125.7 0.0 copy-start.9
  125.7 0.0 copy-start.10
  125.7 91.2 %shard_map.340 = (bf16[256,896]{1,0:T(8,128)(2,1)}, f32[4,48,896]{2,1,0:T(8,128)}) custom-call(bf16[4,4,2,2,96,896]{5,4,3,2,1,0:T(8,128)(2,1)} %get-tuple-element.38.grad_wide_ref, bf16[4,4,2,48,896]{4,3,2,1,0:T(8,128)(2,1)} %get-tuple-element.39.grad_shared_ref, bf16[256,896]{1,0:T(8,128)(2,1)} %bitcast.113, bf16[256,896]{1,0:T(8,128)(2,1)} %get-tuple-element.40.e_ref, ...), custom_call_target="tpu_custom_call" | custom-call | tf_op jit(solution)/shard_map/pallas_call | solution.py:894
  216.9 0.0 copy-start.11
  216.9 0.0 copy-start.12
  217.0 0.0 copy-start.15
  217.0 0.0 copy-start.16
  217.0 0.0 copy-start.2
  217.0 0.0 copy-start.3
  217.0 0.0 copy-start.1
  217.0 0.0 copy-start.19
  217.0 0.0 copy-start.20
  217.0 0.0 copy-start.21
  217.1 1.1 slice.105
  218.2 0.6 fusion.16
  218.9 0.0 copy-done.17
  218.9 0.0 copy-done.18
  218.9 0.6 fusion.18
  219.5 1.1 slice.108
  220.7 0.7 fusion.10
  221.4 0.7 fusion.8
  222.1 0.7 fusion.19
  222.8 0.7 pad_maximum_fusion.tall_ref
  223.6 0.7 pad_maximum_fusion.1.short_ref
  224.3 58.1 %shard_map.341 = (bf16[3,48,896]{2,1,0:T(8,128)(2,1)}, bf16[4,16,896]{2,1,0:T(8,128)(2,1)}) custom-call(bf16[3,48,896]{2,1,0:T(8,128)(2,1)} %pad_maximum_fusion.tall_ref, bf16[4,16,896]{2,1,0:T(8,128)(2,1)} %pad_maximum_fusion.1.short_ref), custom_call_target="tpu_custom_call" | custom-call | tf_op jit(solution)/shard_map/pallas_call | solution.py:1116
  282.3 1.4 bitcast_subtract_fusion.3
  283.7 0.0 copy-done.15
  283.7 1.3 bitcast_subtract_fusion.5
  285.0 0.0 copy-done.3
  285.0 1.7 bitcast_subtract_fusion
  286.7 1.6 bitcast_subtract_fusion.2
  288.2 0.0 copy-done.19
  288.2 0.0 copy-done.21
  288.2 0.5 divide_subtract_fusion
  288.8 0.8 copy.66
  289.6 0.0 copy-done.5
  289.6 0.8 copy.67
  (42 shorter events, 0.4 us)
Async XLA Ops:
  0.7 7.7 %copy-start = (s32[2,128]{1,0:T(2,128)S(1)}, s32[2,128]{1,0:T(2,128)}, u32[]{:S(2)}) copy-start(s32[2,128]{1,0:T(2,128)} %param.22) | copy-start | bytes 3076
  8.3 3.5 %copy-start.6 = (bf16[96,896]{1,0:T(8,128)(2,1)}, bf16[96,896]{1,0:T(8,128)(2,1)S(1)}, u32[]{:S(2)}) copy-start(bf16[96,896]{1,0:T(8,128)(2,1)S(1)} %get-tuple-element.132.wide_ref) | copy-start | bytes 516100
  8.3 3.5 %copy-start.7 = (bf16[96,896]{1,0:T(8,128)(2,1)}, bf16[96,896]{1,0:T(8,128)(2,1)S(1)}, u32[]{:S(2)}) copy-start(bf16[96,896]{1,0:T(8,128)(2,1)S(1)} %get-tuple-element.131.tail_ref) | copy-start | bytes 516100
  125.7 92.5 %copy-start.13 = (f32[7,896]{1,0:T(8,128)S(1)}, f32[7,896]{1,0:T(8,128)}, u32[]{:S(2)}) copy-start(f32[7,896]{1,0:T(8,128)} %param.34) | copy-start | bytes 75268
  125.7 92.5 %copy-start.14 = (f32[7,896]{1,0:T(8,128)S(1)}, f32[7,896]{1,0:T(8,128)}, u32[]{:S(2)}) copy-start(f32[7,896]{1,0:T(8,128)} %param.31) | copy-start | bytes 75268
  125.7 93.2 %copy-start.17 = (f32[7,128]{1,0:T(8,128)S(1)}, f32[7,128]{1,0:T(8,128)}, u32[]{:S(2)}) copy-start(f32[7,128]{1,0:T(8,128)} %param.33) | copy-start | bytes 10756
  125.7 93.2 %copy-start.18 = (f32[7,128]{1,0:T(8,128)S(1)}, f32[7,128]{1,0:T(8,128)}, u32[]{:S(2)}) copy-start(f32[7,128]{1,0:T(8,128)} %param.32) | copy-start | bytes 10756
  125.7 94.9 %copy-start.8 = (f32[896,38]{0,1:T(8,128)S(1)}, f32[896,38]{0,1:T(8,128)}, u32[]{:S(2)}) copy-start(f32[896,38]{0,1:T(8,128)} %param.35) | copy-start | bytes 408580
  125.7 95.6 %copy-start.9 = (f32[896,38]{0,1:T(8,128)S(1)}, f32[896,38]{0,1:T(8,128)}, u32[]{:S(2)}) copy-start(f32[896,38]{0,1:T(8,128)} %param.36) | copy-start | bytes 408580
  125.7 96.3 %copy-start.10 = (f32[38,896]{1,0:T(8,128)S(1)}, f32[38,896]{1,0:T(8,128)}, u32[]{:S(2)}) copy-start(f32[38,896]{1,0:T(8,128)} %param.37) | copy-start | bytes 408580
  216.9 65.4 %copy-start.11 = (f32[7,896]{1,0:T(8,128)S(1)}, f32[7,896]{1,0:T(8,128)}, u32[]{:S(2)}) copy-start(f32[7,896]{1,0:T(8,128)} %param.23) | copy-start | bytes 75268
  216.9 65.4 %copy-start.12 = (f32[7,896]{1,0:T(8,128)S(1)}, f32[7,896]{1,0:T(8,128)}, u32[]{:S(2)}) copy-start(f32[7,896]{1,0:T(8,128)} %param.26) | copy-start | bytes 75268
  217.0 66.8 %copy-start.15 = (f32[7,128]{1,0:T(8,128)S(1)}, f32[7,128]{1,0:T(8,128)}, u32[]{:S(2)}) copy-start(f32[7,128]{1,0:T(8,128)} %param.25) | copy-start | bytes 10756
  217.0 66.7 %copy-start.16 = (f32[7,128]{1,0:T(8,128)S(1)}, f32[7,128]{1,0:T(8,128)}, u32[]{:S(2)}) copy-start(f32[7,128]{1,0:T(8,128)} %param.24) | copy-start | bytes 10756
  217.0 68.0 %copy-start.2 = (f32[896,38]{0,1:T(8,128)S(1)}, f32[896,38]{0,1:T(8,128)}, u32[]{:S(2)}) copy-start(f32[896,38]{0,1:T(8,128)} %param.27) | copy-start | bytes 408580
  217.0 68.0 %copy-start.3 = (f32[896,38]{0,1:T(8,128)S(1)}, f32[896,38]{0,1:T(8,128)}, u32[]{:S(2)}) copy-start(f32[896,38]{0,1:T(8,128)} %param.28) | copy-start | bytes 408580
  217.0 69.7 %copy-start.1 = (f32[38,896]{1,0:T(8,128)S(1)}, f32[38,896]{1,0:T(8,128)}, u32[]{:S(2)}) copy-start(f32[38,896]{1,0:T(8,128)} %param.29) | copy-start | bytes 408580
  217.0 71.2 %copy-start.19 = (f32[23]{0:T(128)S(1)}, f32[23]{0:T(128)}, u32[]{:S(2)}) copy-start(f32[23]{0:T(128)} %param.30) | copy-start | bytes 280
  217.0 71.2 %copy-start.20 = (f32[23]{0:T(128)S(1)}, f32[23]{0:T(128)}, u32[]{:S(2)}) copy-start(f32[23]{0:T(128)} %param.39) | copy-start | bytes 280
  217.0 71.2 %copy-start.21 = (f32[23]{0:T(128)S(1)}, f32[23]{0:T(128)}, u32[]{:S(2)}) copy-start(f32[23]{0:T(128)} %param.38) | copy-start | bytes 280
  217.1 71.7 %copy-start.4 = (bf16[256,896]{1,0:T(8,128)(2,1)S(1)}, bf16[256,896]{1,0:T(8,128)(2,1)}, u32[]{:S(2)}) copy-start(bf16[256,896]{1,0:T(8,128)(2,1)} %get-tuple-element.37) | copy-start | bytes 1376260
  217.1 72.5 %copy-start.5 = (bf16[256,896]{1,0:T(8,128)(2,1)S(1)}, bf16[256,896]{1,0:T(8,128)(2,1)}, u32[]{:S(2)}) copy-start(bf16[256,896]{1,0:T(8,128)(2,1)} %get-tuple-element.51) | copy-start | bytes 1376260

commit v5 on v4

--- a/solution.py
+++ b/solution.py
@@ -2,6 +2,7 @@
 
 import jax
 import jax.numpy as jnp
+import numpy as np
 from jax import lax
 from jax.experimental import pallas as pl
 from jax.experimental.pallas import tpu as pltpu
@@ -45,14 +46,6 @@
     return lax.dot_general(
         left, right, (((1,), (1,)), ((), ())), preferred_element_type=jnp.float32
     )
-
-
-def rotary_tables(length):
-    half = HEAD // 2
-    freqs = ROPE_BASE ** (-jnp.arange(half, dtype=jnp.float32) * 2.0 / HEAD)
-    angles = jnp.arange(length, dtype=jnp.float32)[:, None] * freqs[None, :]
-    angles = jnp.concatenate([angles, angles], axis=-1)
-    return (jnp.cos(angles), jnp.sin(angles))
 
 
 def norm_back(grad, normed, scale):
@@ -103,12 +96,12 @@
 def greet(coords, core):
     barrier = pltpu.get_barrier_semaphore()
     for axis in range(3):
-        for by in (1, 3):
+        for by in (1, 2, 3):
             pl.semaphore_signal(
                 barrier, inc=1, device_id=device_of(shifted(coords, axis, by), core), device_id_type=MESH
             )
     pl.semaphore_signal(barrier, inc=1, device_id=device_of(coords, 1 - core), device_id_type=MESH)
-    pl.semaphore_wait(barrier, 7)
+    pl.semaphore_wait(barrier, 10)
 
 
 def remote(src, dst, send_sem, recv_sem, device):
@@ -153,9 +146,18 @@
 
 
 class Plan:
-    def __init__(self, part, coords, axis, spec, split):
+    def __init__(self, part, stage, coords, axis, spec, split):
         self.coords, self.axis, self.spec, self.split = coords, axis, spec, split
         self.exchange = PARTS[part][4] and axis == 2
+        self.direct = not self.exchange and stage == 0
+
+    def whole(self, by):
+        spec = list(self.spec)
+        spec[self.axis] = (self.coords[self.axis] + by) % 4
+        return (tuple(spec), None)
+
+    def at(self, by):
+        return shifted(self.coords, self.axis, by)
 
     def pieces(self, by):
         spec = list(self.spec)
@@ -172,7 +174,7 @@
 def plan_of(part, stage, coords):
     order = PARTS[part][3]
     spec = tuple(FULL if k in order[:stage] else coords[k] for k in range(3))
-    return Plan(part, coords, order[stage], spec, order[stage - 1] if stage else None)
+    return Plan(part, stage, coords, order[stage], spec, order[stage - 1] if stage else None)
 
 
 class Gather:
@@ -197,6 +199,10 @@
             plan = plan_of(part, phase, self.coords)
             if plan.exchange:
                 self.send(part, phase, 0, plan.own(), facing(self.coords))
+                continue
+            if plan.direct:
+                for by in (1, 3, 2):
+                    self.send(part, phase, by, plan.own(), plan.at(by))
                 continue
             right, left = self.neighbours(plan)
             first, second = plan.pieces(0)
@@ -208,7 +214,7 @@
     def forward(self, parts, phase):
         for part in parts:
             plan = plan_of(part, phase, self.coords)
-            if plan.exchange:
+            if plan.exchange or plan.direct:
                 continue
             right, left = self.neighbours(plan)
             piece = plan.pieces(3)[0]
@@ -224,6 +230,10 @@
             if plan.exchange:
                 self.copy(part, phase, 0, plan.facing(), facing(self.coords)).wait_recv()
                 continue
+            if plan.direct:
+                for by in (1, 3):
+                    self.copy(part, phase, by, plan.whole(4 - by), plan.at(by)).wait_recv()
+                continue
             right, left = self.neighbours(plan)
             self.copy(part, phase, 2, plan.pieces(3)[1], right).wait_recv()
             self.copy(part, phase, 3, plan.pieces(1)[0], left).wait_recv()
@@ -232,6 +242,9 @@
         for part in parts:
             plan = plan_of(part, phase, self.coords)
             if plan.exchange:
+                continue
+            if plan.direct:
+                self.copy(part, phase, 2, plan.whole(2), plan.at(2)).wait_recv()
                 continue
             right, left = self.neighbours(plan)
             self.copy(part, phase, 4, plan.pieces(2)[0], right).wait_recv()
@@ -248,6 +261,10 @@
                 if plan.exchange:
                     self.copy(part, phase, 0, plan.own(), facing(self.coords)).wait_send()
                     continue
+                if plan.direct:
+                    for by in (1, 3, 2):
+                        self.copy(part, phase, by, plan.own(), plan.at(by)).wait_send()
+                    continue
                 right, _ = self.neighbours(plan)
                 for slot, which in enumerate((0, 1, 1, 0, 0, 1)):
                     self.copy(part, phase, slot, plan.pieces(0)[which], right).wait_send()
@@ -272,8 +289,8 @@
 
 
 class Scatter:
-    def __init__(self, arrays, coords, core, buffers, send_sems, recv_sems):
-        self.arrays, self.coords, self.core = arrays, coords, core
+    def __init__(self, arrays, coords, core, buffers, send_sems, recv_sems, done):
+        self.arrays, self.coords, self.core, self.done = arrays, coords, core, done
         self.buffers, self.send_sems, self.recv_sems = buffers, send_sems, recv_sems
 
     def copy(self, part, phase, slot, piece, coords):
@@ -283,10 +300,12 @@
         return remote(ref, self.buffers[part, phase][slot], *sems, device_of(coords, self.core))
 
     def send(self, *args):
-        self.copy(*args).start()
+        if args[:3] not in self.done:
+            self.copy(*args).start()
 
     def arrive(self, *args):
-        self.copy(*args).wait_recv()
+        if args[:3] not in self.done:
+            self.copy(*args).wait_recv()
 
     def add(self, part, phase, piece, *slots):
         sources = [self.buffers[part, phase][slot] for slot in slots]
@@ -315,7 +334,7 @@
     def start_far(self, parts, phase):
         for part in parts:
             plan = plan_of(part, phase, self.coords)
-            if plan.exchange:
+            if plan.exchange or plan.direct:
                 continue
             right, left = self.neighbours(plan)
             self.send(part, phase, 0, plan.pieces(2)[0], right)
@@ -327,6 +346,10 @@
             if plan.exchange:
                 self.send(part, phase, 0, plan.facing(), facing(self.coords))
                 continue
+            if plan.direct:
+                for by in (1, 3, 2):
+                    self.send(part, phase, by, plan.whole(by), plan.at(by))
+                continue
             right, left = self.neighbours(plan)
             self.send(part, phase, 2, plan.pieces(1)[1], right)
             self.send(part, phase, 3, plan.pieces(3)[0], left)
@@ -338,7 +361,7 @@
     def forward(self, parts, phase):
         for part in parts:
             plan = plan_of(part, phase, self.coords)
-            if plan.exchange:
+            if plan.exchange or plan.direct:
                 continue
             right, left = self.neighbours(plan)
             self.arrive(part, phase, 0, plan.pieces(2)[0], right)
@@ -355,6 +378,11 @@
                 self.arrive(part, phase, 0, plan.facing(), facing(self.coords))
                 self.add(part, phase, plan.own(), 0)
                 continue
+            if plan.direct:
+                for by in (1, 3, 2):
+                    self.arrive(part, phase, by, plan.whole(by), plan.at(by))
+                self.add(part, phase, plan.own(), 1, 3, 2)
+                continue
             right, left = self.neighbours(plan)
             self.arrive(part, phase, 3, plan.pieces(3)[0], left)
             self.arrive(part, phase, 4, plan.pieces(1)[0], right)
@@ -370,9 +398,18 @@
                 if plan.exchange:
                     self.copy(part, phase, 0, plan.own(), facing(self.coords)).wait_send()
                     continue
+                if plan.direct:
+                    for by in (1, 3, 2):
+                        self.copy(part, phase, by, plan.whole(by), plan.at(by)).wait_send()
+                    continue
                 right, _ = self.neighbours(plan)
                 for slot, which in enumerate((0, 1, 1, 0, 0, 1)):
+                    if (part, phase, slot) in self.done:
+                        continue
                     self.copy(part, phase, slot, plan.pieces(0)[which], right).wait_send()
+
+
+EARLY = tuple((part, 2, slot) for part in WIDE for slot in (2, 3))
 
 
 def scatter_buffer_shapes():
@@ -382,6 +419,8 @@
             plan = plan_of(part, phase, (0, 0, 0))
             if plan.exchange:
                 shapes = [shape_of(part, plan.own())]
+            elif plan.direct:
+                shapes = [None] + [shape_of(part, plan.own())] * 3
             else:
                 first, second = (shape_of(part, piece) for piece in plan.pieces(0))
                 shapes = [first, second, second, first, first, second]
@@ -485,7 +524,8 @@
     rows = []
     for b in range(2):
         here = slice(128 * b, 128 * b + 128)
-        allowed = causal & (other < len_ref[here, :])
+        length = len_ref[b : b + 1, :]
+        allowed = causal & (other < jnp.concatenate([length, length], axis=1))
         key_tiles = paired(keys[here])
         value_tiles = paired(values[here])
         tiles = []
@@ -528,18 +568,55 @@
     return [half(grad).reshape(*lead, 16, D) for grad in grads]
 
 
+KEPT = 17
+
+
 def gather_kernel(
-    wide_ref, tail_ref, x_ref, cot_ref, len_ref, cos_ref, sin_ref, slot_ref,
-    middle_ref, e_ref, h1p_ref, q_ref, k_ref, v_ref, mixed_ref, probs_ref, vector_ref,
-    output_ref, dh2_ref, grad_wide_ref, grad_shared_ref, rest_ref,
-    wide, shared, rest, stage0, stage1, stage2, h_all, e_all, out_acc, back_acc, parcel, arrived, tail,
-    local_sems, send_sems, recv_sems, twin_sems, store_sems,
+    gate_ref, up_ref, down_ref, query_ref, out_ref, narrow_ref,
+    x_ref, cot_ref, len_ref, cos_ref, sin_ref, slot_ref, *refs,
 ):
     coords, core = my_coords()
     z, y, x = coords
     pair, odd = x // 2, x % 2
-    load = pltpu.make_async_copy(wide_ref, wide.at[z, y, pair, odd], local_sems.at[0])
-    load.start()
+    results, (grad_wide_ref, grad_shared_ref, rest_ref) = refs[:KEPT], refs[KEPT : KEPT + 3]
+    held = refs[KEPT + 3 : 2 * KEPT + 3]
+    (
+        wide, shared, rest, stage0, stage1, stage2, h_all, e_all, out_acc, back_acc, parcel, arrived,
+        tail, tail_own, tail_wide,
+        local_sems, send_sems, recv_sems, twin_sems, store_sems, early_sems, kept_sems,
+    ) = refs[2 * KEPT + 3 :]
+    (
+        middle_ref, e_ref, h1p_ref, q_ref, k_ref, v_ref, mixed_ref, probs_ref, vector_ref,
+        output_ref, dh2_ref,
+    ) = held[:11]
+    early = held[11:]
+
+    def keep(first, last):
+        return [
+            pltpu.make_async_copy(held[n], results[n], kept_sems.at[n]) for n in range(first, last)
+        ]
+
+    units = (gate_ref, up_ref, down_ref)
+    for n, ref in enumerate(units):
+        for k in range(2):
+            wide[z, y, pair, odd, CHUNK * k + 16 * n : CHUNK * k + 16 * n + 16] = half(
+                ref[16 * k : 16 * k + 16]
+            )
+    tail_wide[...] = jnp.zeros_like(tail_wide)
+    for parity in range(2):
+
+        @pl.when(odd == parity)
+        def _():
+            for n, ref in enumerate(units):
+                start = 16 * n + 6 * parity
+                tail_wide[start : start + 6] = ref[32:38]
+            for n, ref in enumerate((query_ref, out_ref)):
+                start = CHUNK + 16 * n + 7 * parity
+                tail_wide[start : start + 7] = ref[...]
+            start = CHUNK + 32 + 7 * parity
+            tail_wide[start : start + 7, 0:384] = narrow_ref[...]
+
+    tail_own[...] = half(tail_wide[...])
     greet(coords, core)
     twin = device_of(coords, 1 - core)
 
@@ -548,18 +625,17 @@
 
     gather = Gather(((wide, ()), (shared, ()), (rest, (core,))), coords, core, send_sems, recv_sems)
     partner = device_of((z, y, x + 1 - 2 * odd), core)
-    tail_copy = remote(tail_ref, tail, twin_sems.at[0, 4], twin_sems.at[1, 4], partner)
+    tail_copy = remote(tail_own, tail, twin_sems.at[0, 4], twin_sems.at[1, 4], partner)
     tail_copy.start()
-    load.wait()
     gather.start((0, 1), 0)
-    token = lax.broadcasted_iota(jnp.int32, (TOKENS, 1), 0) & 127
-    live = (token < len_ref[...]).astype(F32)
+    token = lax.broadcasted_iota(jnp.int32, (128, 1), 0)
+    live = jnp.concatenate([(token < len_ref[b : b + 1, 0:1]).astype(F32) for b in range(2)])
     e_ref[...] = half(cot_ref[...].astype(F32) * live)
     e_all[core] = e_ref[...]
     e_copy = to_twin(e_ref, e_all.at[core], 0)
     e_copy.start()
     tail_copy.wait()
-    both = half(tail_ref[...].astype(F32) + tail[...].astype(F32))
+    both = half(tail_wide[...] + tail[...].astype(F32))
     shared[z, y, pair] = both[:CHUNK]
     rest[core, z, y, pair] = both[CHUNK:]
     gather.start(THIN, 0)
@@ -589,11 +665,26 @@
     )
     h_copy = to_twin(h_all.at[core], h_all.at[core], 2)
     h_copy.start()
+    for copy in keep(0, 9):
+        copy.start()
     out_acc[...] = jnp.zeros_like(out_acc)
     back_acc[...] = jnp.zeros_like(back_acc)
     e_copy.wait()
     h_copy.wait()
     stages = (stage0, stage1, stage2)
+
+    def early_copy(t, slot):
+        axis = PARTS[t][3][2]
+        which = 3 - slot
+        place = [slice(None)] * (len(stages[t].shape) - 1)
+        place[1 if t == 2 else 0] = pl.ds(which, 1) if t == 2 else pl.ds(2 * which, 2)
+        return remote(
+            stages[t].at[(slot - 1) % 2].at[tuple(place)],
+            early[2 * t + slot - 2],
+            early_sems.at[0, t, slot - 2],
+            early_sems.at[1, t, slot - 2],
+            device_of(shifted(coords, axis, 1 if slot == 2 else 3), core),
+        )
 
     def tile_places(j):
         return (
@@ -619,16 +710,28 @@
             source, target, index = tile_places(j)[t]
             grads = mlp_tile(source[(*index, slice(None))], h, e, out_acc, back_acc)
             copy = pltpu.make_async_copy(
-                stages[t], target.at[(*index, slice(None))], store_sems.at[t]
+                stages[t].at[k % 2], target.at[(*index, slice(None))], store_sems.at[t, k % 2]
             )
 
-            @pl.when(k > 0)
+            @pl.when(k > 1)
             def _():
                 copy.wait()
 
+            @pl.when(k == 3)
+            def _():
+                early_copy(t, 2).wait_send()
+
             for place, grad in enumerate(grads):
-                stages[t][..., 16 * place : 16 * place + 16, :] = grad
+                stages[t][k % 2, ..., 16 * place : 16 * place + 16, :] = grad
             copy.start()
+
+            @pl.when(k == 1)
+            def _():
+                early_copy(t, 2).start()
+
+            @pl.when(k == 2)
+            def _():
+                early_copy(t, 3).start()
 
         @pl.when(k == 0)
         def _():
@@ -646,12 +749,22 @@
         (middle_ref[...] + (out_acc[core] + arrived[0].astype(F32))) * live
     )
     dh2_ref[...] = back_acc[core] + arrived[1].astype(F32)
+    for copy in keep(9, 11):
+        copy.start()
     for t in range(3):
         _, target, index = tile_places(0)[t]
-        pltpu.make_async_copy(
-            stages[t], target.at[(*index, slice(None))], store_sems.at[t]
-        ).wait()
+        for which in range(2):
+            pltpu.make_async_copy(
+                stages[t].at[which], target.at[(*index, slice(None))], store_sems.at[t, which]
+            ).wait()
+        early_copy(t, 3).wait_send()
+        early_copy(t, 2).wait_recv()
+        early_copy(t, 3).wait_recv()
+        for copy in keep(11 + 2 * t, 13 + 2 * t):
+            copy.start()
     rest_store.wait()
+    for copy in keep(0, KEPT):
+        copy.wait()
     gather.drain()
 
 
@@ -680,8 +793,6 @@
     low = low_lanes((128, 128))
     query_rows, key_rows, value_rows = [], [], []
     for b in range(2):
-        if b == 1:
-            between()
         here = slice(128 * b, 128 * b + 128)
         key_tiles = paired(k_ref[here, :].astype(jnp.float32))
         value_tiles = paired(v_ref[here, :].astype(jnp.float32))
@@ -712,6 +823,7 @@
             )
         key_rows.append(joined[0] * SCALE)
         value_rows.append(joined[1])
+    between()
     grad_query = half(rotated_back(jnp.concatenate(query_rows), cosine, sine))
     grad_key = half(rotated_back(jnp.concatenate(key_rows), cosine, sine))
     grad_narrow = jnp.concatenate([grad_key, half(jnp.concatenate(value_rows))], axis=1)
@@ -742,21 +854,43 @@
     grad_ref[:, :, :, :, 32:48, 384:] = jnp.zeros((2, 4, 4, 2, 16, D - 384), jnp.bfloat16)
 
 
+LOADED = ("x", "e", "rest", "middle", "h1p", "q", "k", "v", "mixed", "probs", "vector", "dh2")
+
+
 def scatter_kernel(
-    grad_wide_ref, grad_shared_ref, x_ref, e_ref, rest_ref, cos_ref, sin_ref, slot_ref,
-    middle_ref, h1p_ref, q_ref, k_ref, v_ref, mixed_ref, probs_ref, vector_ref, dh2_ref,
-    input_grad_ref, out_ref,
-    wide, shared, thin, joined, mine, theirs, load_sems, send_sems, recv_sems, twin_sems, pair_sems,
-    *buffers,
+    cos_ref, sin_ref, slot_ref, grad_wide_ref, grad_shared_ref, *refs,
 ):
     coords, core = my_coords()
     z, y, x = coords
     pair, odd = x // 2, x % 2
+    count = len(LOADED) + len(EARLY)
+    sources, (input_grad_ref, out_ref) = refs[:count], refs[count : count + 2]
+    held = refs[count + 2 : 2 * count + 2]
+    (
+        wide, shared, thin, joined, mine, theirs,
+        load_sems, send_sems, recv_sems, twin_sems, pair_sems, held_sems,
+    ) = refs[2 * count + 2 : 2 * count + 14]
+    buffers = refs[2 * count + 14 :]
+    (
+        x_ref, e_ref, rest_ref, middle_ref, h1p_ref, q_ref, k_ref, v_ref, mixed_ref, probs_ref,
+        vector_ref, dh2_ref,
+    ) = held[: len(LOADED)]
+    fetches = [
+        pltpu.make_async_copy(sources[n], held[n], held_sems.at[n]) for n in range(count)
+    ]
     named, position = {}, 0
+    early = dict(zip(EARLY, held[len(LOADED) :]))
     for key, shapes in scatter_buffer_shapes():
-        named[key] = buffers[position : position + len(shapes)]
-        position += len(shapes)
-    scatter = Scatter(((wide, ()), (shared, ()), (thin, (core,))), coords, core, named, send_sems, recv_sems)
+        named[key] = []
+        for slot in range(len(shapes)):
+            if (*key, slot) in early:
+                named[key].append(early[(*key, slot)])
+            elif shapes[slot] is None:
+                named[key].append(None)
+            else:
+                named[key].append(buffers[position])
+                position += 1
+    scatter = Scatter(((wide, ()), (shared, ()), (thin, (core,))), coords, core, named, send_sems, recv_sems, EARLY)
 
     def load(part, by):
         spec = [FULL] * 3
@@ -770,6 +904,8 @@
     for by in (2, 1, 3, 0):
         for part in WIDE:
             load(part, by).start()
+    for copy in fetches:
+        copy.start()
     greet(coords, core)
 
     for part in WIDE:
@@ -778,11 +914,12 @@
     for part in WIDE:
         load(part, 1).wait()
         load(part, 3).wait()
-        scatter.start_near((part,), 2)
 
     def between():
         scatter.forward(WIDE, 2)
 
+    for copy in fetches:
+        copy.wait()
     attention_backward(
         between, x_ref, e_ref, rest_ref, cos_ref, sin_ref, slot_ref,
         middle_ref, h1p_ref, q_ref, k_ref, v_ref, mixed_ref, probs_ref, vector_ref, dh2_ref,
@@ -831,109 +968,121 @@
     scatter.drain()
 
 
-def layer(blocks, tokens, cotangent, lengths):
+def layer(weights, tokens, cotangent, lengths):
     vmem = pl.BlockSpec(memory_space=pltpu.VMEM)
     anywhere = pl.BlockSpec(memory_space=pl.ANY)
     x = tokens.reshape(TOKENS, D)
-    rows = jnp.repeat(lengths, 128)[:, None]
-    cosine, sine = rotary_tables(128)
+    freqs = ROPE_BASE ** (-np.arange(HEAD // 2) * 2.0 / HEAD)
+    angles = np.tile(np.arange(128)[:, None] * freqs[None, :], (2, 4))
     tables = (
-        jnp.tile(cosine, (2, 2)),
-        jnp.tile(sine, (2, 2)),
-        (jnp.arange(2944, dtype=jnp.int32) % 23)[None],
-    )
-
-    def shapes(*pairs):
+        np.cos(angles).astype(np.float32),
+        np.sin(angles).astype(np.float32),
+        (np.arange(2944, dtype=np.int32) % 23)[None],
+    )
+    buffers = dict(scatter_buffer_shapes())
+    kept = [
+        ((TOKENS, D), F32),
+        ((TOKENS, D), BF16),
+        ((TOKENS, 1024), BF16),
+        ((TOKENS, D), BF16),
+        ((TOKENS, 128), BF16),
+        ((TOKENS, 128), BF16),
+        ((TOKENS, 1024), BF16),
+        ((2, 7, 128, 256), F32),
+        ((1, 2944), F32),
+        ((TOKENS, D), BF16),
+        ((TOKENS, D), F32),
+    ] + [(buffers[part, stage][slot], BF16) for part, stage, slot in EARLY]
+    large = [
+        ((4, 4, 2, 2, 2 * CHUNK, D), BF16),
+        ((4, 4, 2, CHUNK, D), BF16),
+        ((2, 4, 4, 2, CHUNK, D), BF16),
+    ]
+
+    def shapes(pairs):
         return [jax.ShapeDtypeStruct(shape, dtype) for shape, dtype in pairs]
 
-    kept = pl.pallas_call(
+    def scratch(pairs):
+        return [pltpu.VMEM(shape, dtype) for shape, dtype in pairs]
+
+    results = pl.pallas_call(
         gather_kernel,
-        out_shape=shapes(
-            ((TOKENS, D), F32),
-            ((TOKENS, D), BF16),
-            ((TOKENS, 1024), BF16),
-            ((TOKENS, D), BF16),
-            ((TOKENS, 128), BF16),
-            ((TOKENS, 128), BF16),
-            ((TOKENS, 1024), BF16),
-            ((2, 7, 128, 256), F32),
-            ((1, 2944), F32),
-            ((TOKENS, D), BF16),
-            ((TOKENS, D), F32),
-            ((4, 4, 2, 2, 2 * CHUNK, D), BF16),
-            ((4, 4, 2, CHUNK, D), BF16),
-            ((2, 4, 4, 2, CHUNK, D), BF16),
-        ),
-        in_specs=[anywhere] + [vmem] * 7,
-        out_specs=[vmem] * 11 + [anywhere] * 3,
-        scratch_shapes=[
-            pltpu.VMEM((4, 4, 2, 2, 2 * CHUNK, D), BF16),
-            pltpu.VMEM((4, 4, 2, CHUNK, D), BF16),
-            pltpu.VMEM((2, 4, 4, 2, CHUNK, D), BF16),
-            pltpu.VMEM((4, 2, 2, CHUNK, D), BF16),
-            pltpu.VMEM((4, 4, CHUNK, D), BF16),
-            pltpu.VMEM((4, 2, CHUNK, D), BF16),
-            pltpu.VMEM((2, TOKENS, D), BF16),
-            pltpu.VMEM((2, TOKENS, D), BF16),
-            pltpu.VMEM((2, TOKENS, D), F32),
-            pltpu.VMEM((2, TOKENS, D), F32),
-            pltpu.VMEM((2, TOKENS, D), BF16),
-            pltpu.VMEM((2, TOKENS, D), BF16),
-            pltpu.VMEM((2 * CHUNK, D), BF16),
+        out_shape=shapes(kept + large),
+        in_specs=[vmem] * 12,
+        out_specs=[anywhere] * (KEPT + 3),
+        scratch_shapes=scratch(
+            kept
+            + large
+            + [
+                ((2, 4, 2, 2, CHUNK, D), BF16),
+                ((2, 4, 4, CHUNK, D), BF16),
+                ((2, 4, 2, CHUNK, D), BF16),
+                ((2, TOKENS, D), BF16),
+                ((2, TOKENS, D), BF16),
+                ((2, TOKENS, D), F32),
+                ((2, TOKENS, D), F32),
+                ((2, TOKENS, D), BF16),
+                ((2, TOKENS, D), BF16),
+                ((2 * CHUNK, D), BF16),
+                ((2 * CHUNK, D), BF16),
+                ((2 * CHUNK, D), F32),
+            ]
+        )
+        + [
             pltpu.SemaphoreType.DMA((3,)),
             pltpu.SemaphoreType.DMA((6, 3, 6)),
             pltpu.SemaphoreType.DMA((6, 3, 6)),
             pltpu.SemaphoreType.DMA((2, 5)),
-            pltpu.SemaphoreType.DMA((3,)),
+            pltpu.SemaphoreType.DMA((3, 2)),
+            pltpu.SemaphoreType.DMA((2, 3, 2)),
+            pltpu.SemaphoreType.DMA((KEPT,)),
         ],
         compiler_params=pltpu.CompilerParams(
-            collective_id=0, has_side_effects=True, vmem_limit_bytes=60 * 2**20
+            collective_id=0, has_side_effects=True, vmem_limit_bytes=61 * 2**20
         ),
-    )(*blocks, x, cotangent.reshape(TOKENS, D), rows, *tables)
-    (middle, e, h1p, q, k, v, mixed, probs, vector, output, dh2, grad_wide, grad_shared, rest) = kept
+    )(*weights, x, cotangent.reshape(TOKENS, D), lengths, *tables)
+    middle, e, h1p, q, k, v, mixed, probs, vector, output, dh2 = results[:11]
+    early = results[11:KEPT]
+    grad_wide, grad_shared, rest = results[KEPT:]
+    loaded = dict(
+        x=x, e=e, rest=rest, middle=middle, h1p=h1p, q=q, k=k, v=v, mixed=mixed, probs=probs,
+        vector=vector, dh2=dh2,
+    )
+    fetched = [loaded[name] for name in LOADED] + list(early)
     input_grad, grads = pl.pallas_call(
         scatter_kernel,
-        out_shape=shapes(((TOKENS, D), BF16), ((4, CHUNK, D), F32)),
-        in_specs=[anywhere] * 2 + [vmem] * 15,
+        out_shape=shapes([((TOKENS, D), BF16), ((4, CHUNK, D), F32)]),
+        in_specs=[vmem] * 3 + [anywhere] * (2 + len(fetched)),
         out_specs=[vmem] * 2,
-        scratch_shapes=[
-            pltpu.VMEM((4, 4, 2, 2, 2 * CHUNK, D), BF16),
-            pltpu.VMEM((4, 4, 2, CHUNK, D), BF16),
-            pltpu.VMEM((2, 4, 4, 2, CHUNK, D), BF16),
-            pltpu.VMEM((4, 4, 2, CHUNK, D), BF16),
-            pltpu.VMEM((2, CHUNK, D), BF16),
-            pltpu.VMEM((2, CHUNK, D), BF16),
+        scratch_shapes=scratch(
+            [(value.shape, value.dtype) for value in fetched]
+            + large[:2]
+            + [
+                ((2, 4, 4, 2, CHUNK, D), BF16),
+                ((4, 4, 2, CHUNK, D), BF16),
+                ((2, CHUNK, D), BF16),
+                ((2, CHUNK, D), BF16),
+            ]
+        )
+        + [
             pltpu.SemaphoreType.DMA((3, 4)),
             pltpu.SemaphoreType.DMA((6, 3, 6)),
             pltpu.SemaphoreType.DMA((6, 3, 6)),
             pltpu.SemaphoreType.DMA((2,)),
             pltpu.SemaphoreType.DMA((2,)),
+            pltpu.SemaphoreType.DMA((len(fetched),)),
         ]
-        + [pltpu.VMEM(shape, BF16) for _, group in scatter_buffer_shapes() for shape in group],
+        + [
+            pltpu.VMEM(shape, BF16)
+            for key, group in buffers.items()
+            for slot, shape in enumerate(group)
+            if shape is not None and (*key, slot) not in EARLY
+        ],
         compiler_params=pltpu.CompilerParams(
             collective_id=1, has_side_effects=True, vmem_limit_bytes=62 * 2**20
         ),
-    )(grad_wide, grad_shared, x, e, rest, *tables, middle, h1p, q, k, v, mixed, probs, vector, dh2)
+    )(*tables, grad_wide, grad_shared, *fetched)
     return output.reshape(2, 1, 128, D), input_grad.reshape(2, 1, 128, D), grads
-
-
-def pack(units, query, out, narrow, vector, parity):
-    wide = jnp.concatenate(
-        [half(rows[16 * k : 16 * k + 16]) for k in range(2) for rows in units]
-    )
-    narrow = jnp.concatenate(
-        [narrow, jnp.pad(vector[None], ((0, 6), (0, D - 256 - vector.shape[0])))], axis=1
-    )
-
-    def placed(rows, size):
-        low = jnp.pad(rows, ((0, 16 - size), (0, 0)))
-        high = jnp.pad(rows, ((size, 16 - 2 * size), (0, 0)))
-        return jnp.where(parity == 0, low, high)
-
-    shared = [placed(rows[32:38], 6) for rows in units] + [
-        placed(rows, 7) for rows in (query, out, narrow)
-    ]
-    return wide, half(jnp.concatenate(shared))
 
 
 def newton_schulz(gram, values):
@@ -1170,16 +1319,16 @@
     core = lax.axis_index("narrow")
     parity = chip % 2
     kv_width = key_weight.shape[1]
-    blocks = pack(
-        (gate_weight.T, up_weight.T, down_weight),
-        query_weight,
-        out_weight,
-        jnp.concatenate([key_weight, value_weight], axis=1),
-        vectors,
-        parity,
-    )
-    own_lengths = lax.dynamic_slice_in_dim(lengths, chip * 2 + core, 1, axis=1)[:, 0]
-    block_output, input_grad, grads = layer(blocks, inputs[:, 0], cotangent[:, 0], own_lengths)
+    narrow_rows = jnp.concatenate(
+        [key_weight, value_weight, jnp.pad(vectors[None], ((0, 6), (0, 128 - vectors.shape[0])))],
+        axis=1,
+    )
+    weights = (
+        gate_weight.T, up_weight.T, down_weight, query_weight, out_weight, narrow_rows
+    )
+    own_lengths = lax.dynamic_slice_in_dim(lengths, chip * 2 + core, 1, axis=1)
+    own_lengths = jnp.broadcast_to(own_lengths, (2, 128))
+    block_output, input_grad, grads = layer(weights, inputs[:, 0], cotangent[:, 0], own_lengths)
     units = grads[:3].reshape(3, 3, 16, D)
     thin = grads[3]
 

time: 296 us -> 274 us (0.926)
  Pallas kernels: 263 us -> 250 us
  other arithmetic: 17.2 us -> 12.5 us
  local copies, waits for them, and re-layouts: 8.96 us -> 4.78 us
    pallas_call x2, Pallas kernels: 205 us -> 191 us  [the longest x1 116 us: layer(): pl.pallas_call(gather_kernel, out_shape=shapes(kept + large), in_specs=[v...]
    another operation x8 -> x5, other arithmetic: 6.06 us -> 3.3 us
where the time goes in v5:
time: 274 us; the launch traced here: 268 us
  Pallas kernels  250 us (91%)
  other arithmetic  12.5 us (5%)
  local copies, waits for them, and re-layouts  4.78 us (2%)
    pallas_call x1, Pallas kernels, layer(): pl.pallas_call(gather_kernel, out_shape=shapes(kept + large), in_specs=[v...  116 us
    pallas_call x1, Pallas kernels, layer(): pl.pallas_call(scatter_kernel, out_shape=shapes([((TOKENS, D), BF16), ((4...  74.7 us
    pallas_call x1, Pallas kernels, muon(): pl.pallas_call(muon_kernel, out_shape=(jax.ShapeDtypeStruct((3, 48, D), B...  58.4 us
    sub x4, other arithmetic, body(): masters[k] * (1.0 - MUON_RATE * MUON_DECAY) - factor * current  5.89 us

profile of v5, /device:TPU:1, one launch (start us, length us, event | category | flops | bytes accessed | tf_op | source)
XLA Modules:
  0.0 268.3 jit_solution(14623980514260448624)
XLA Ops:
  0.7 0.0 copy-start
  0.7 1.3 select_maximum_fusion.narrow_ref
  2.0 0.0 copy-done
  2.0 0.2 fusion.4
  2.2 0.6 broadcast_in_dim.12.len_ref
  2.8 116.5 %shard_map.366 = (f32[256,896]{1,0:T(8,128)}, bf16[256,896]{1,0:T(8,128)(2,1)}, bf16[256,1024]{1,0:T(8,128)(2,1)}, bf16[256,896]{1,0:T(8,128)(2,1)}, bf16[256,12...) custom-call(f32[38,896]{1,0:T(8,128)} %bitcast.97, ...), custom_call_target="tpu_custom_call" | custom-call | tf_op jit(solution)/shard_map/pallas_call | solution.py:1008
  119.3 0.0 copy-start.11
  119.3 0.0 copy-start.12
  119.3 0.0 copy-start.15
  119.3 0.0 copy-start.16
  119.3 0.0 copy-start.6
  119.4 0.0 copy-start.7
  119.4 0.0 copy-start.8
  119.4 74.7 %shard_map.367 = (bf16[256,896]{1,0:T(8,128)(2,1)}, f32[4,48,896]{2,1,0:T(8,128)}) custom-call(f32[256,128]{1,0:T(8,128)} %constant.89.clone.cos_ref, f32[256,128]{1,0:T(8,128)} %constant.90.clone.sin_ref, s32[1,2944]{1,0:T(1,128)} %constant.91.clone.slot_ref, bf16[4,4,2,2,96,896]{5,4,3,2,1,0:T(8,128)(2,1)} %get-tuple-element.44.grad_wide_ref, ...), custom_call_target="tpu_custom_call" | custom-call | tf_op jit(solution)/shard_map/pallas_call | solution.py:1052
  194.1 0.0 copy-start.9
  194.1 0.0 copy-start.10
  194.1 0.0 copy-start.13
  194.1 0.0 copy-start.14
  194.1 0.0 copy-start.2
  194.1 0.0 copy-start.3
  194.1 0.0 copy-start.1
  194.2 0.0 copy-start.17
  194.2 0.0 copy-start.18
  194.2 0.0 copy-start.19
  194.2 0.0 copy-start.4
  194.2 0.0 copy-start.5
  194.2 1.1 slice.63
  195.4 0.0 copy-done.11
  195.4 0.0 copy-done.12
  195.4 0.6 fusion.8
  196.0 0.0 copy-done.15
  196.0 0.0 copy-done.16
  196.0 0.6 fusion.10
  196.7 1.1 slice.66
  197.8 0.0 copy-done.6
  197.8 0.7 fusion.2
  198.5 0.0 copy-done.7
  198.5 0.7 fusion
  199.2 0.0 copy-done.8
  199.2 0.7 fusion.11
  199.9 0.7 pad_maximum_fusion.tall_ref
  200.7 0.7 pad_maximum_fusion.1.short_ref
  201.4 58.4 %shard_map.368 = (bf16[3,48,896]{2,1,0:T(8,128)(2,1)}, bf16[4,16,896]{2,1,0:T(8,128)(2,1)}) custom-call(bf16[3,48,896]{2,1,0:T(8,128)(2,1)} %pad_maximum_fusion.tall_ref, bf16[4,16,896]{2,1,0:T(8,128)(2,1)} %pad_maximum_fusion.1.short_ref), custom_call_target="tpu_custom_call" | custom-call | tf_op jit(solution)/shard_map/pallas_call | solution.py:1265
  259.8 0.0 copy-done.9
  259.8 0.0 copy-done.10
  259.8 1.4 bitcast_subtract_fusion.3
  261.2 0.0 copy-done.13
  261.2 0.0 copy-done.14
  261.2 1.3 bitcast_subtract_fusion.5
  262.5 0.0 copy-done.2
  262.5 0.0 copy-done.3
  262.5 1.7 bitcast_subtract_fusion
  264.2 0.0 copy-done.1
  264.2 1.6 bitcast_subtract_fusion.2
  265.7 0.0 copy-done.17
  265.7 0.0 copy-done.18
  265.7 0.0 copy-done.19
  265.8 0.5 divide_subtract_fusion
  266.3 0.0 copy-done.4
  266.3 0.8 copy.46
  267.1 0.0 copy-done.5
  267.1 0.8 copy.47
  (9 shorter events, 0.1 us)
Async XLA Ops:
  0.7 1.3 copy-start
  119.3 76.1 %copy-start.11 = (f32[7,896]{1,0:T(8,128)S(1)}, f32[7,896]{1,0:T(8,128)}, u32[]{:S(2)}) copy-start(f32[7,896]{1,0:T(8,128)} %param.37) | copy-start | bytes 75268
  119.3 76.1 %copy-start.12 = (f32[7,896]{1,0:T(8,128)S(1)}, f32[7,896]{1,0:T(8,128)}, u32[]{:S(2)}) copy-start(f32[7,896]{1,0:T(8,128)} %param.34) | copy-start | bytes 75268
  119.3 76.7 %copy-start.15 = (f32[7,128]{1,0:T(8,128)S(1)}, f32[7,128]{1,0:T(8,128)}, u32[]{:S(2)}) copy-start(f32[7,128]{1,0:T(8,128)} %param.36) | copy-start | bytes 10756
  119.3 76.7 %copy-start.16 = (f32[7,128]{1,0:T(8,128)S(1)}, f32[7,128]{1,0:T(8,128)}, u32[]{:S(2)}) copy-start(f32[7,128]{1,0:T(8,128)} %param.35) | copy-start | bytes 10756
  119.3 78.5 %copy-start.6 = (f32[896,38]{0,1:T(8,128)S(1)}, f32[896,38]{0,1:T(8,128)}, u32[]{:S(2)}) copy-start(f32[896,38]{0,1:T(8,128)} %param.38) | copy-start | bytes 408580
  119.4 79.2 %copy-start.7 = (f32[896,38]{0,1:T(8,128)S(1)}, f32[896,38]{0,1:T(8,128)}, u32[]{:S(2)}) copy-start(f32[896,38]{0,1:T(8,128)} %param.39) | copy-start | bytes 408580
  119.4 79.8 %copy-start.8 = (f32[38,896]{1,0:T(8,128)S(1)}, f32[38,896]{1,0:T(8,128)}, u32[]{:S(2)}) copy-start(f32[38,896]{1,0:T(8,128)} %param.40) | copy-start | bytes 408580
  194.1 65.7 %copy-start.9 = (f32[7,896]{1,0:T(8,128)S(1)}, f32[7,896]{1,0:T(8,128)}, u32[]{:S(2)}) copy-start(f32[7,896]{1,0:T(8,128)} %query_ref.1) | copy-start | bytes 75268
  194.1 65.7 %copy-start.10 = (f32[7,896]{1,0:T(8,128)S(1)}, f32[7,896]{1,0:T(8,128)}, u32[]{:S(2)}) copy-start(f32[7,896]{1,0:T(8,128)} %out_ref.1) | copy-start | bytes 75268
  194.1 67.1 %copy-start.13 = (f32[7,128]{1,0:T(8,128)S(1)}, f32[7,128]{1,0:T(8,128)}, u32[]{:S(2)}) copy-start(f32[7,128]{1,0:T(8,128)} %param.28) | copy-start | bytes 10756
  194.1 67.1 %copy-start.14 = (f32[7,128]{1,0:T(8,128)S(1)}, f32[7,128]{1,0:T(8,128)}, u32[]{:S(2)}) copy-start(f32[7,128]{1,0:T(8,128)} %param.27) | copy-start | bytes 10756
  194.1 68.4 %copy-start.2 = (f32[896,38]{0,1:T(8,128)S(1)}, f32[896,38]{0,1:T(8,128)}, u32[]{:S(2)}) copy-start(f32[896,38]{0,1:T(8,128)} %param.30) | copy-start | bytes 408580
  194.1 68.4 %copy-start.3 = (f32[896,38]{0,1:T(8,128)S(1)}, f32[896,38]{0,1:T(8,128)}, u32[]{:S(2)}) copy-start(f32[896,38]{0,1:T(8,128)} %param.31) | copy-start | bytes 408580
  194.1 70.0 %copy-start.1 = (f32[38,896]{1,0:T(8,128)S(1)}, f32[38,896]{1,0:T(8,128)}, u32[]{:S(2)}) copy-start(f32[38,896]{1,0:T(8,128)} %down_ref.1) | copy-start | bytes 408580
  194.2 71.6 %copy-start.17 = (f32[23]{0:T(128)S(1)}, f32[23]{0:T(128)}, u32[]{:S(2)}) copy-start(f32[23]{0:T(128)} %param.33) | copy-start | bytes 280
  194.2 71.6 %copy-start.18 = (f32[23]{0:T(128)S(1)}, f32[23]{0:T(128)}, u32[]{:S(2)}) copy-start(f32[23]{0:T(128)} %param.42) | copy-start | bytes 280
  194.2 71.6 %copy-start.19 = (f32[23]{0:T(128)S(1)}, f32[23]{0:T(128)}, u32[]{:S(2)}) copy-start(f32[23]{0:T(128)} %param.41) | copy-start | bytes 280
  194.2 72.1 %copy-start.4 = (bf16[256,896]{1,0:T(8,128)(2,1)S(1)}, bf16[256,896]{1,0:T(8,128)(2,1)}, u32[]{:S(2)}) copy-start(bf16[256,896]{1,0:T(8,128)(2,1)} %get-tuple-element.43) | copy-start | bytes 1376260
  194.2 72.9 %copy-start.5 = (bf16[256,896]{1,0:T(8,128)(2,1)S(1)}, bf16[256,896]{1,0:T(8,128)(2,1)}, u32[]{:S(2)}) copy-start(bf16[256,896]{1,0:T(8,128)(2,1)} %get-tuple-element.63) | copy-start | bytes 1376260

commit v6 on v5

--- a/solution.py
+++ b/solution.py
@@ -63,15 +63,16 @@
 F32 = jnp.float32
 CHUNK = 48
 PARTS = (
-    (0, 0, CHUNK, (2, 1, 0), False),
-    (0, CHUNK, CHUNK, (1, 0, 2), False),
-    (1, 0, CHUNK, (0, 2, 1), True),
-    (2, 0, 16, (2, 1, 0), True),
-    (2, 16, 16, (1, 0, 2), True),
-    (2, 32, 16, (0, 2, 1), True),
+    (0, 0, CHUNK, (2, 1, 0), False, (0, D)),
+    (0, CHUNK, CHUNK, (1, 0, 2), False, (0, D)),
+    (1, 0, CHUNK, (0, 2, 1), True, (0, D)),
+    (2, 0, 16, (2, 1, 0), True, (0, D)),
+    (2, 16, 16, (1, 0, 2), True, (0, 512)),
+    (2, 16, 16, (0, 2, 1), True, (512, 384)),
+    (2, 32, 16, (0, 2, 1), True, (0, 384)),
 )
 WIDE = (0, 1, 2)
-THIN = (3, 4, 5)
+THIN = (3, 4, 5, 6)
 
 
 def my_coords():
@@ -115,9 +116,8 @@
     )
 
 
-def place_of(part, piece):
-    spec, columns = piece
-    _, first, rows, _, shared = PARTS[part]
+def place_of(part, spec):
+    _, first, rows, _, shared, columns = PARTS[part]
     index = [pl.ds(*s) if isinstance(s, tuple) else s for s in spec[:2]]
     s = spec[2]
     if isinstance(s, tuple):
@@ -126,23 +126,11 @@
     else:
         index.append(s // 2)
         index += [] if shared else [s % 2]
-    columns = (0, D) if columns is None else columns
     return (*index, pl.ds(first, rows), pl.ds(*columns))
 
 
-def shape_of(part, piece):
-    return tuple(entry.size for entry in place_of(part, piece) if isinstance(entry, pl.Slice))
-
-
-def halves(spec, axis):
-    if axis is None:
-        return [(spec, (0, 512)), (spec, (512, 384))]
-    out = []
-    for h in range(2):
-        s = list(spec)
-        s[axis] = (2 * h, 2)
-        out.append((tuple(s), None))
-    return out
+def shape_of(part, spec):
+    return tuple(entry.size for entry in place_of(part, spec) if isinstance(entry, pl.Slice))
 
 
 class Plan:
@@ -151,24 +139,27 @@
         self.exchange = PARTS[part][4] and axis == 2
         self.direct = not self.exchange and stage == 0
 
+    def at(self, by):
+        return shifted(self.coords, self.axis, by)
+
     def whole(self, by):
         spec = list(self.spec)
         spec[self.axis] = (self.coords[self.axis] + by) % 4
-        return (tuple(spec), None)
-
-    def at(self, by):
-        return shifted(self.coords, self.axis, by)
+        return tuple(spec)
 
     def pieces(self, by):
-        spec = list(self.spec)
-        spec[self.axis] = (self.coords[self.axis] + by) % 4
-        return halves(tuple(spec), self.split)
+        out = []
+        for h in range(2):
+            spec = list(self.whole(by))
+            spec[self.split] = (2 * h, 2)
+            out.append(tuple(spec))
+        return out
 
     def facing(self):
-        return ((*self.spec[:2], 3 - self.coords[2]), None)
+        return (*self.spec[:2], 3 - self.coords[2])
 
     def own(self):
-        return (self.spec, None)
+        return self.spec
 
 
 def plan_of(part, stage, coords):
@@ -255,7 +246,7 @@
         self.far(parts, phase)
 
     def drain(self):
-        for part in range(6):
+        for part in range(len(PARTS)):
             for phase in range(3):
                 plan = plan_of(part, phase, self.coords)
                 if plan.exchange:
@@ -392,7 +383,7 @@
             self.add(part, phase, plan.pieces(0)[1], 2, 5)
 
     def drain(self):
-        for part in range(6):
+        for part in range(len(PARTS)):
             for phase in range(3):
                 plan = plan_of(part, phase, self.coords)
                 if plan.exchange:
@@ -414,7 +405,7 @@
 
 def scatter_buffer_shapes():
     out = []
-    for part in range(6):
+    for part in range(len(PARTS)):
         for phase in range(3):
             plan = plan_of(part, phase, (0, 0, 0))
             if plan.exchange:
@@ -490,6 +481,11 @@
 
 def slot_mask(slots):
     return lax.broadcasted_iota(jnp.int32, (128, 2944), 0) == slots
+
+
+def live_tokens(len_ref):
+    token = lax.broadcasted_iota(jnp.int32, (128, 1), 0)
+    return jnp.concatenate([(token < len_ref[b : b + 1, 0:1]).astype(F32) for b in range(2)])
 
 
 def attention_forward(
@@ -548,7 +544,7 @@
     return half(middle * second_scale * second_gain)
 
 
-def mlp_tile(weights, h, e, out_acc, back_acc):
+def mlp_tile(weights, h, e, sums):
     lead = weights.shape[:-2]
     units = 16 * math.prod(lead)
     gate_w, up_w, down_w = (
@@ -560,10 +556,10 @@
     silu = gate * sigma
     hidden = half(silu * up)
     grad_hidden = outer_cols(e, down_w)
-    out_acc[...] += product(hidden, down_w).reshape(2, TOKENS, D)
+    sums[0] += product(hidden, down_w).reshape(2, TOKENS, D)
     grad_gate = half(grad_hidden * up * sigma * (1.0 + gate * (1.0 - sigma)))
     grad_up = half(grad_hidden * silu)
-    back_acc[...] += (product(grad_gate, gate_w) + product(grad_up, up_w)).reshape(2, TOKENS, D)
+    sums[1] += (product(grad_gate, gate_w) + product(grad_up, up_w)).reshape(2, TOKENS, D)
     grads = (inner_rows(grad_gate, h), inner_rows(grad_up, h), inner_rows(hidden, e))
     return [half(grad).reshape(*lead, 16, D) for grad in grads]
 
@@ -579,21 +575,18 @@
     z, y, x = coords
     pair, odd = x // 2, x % 2
     results, (grad_wide_ref, grad_shared_ref, rest_ref) = refs[:KEPT], refs[KEPT : KEPT + 3]
-    held = refs[KEPT + 3 : 2 * KEPT + 3]
+    held = refs[KEPT + 3 : 2 * KEPT + 1]
     (
-        wide, shared, rest, stage0, stage1, stage2, h_all, e_all, out_acc, back_acc, parcel, arrived,
-        tail, tail_own, tail_wide,
+        wide, shared, rest, stage0, stage1, stage2, h_all, e_all, sums, parcel, tail, tail_own, tail_wide,
         local_sems, send_sems, recv_sems, twin_sems, store_sems, early_sems, kept_sems,
-    ) = refs[2 * KEPT + 3 :]
-    (
-        middle_ref, e_ref, h1p_ref, q_ref, k_ref, v_ref, mixed_ref, probs_ref, vector_ref,
-        output_ref, dh2_ref,
-    ) = held[:11]
-    early = held[11:]
+    ) = refs[2 * KEPT + 1 :]
+    middle_ref, e_ref, h1p_ref, q_ref, k_ref, v_ref, mixed_ref, probs_ref, vector_ref = held[:9]
+    early = held[9:]
+    kept = [*held[:9], sums.at[:, core], parcel, *early]
 
     def keep(first, last):
         return [
-            pltpu.make_async_copy(held[n], results[n], kept_sems.at[n]) for n in range(first, last)
+            pltpu.make_async_copy(kept[n], results[n], kept_sems.at[n]) for n in range(first, last)
         ]
 
     units = (gate_ref, up_ref, down_ref)
@@ -628,9 +621,7 @@
     tail_copy = remote(tail_own, tail, twin_sems.at[0, 4], twin_sems.at[1, 4], partner)
     tail_copy.start()
     gather.start((0, 1), 0)
-    token = lax.broadcasted_iota(jnp.int32, (128, 1), 0)
-    live = jnp.concatenate([(token < len_ref[b : b + 1, 0:1]).astype(F32) for b in range(2)])
-    e_ref[...] = half(cot_ref[...].astype(F32) * live)
+    e_ref[...] = half(cot_ref[...].astype(F32) * live_tokens(len_ref))
     e_all[core] = e_ref[...]
     e_copy = to_twin(e_ref, e_all.at[core], 0)
     e_copy.start()
@@ -667,8 +658,7 @@
     h_copy.start()
     for copy in keep(0, 9):
         copy.start()
-    out_acc[...] = jnp.zeros_like(out_acc)
-    back_acc[...] = jnp.zeros_like(back_acc)
+    sums[...] = jnp.zeros_like(sums)
     e_copy.wait()
     h_copy.wait()
     stages = (stage0, stage1, stage2)
@@ -708,7 +698,7 @@
         for t, axis in enumerate((0, 2, 1)):
             j = (coords[axis] + offset) % 4
             source, target, index = tile_places(j)[t]
-            grads = mlp_tile(source[(*index, slice(None))], h, e, out_acc, back_acc)
+            grads = mlp_tile(source[(*index, slice(None))], h, e, sums)
             copy = pltpu.make_async_copy(
                 stages[t].at[k % 2], target.at[(*index, slice(None))], store_sems.at[t, k % 2]
             )
@@ -740,15 +730,7 @@
         return carry
 
     lax.fori_loop(0, 4, step, 0)
-    parcel[0] = half(out_acc[1 - core])
-    parcel[1] = half(back_acc[1 - core])
-    parcel_copy = to_twin(parcel, arrived, 3)
-    parcel_copy.start()
-    parcel_copy.wait()
-    output_ref[...] = half(
-        (middle_ref[...] + (out_acc[core] + arrived[0].astype(F32))) * live
-    )
-    dh2_ref[...] = back_acc[core] + arrived[1].astype(F32)
+    parcel[...] = half(sums[:, 1 - core])
     for copy in keep(9, 11):
         copy.start()
     for t in range(3):
@@ -854,26 +836,28 @@
     grad_ref[:, :, :, :, 32:48, 384:] = jnp.zeros((2, 4, 4, 2, 16, D - 384), jnp.bfloat16)
 
 
-LOADED = ("x", "e", "rest", "middle", "h1p", "q", "k", "v", "mixed", "probs", "vector", "dh2")
+LOADED = (
+    "parcel", "own", "middle", "e", "x", "rest", "h1p", "q", "k", "v", "mixed", "probs", "vector",
+)
 
 
 def scatter_kernel(
-    cos_ref, sin_ref, slot_ref, grad_wide_ref, grad_shared_ref, *refs,
+    len_ref, cos_ref, sin_ref, slot_ref, grad_wide_ref, grad_shared_ref, *refs,
 ):
     coords, core = my_coords()
     z, y, x = coords
     pair, odd = x // 2, x % 2
     count = len(LOADED) + len(EARLY)
-    sources, (input_grad_ref, out_ref) = refs[:count], refs[count : count + 2]
-    held = refs[count + 2 : 2 * count + 2]
+    sources, (output_ref, input_grad_ref, out_ref) = refs[:count], refs[count : count + 3]
+    held = refs[count + 3 : 2 * count + 3]
     (
-        wide, shared, thin, joined, mine, theirs,
+        wide, shared, thin, joined, mine, theirs, arrived, dh2_ref,
         load_sems, send_sems, recv_sems, twin_sems, pair_sems, held_sems,
-    ) = refs[2 * count + 2 : 2 * count + 14]
-    buffers = refs[2 * count + 14 :]
+    ) = refs[2 * count + 3 : 2 * count + 17]
+    buffers = refs[2 * count + 17 :]
     (
-        x_ref, e_ref, rest_ref, middle_ref, h1p_ref, q_ref, k_ref, v_ref, mixed_ref, probs_ref,
-        vector_ref, dh2_ref,
+        parcel_ref, own_ref, middle_ref, e_ref, x_ref, rest_ref, h1p_ref, q_ref, k_ref, v_ref,
+        mixed_ref, probs_ref, vector_ref,
     ) = held[: len(LOADED)]
     fetches = [
         pltpu.make_async_copy(sources[n], held[n], held_sems.at[n]) for n in range(count)
@@ -896,7 +880,7 @@
         spec = [FULL] * 3
         axis = PARTS[part][3][2]
         spec[axis] = (coords[axis] + by) % 4
-        place = place_of(part, (tuple(spec), None))
+        place = place_of(part, tuple(spec))
         source = (grad_wide_ref, grad_shared_ref)[PARTS[part][0]]
         target = (wide, shared)[PARTS[part][0]]
         return pltpu.make_async_copy(source.at[place], target.at[place], load_sems.at[part, by])
@@ -918,15 +902,26 @@
     def between():
         scatter.forward(WIDE, 2)
 
-    for copy in fetches:
+    for copy in fetches[:3]:
         copy.wait()
+    parcel_copy = remote(
+        parcel_ref, arrived, twin_sems.at[0, 1], twin_sems.at[1, 1], device_of(coords, 1 - core)
+    )
+    parcel_copy.start()
+    for copy in fetches[3:]:
+        copy.wait()
+    parcel_copy.wait()
+    output_ref[...] = half(
+        (middle_ref[...] + (own_ref[0] + arrived[0].astype(F32))) * live_tokens(len_ref)
+    )
+    dh2_ref[...] = own_ref[1] + arrived[1].astype(F32)
     attention_backward(
         between, x_ref, e_ref, rest_ref, cos_ref, sin_ref, slot_ref,
         middle_ref, h1p_ref, q_ref, k_ref, v_ref, mixed_ref, probs_ref, vector_ref, dh2_ref,
         input_grad_ref, thin,
     )
     twin_copy = remote(
-        thin.at[1 - core], joined, twin_sems.at[0], twin_sems.at[1], device_of(coords, 1 - core)
+        thin.at[1 - core], joined, twin_sems.at[0, 0], twin_sems.at[1, 0], device_of(coords, 1 - core)
     )
     twin_copy.start()
     for part in WIDE:
@@ -990,8 +985,8 @@
         ((TOKENS, 1024), BF16),
         ((2, 7, 128, 256), F32),
         ((1, 2944), F32),
-        ((TOKENS, D), BF16),
-        ((TOKENS, D), F32),
+        ((2, TOKENS, D), F32),
+        ((2, TOKENS, D), BF16),
     ] + [(buffers[part, stage][slot], BF16) for part, stage, slot in EARLY]
     large = [
         ((4, 4, 2, 2, 2 * CHUNK, D), BF16),
@@ -1011,7 +1006,8 @@
         in_specs=[vmem] * 12,
         out_specs=[anywhere] * (KEPT + 3),
         scratch_shapes=scratch(
-            kept
+            kept[:9]
+            + kept[11:]
             + large
             + [
                 ((2, 4, 2, 2, CHUNK, D), BF16),
@@ -1019,9 +1015,7 @@
                 ((2, 4, 2, CHUNK, D), BF16),
                 ((2, TOKENS, D), BF16),
                 ((2, TOKENS, D), BF16),
-                ((2, TOKENS, D), F32),
-                ((2, TOKENS, D), F32),
-                ((2, TOKENS, D), BF16),
+                ((2, 2, TOKENS, D), F32),
                 ((2, TOKENS, D), BF16),
                 ((2 * CHUNK, D), BF16),
                 ((2 * CHUNK, D), BF16),
@@ -1030,8 +1024,8 @@
         )
         + [
             pltpu.SemaphoreType.DMA((3,)),
-            pltpu.SemaphoreType.DMA((6, 3, 6)),
-            pltpu.SemaphoreType.DMA((6, 3, 6)),
+            pltpu.SemaphoreType.DMA((len(PARTS), 3, 6)),
+            pltpu.SemaphoreType.DMA((len(PARTS), 3, 6)),
             pltpu.SemaphoreType.DMA((2, 5)),
             pltpu.SemaphoreType.DMA((3, 2)),
             pltpu.SemaphoreType.DMA((2, 3, 2)),
@@ -1041,19 +1035,19 @@
             collective_id=0, has_side_effects=True, vmem_limit_bytes=61 * 2**20
         ),
     )(*weights, x, cotangent.reshape(TOKENS, D), lengths, *tables)
-    middle, e, h1p, q, k, v, mixed, probs, vector, output, dh2 = results[:11]
+    middle, e, h1p, q, k, v, mixed, probs, vector, own, parcel = results[:11]
     early = results[11:KEPT]
     grad_wide, grad_shared, rest = results[KEPT:]
     loaded = dict(
         x=x, e=e, rest=rest, middle=middle, h1p=h1p, q=q, k=k, v=v, mixed=mixed, probs=probs,
-        vector=vector, dh2=dh2,
+        vector=vector, own=own, parcel=parcel,
     )
     fetched = [loaded[name] for name in LOADED] + list(early)
-    input_grad, grads = pl.pallas_call(
+    output, input_grad, grads = pl.pallas_call(
         scatter_kernel,
-        out_shape=shapes([((TOKENS, D), BF16), ((4, CHUNK, D), F32)]),
-        in_specs=[vmem] * 3 + [anywhere] * (2 + len(fetched)),
-        out_specs=[vmem] * 2,
+        out_shape=shapes([((TOKENS, D), BF16), ((TOKENS, D), BF16), ((4, CHUNK, D), F32)]),
+        in_specs=[vmem] * 4 + [anywhere] * (2 + len(fetched)),
+        out_specs=[vmem] * 3,
         scratch_shapes=scratch(
             [(value.shape, value.dtype) for value in fetched]
             + large[:2]
@@ -1062,13 +1056,15 @@
                 ((4, 4, 2, CHUNK, D), BF16),
                 ((2, CHUNK, D), BF16),
                 ((2, CHUNK, D), BF16),
+                ((2, TOKENS, D), BF16),
+                ((TOKENS, D), F32),
             ]
         )
         + [
             pltpu.SemaphoreType.DMA((3, 4)),
-            pltpu.SemaphoreType.DMA((6, 3, 6)),
-            pltpu.SemaphoreType.DMA((6, 3, 6)),
-            pltpu.SemaphoreType.DMA((2,)),
+            pltpu.SemaphoreType.DMA((len(PARTS), 3, 6)),
+            pltpu.SemaphoreType.DMA((len(PARTS), 3, 6)),
+            pltpu.SemaphoreType.DMA((2, 2)),
             pltpu.SemaphoreType.DMA((2,)),
             pltpu.SemaphoreType.DMA((len(fetched),)),
         ]
@@ -1081,7 +1077,7 @@
         compiler_params=pltpu.CompilerParams(
             collective_id=1, has_side_effects=True, vmem_limit_bytes=62 * 2**20
         ),
-    )(*tables, grad_wide, grad_shared, *fetched)
+    )(lengths, *tables, grad_wide, grad_shared, *fetched)
     return output.reshape(2, 1, 128, D), input_grad.reshape(2, 1, 128, D), grads
 
 
@@ -1100,16 +1096,76 @@
 JOB_ROWS = (48, 48, 48, 16, 16, 16, 16)
 
 
+def own_momenta(grads_ref, priors, momenta, odd):
+    for parity in range(2):
+
+        @pl.when(odd == parity)
+        def _():
+            for n in range(3):
+                for k, (start, size) in enumerate(((0, 16), (16, 16), (32, 6))):
+                    base = 16 * n + (6 * parity if k == 2 else 0)
+                    momenta[n][start : start + size] = (
+                        MOMENTUM * priors[n][start : start + size] + grads_ref[k, base : base + size]
+                    )
+            for n in range(4):
+                base = 16 * min(n, 2) + 7 * parity
+                lanes = slice(0, D) if n < 2 else slice(128 * n - 256, 128 * n - 128)
+                momenta[3 + n][...] = (
+                    MOMENTUM * priors[3 + n][...] + grads_ref[3, base : base + 7, lanes]
+                )
+
+
+def update_kernel(grads_ref, tall_ref, short_ref, *refs):
+    priors, masters, (first_ref, second_ref, vector_ref) = refs[:7], refs[7:14], refs[14:17]
+    momenta, updated, vector_outs = refs[17:24], refs[24:31], refs[31:34]
+    odd = lax.axis_index("dp") % 2
+    own_momenta(grads_ref, priors, momenta, odd)
+    for n in range(7):
+        size = FF if n < 3 else D
+        got = tall_ref[n].astype(F32)[:38] if n < 3 else short_ref[n - 3].astype(F32)[:7]
+        got = got[:, :128] if n > 4 else got
+        updated[n][...] = masters[n][...] * (1.0 - MUON_RATE * MUON_DECAY) - (
+            MUON_RATE * 0.2 * math.sqrt(size) * got
+        )
+    for parity in range(2):
+
+        @pl.when(odd == parity)
+        def _():
+            start = 32 + 7 * parity
+            grad = grads_ref[3, start : start + 1, 256:384][:, :23]
+            first = BETA_FIRST * first_ref[...] + (1.0 - BETA_FIRST) * grad
+            second = BETA_SECOND * second_ref[...] + (1.0 - BETA_SECOND) * grad * grad
+            first_hat = first / (1.0 - BETA_FIRST**STEP)
+            second_hat = second / (1.0 - BETA_SECOND**STEP)
+            vector_outs[0][...] = first
+            vector_outs[1][...] = second
+            vector_outs[2][...] = vector_ref[...] * (1.0 - ADAM_RATE * ADAM_DECAY) - (
+                ADAM_RATE * first_hat / (jnp.sqrt(second_hat) + ADAM_EPSILON)
+            )
+
+
 def muon_kernel(
-    tall_ref, short_ref, tall_out_ref, short_out_ref,
-    rows, gram_out, gram_twin, gram_half_sum, gram_in, gram_all, gram, back, tall_got, short_got,
+    grads_ref, prior0, prior1, prior2, prior3, prior4, prior5, prior6, tall_out_ref, short_out_ref,
+    momentum0, momentum1, momentum2, momentum3, momentum4, momentum5, momentum6,
+    tall_wide, short_wide, tall_ref, short_ref, rows, gram_out, gram_twin, gram_half_sum, gram_in, gram_all, gram, back, tall_got, short_got,
     job_sems, twin_sems, sum_sems, all_sems, back_sems,
 ):
+    priors = (prior0, prior1, prior2, prior3, prior4, prior5, prior6)
+    momenta = (momentum0, momentum1, momentum2, momentum3, momentum4, momentum5, momentum6)
     coords, core = my_coords()
     z, y, x = coords
     job = z * 2 + y // 2
     source = z * 2 + y // 2
     member = (y % 2) * 4 + x
+    tall_wide[...] = jnp.zeros_like(tall_wide)
+    short_wide[...] = jnp.zeros_like(short_wide)
+    own_momenta(grads_ref, priors, momenta, x % 2)
+    for n in range(3):
+        tall_wide[n, 0:38] = momenta[n][...]
+    for n in range(4):
+        short_wide[n, 0:7, 0 : D if n < 2 else 128] = momenta[3 + n][...]
+    tall_ref[...] = half(tall_wide[...])
+    short_ref[...] = half(short_wide[...])
     twin = device_of(coords, 1 - core)
 
     def group(peer):
@@ -1260,17 +1316,22 @@
     short_out_ref[...] = short_got[...]
 
 
-def muon(tall, short):
+def muon(grads, priors, masters, vectors):
     vmem = pl.BlockSpec(memory_space=pltpu.VMEM)
-    return pl.pallas_call(
+    tall, short = pl.pallas_call(
         muon_kernel,
         out_shape=(
             jax.ShapeDtypeStruct((3, 48, D), BF16),
             jax.ShapeDtypeStruct((4, 16, D), BF16),
         ),
-        in_specs=[vmem] * 2,
-        out_specs=(vmem,) * 2,
+        in_specs=[vmem] * 8,
+        out_specs=[vmem] * 2,
         scratch_shapes=[
+            *(pltpu.VMEM(value.shape, F32) for value in priors),
+            pltpu.VMEM((3, 48, D), F32),
+            pltpu.VMEM((4, 16, D), F32),
+            pltpu.VMEM((3, 48, D), BF16),
+            pltpu.VMEM((4, 16, D), BF16),
             pltpu.VMEM((8, 48, D), BF16),
             pltpu.VMEM((2, 16, 128, 128), BF16),
             pltpu.VMEM((16, 128, 128), BF16),
@@ -1290,7 +1351,14 @@
         compiler_params=pltpu.CompilerParams(
             collective_id=3, has_side_effects=True, vmem_limit_bytes=58 * 2**20
         ),
-    )(tall, short)
+    )(grads, *priors)
+    outs = [*priors, *masters, *vectors]
+    return pl.pallas_call(
+        update_kernel,
+        out_shape=[jax.ShapeDtypeStruct(value.shape, F32) for value in outs],
+        in_specs=[vmem] * 20,
+        out_specs=[vmem] * 17,
+    )(grads, tall, short, *outs)
 
 
 def body(
@@ -1317,8 +1385,6 @@
 ):
     chip = lax.axis_index("dp")
     core = lax.axis_index("narrow")
-    parity = chip % 2
-    kv_width = key_weight.shape[1]
     narrow_rows = jnp.concatenate(
         [key_weight, value_weight, jnp.pad(vectors[None], ((0, 6), (0, 128 - vectors.shape[0])))],
         axis=1,
@@ -1329,83 +1395,22 @@
     own_lengths = lax.dynamic_slice_in_dim(lengths, chip * 2 + core, 1, axis=1)
     own_lengths = jnp.broadcast_to(own_lengths, (2, 128))
     block_output, input_grad, grads = layer(weights, inputs[:, 0], cotangent[:, 0], own_lengths)
-    units = grads[:3].reshape(3, 3, 16, D)
-    thin = grads[3]
-
-    def mine(which, size):
-        if size == 7:
-            return lax.dynamic_slice_in_dim(thin, 16 * which + parity * 7, 7, axis=0)
-        last = lax.dynamic_slice_in_dim(units[2, which], parity * 6, 6, axis=0)
-        return jnp.concatenate([units[0, which], units[1, which], last])
-
-    own_narrow = mine(2, 7)
-    grad_vector = own_narrow[0, 2 * kv_width : 2 * kv_width + 23]
-    owned = (
-        mine(0, 7),
-        own_narrow[:, :kv_width],
-        own_narrow[:, kv_width : 2 * kv_width],
-        mine(1, 7),
-        mine(0, 38),
-        mine(1, 38),
-        mine(2, 38),
-    )
-    priors = (
-        query_prior,
-        key_prior,
-        value_prior,
-        out_prior,
-        gate_prior.T,
-        up_prior.T,
-        down_prior,
-    )
-    masters = (
-        query_weight,
-        key_weight,
-        value_weight,
-        out_weight,
-        gate_weight,
-        up_weight,
-        down_weight,
-    )
-    shapes = ((D, D), (D, kv_width), (D, kv_width), (D, D), (D, FF), (D, FF), (FF, D))
-    lefts = (False, False, False, False, True, True, False)
-    momenta = tuple((MOMENTUM * priors[k] + owned[k] for k in range(7)))
-
-    def padded(value, count):
-        return jnp.pad(value, ((0, count - value.shape[0]), (0, D - value.shape[1])))
-
-    tall, short = muon(
-        half(jnp.stack([padded(momenta[k], 48) for k in (4, 5, 6)])),
-        half(jnp.stack([padded(momenta[k], 16) for k in (0, 3, 1, 2)])),
-    )
-    finals = (
-        short[0, :7], short[2, :7, :128], short[3, :7, :128], short[1, :7], tall[0, :38], tall[1, :38],
-        tall[2, :38],
-    )
-    updated = []
-    kept = []
-    for k in range(7):
-        current = finals[k].astype(jnp.float32)
-        factor = MUON_RATE * 0.2 * math.sqrt(max(shapes[k][0], shapes[k][1]))
-        if lefts[k]:
-            current = current.T
-        updated.append(masters[k] * (1.0 - MUON_RATE * MUON_DECAY) - factor * current)
-        kept.append(momenta[k].T if lefts[k] else momenta[k])
-    vector_first = BETA_FIRST * first_prior + (1.0 - BETA_FIRST) * grad_vector
-    vector_second = BETA_SECOND * second_prior + (1.0 - BETA_SECOND) * grad_vector * grad_vector
-    first_hat = vector_first / (1.0 - BETA_FIRST**STEP)
-    second_hat = vector_second / (1.0 - BETA_SECOND**STEP)
-    vector_new = vectors * (1.0 - ADAM_RATE * ADAM_DECAY) - ADAM_RATE * first_hat / (
-        jnp.sqrt(second_hat) + ADAM_EPSILON
-    )
+    results = muon(
+        grads,
+        (gate_prior.T, up_prior.T, down_prior, query_prior, out_prior, key_prior, value_prior),
+        (gate_weight.T, up_weight.T, down_weight, query_weight, out_weight, key_weight, value_weight),
+        (first_prior[None], second_prior[None], vectors[None]),
+    )
+
+    def ordered(gate, up, down, query, out, key, value):
+        return query, key, value, out, gate.T, up.T, down
+
     return (
         block_output,
         input_grad,
-        *kept,
-        *updated,
-        vector_first,
-        vector_second,
-        vector_new,
+        *ordered(*results[:7]),
+        *ordered(*results[7:14]),
+        *(value[0] for value in results[14:]),
     )
 
 

time: 274 us -> 258 us (0.942)
  other arithmetic: 12.5 us -> 1.32 us
  Pallas kernels: 250 us -> 247 us
    pallas_call x1, Pallas kernels: 116 us -> 106 us  [layer(): pl.pallas_call(gather_kernel, out_shape=shapes(kept + large), in_specs=[v...]
    pallas_call x1 -> x2, Pallas kernels: 74.7 us -> 83 us  [the longest x1 80.1 us: layer(): pl.pallas_call(scatter_kernel, out_shape=shapes([((TOKENS, D), BF16), ((T...]
    sub x5 -> x0, other arithmetic: 6.42 us -> none  [the longest x4 5.89 us: body(): masters[k] * (1.0 - MUON_RATE * MUON_DECAY) - factor * current]
    another operation x7 -> x0, other arithmetic: 4.7 us -> none
where the time goes in v6:
time: 258 us; the launch traced here: 253 us
  Pallas kernels  247 us (96%)
  local copies, waits for them, and re-layouts  3.04 us (1%)
    pallas_call x1, Pallas kernels, layer(): pl.pallas_call(gather_kernel, out_shape=shapes(kept + large), in_specs=[v...  106 us
    pallas_call x1, Pallas kernels, layer(): pl.pallas_call(scatter_kernel, out_shape=shapes([((TOKENS, D), BF16), ((T...  80.1 us
    pallas_call x1, Pallas kernels, muon(): pl.pallas_call(muon_kernel, out_shape=(jax.ShapeDtypeStruct((3, 48, D), B...  58.4 us

profile of v6, /device:TPU:1, one launch (start us, length us, event | category | flops | bytes accessed | tf_op | source)
XLA Modules:
  0.0 252.6 jit_solution(12679147086023055272)
XLA Ops:
  0.7 0.0 copy-start
  0.7 0.7 copy-done
  1.3 0.2 dynamic-slice_reduce_fusion
  1.5 0.6 broadcast_in_dim.18.len_ref
  2.2 1.3 select_maximum_fusion.narrow_ref
  3.5 105.6 %shard_map.366 = (f32[256,896]{1,0:T(8,128)}, bf16[256,896]{1,0:T(8,128)(2,1)}, bf16[256,1024]{1,0:T(8,128)(2,1)}, bf16[256,896]{1,0:T(8,128)(2,1)}, bf16[256,12...) custom-call(f32[38,896]{1,0:T(8,128)} %bitcast.24, ...), custom_call_target="tpu_custom_call" | custom-call | tf_op jit(solution)/shard_map/pallas_call | solution.py:1003
  109.1 80.1 %shard_map.367 = (bf16[256,896]{1,0:T(8,128)(2,1)}, bf16[256,896]{1,0:T(8,128)(2,1)}, f32[4,48,896]{2,1,0:T(8,128)}) custom-call(s32[2,128]{1,0:T(2,128)} %broadcast_in_dim.18.len_ref, f32[256,128]{1,0:T(8,128)} %constant.22.clone.cos_ref, f32[256,128]{1,0:T(8,128)} %constant.23.clone.sin_ref, s32[1,2944]{1,0:T(1,128)} %constant.24.clone.slot_ref, ...), custom_call_target="tpu_custom_call" | custom-call | tf_op jit(solution)/shard_map/pallas_call | solution.py:1046
  189.3 0.0 copy-start.2
  189.3 0.0 copy-start.1
  189.3 58.4 %shard_map.368 = (bf16[3,48,896]{2,1,0:T(8,128)(2,1)}, bf16[4,16,896]{2,1,0:T(8,128)(2,1)}) custom-call(f32[4,48,896]{2,1,0:T(8,128)} %get-tuple-element.83.grads_ref, f32[38,896]{1,0:T(8,128)} %bitcast.28, f32[38,896]{1,0:T(8,128)} %bitcast.30, f32[38,896]{1,0:T(8,128)} %refs_2_.1, f32[7,896]{1,0:T(8,128)} %refs_3_.1, f32[7,896]{1,0:T(8,128)} %refs_4_.1, ...), custom_call_target="tpu_custom_call" | custom-call | tf_op jit(solution)/shard_map/pallas_call | solution.py:1321
  247.7 2.9 %shard_map.369 = (f32[38,896]{1,0:T(8,128)}, f32[38,896]{1,0:T(8,128)}, f32[38,896]{1,0:T(8,128)}, f32[7,896]{1,0:T(8,128)}, f32[7,896]{1,0:T(8,128)}, /*index=5...) custom-call(f32[4,48,896]{2,1,0:T(8,128)} %get-tuple-element.83.grad, ...), custom_call_target="tpu_custom_call" | custom-call | tf_op jit(solution)/shard_map/pallas_call | solution.py:1356
  250.6 0.0 copy-done.2
  250.6 0.8 copy.46
  251.4 0.0 copy-done.1
  251.4 0.8 copy.47
Async XLA Ops:
  0.7 0.7 copy-start
  189.3 61.4 %copy-start.2 = (bf16[256,896]{1,0:T(8,128)(2,1)S(1)}, bf16[256,896]{1,0:T(8,128)(2,1)}, u32[]{:S(2)}) copy-start(bf16[256,896]{1,0:T(8,128)(2,1)} %get-tuple-element.81) | copy-start | bytes 1376260
  189.3 62.1 %copy-start.1 = (bf16[256,896]{1,0:T(8,128)(2,1)S(1)}, bf16[256,896]{1,0:T(8,128)(2,1)}, u32[]{:S(2)}) copy-start(bf16[256,896]{1,0:T(8,128)(2,1)} %get-tuple-element.82) | copy-start | bytes 1376260
